TPU v7x, 768 devices: a whole 4x8x12 slice. The times are simulated.
768 devices in a mesh: sub: 64 (over z_hi, y, core), grp: 12 (over z_lo, x).
Axes of the slice: x: 4, y: 8, z: 12 (z_hi: 4, z_lo: 3; z = z_hi * 3 + z_lo), core: 2. Of those that a mesh axis runs over, the one named last changes fastest.
Arguments:
- impedance: bfloat16 [64, 12, 2048, 512], P('sub', 'grp'), may hold values from -0.125 to 0.125
- incident: bfloat16 [64, 12, 96, 512], P('sub', 'grp'), may hold values from -6 to 6
- face_order: int32 [64, 12, 192], P('sub', 'grp'), may hold values from 0 to 191, each once within a row
- near_tiles: bfloat16 [64, 12, 3, 128, 128], P('sub', 'grp'), may hold values from -0.3125 to 0.3125
- basis_right: bfloat16 [64, 12, 128, 128], P('sub', 'grp'), may hold values from -0.078125 to 0.078125
- rank_scale: float32 [64, 128], P('sub'), may hold values from 0.3 to 3
- rank_counts: int32 [16], replicated, may hold values from 32 to 128
- coupling: bfloat16 [64, 16, 128, 128], P('sub'), may hold values from -0.0625 to 0.0625
- basis_left: bfloat16 [64, 12, 128, 128], P('sub', 'grp'), may hold values from -0.5 to 0.5
Outputs:
- traces: bfloat16 [64, 12, 96, 512], P('sub', 'grp')
Inputs may be any that keep to these rules, and one draw needn't show every extreme that they name: `face_order`: each row is a permutation of 0 to 191.
All inputs are finite; a program needn't handle non-finite values.
Results may differ from a plain program's by a relative error of at most 0.012.
Values may be sent and summed in bfloat16 or wider, within the bound.
No kernel may reach another device: no remote copies, remote signals or barrier semaphores. Data moves between devices by JAX's collectives and lax.ppermute only.
A program may use at most 32 MiB of HBM per device.

v0:
```python
import jax
import jax.numpy as jnp
from jax import lax
from jax.sharding import PartitionSpec as P

FACE_Q = 192
ITERS = 3


def from_partner(value, axis, distance):
    mask = 2**distance
    pairs = [(source, source ^ mask) for source in range(lax.axis_size(axis))]
    return lax.ppermute(value, axis, pairs)


def cut_along(array, dim, peers):
    lengths = array.shape
    pieces = array.reshape(*lengths[:dim], peers, lengths[dim] // peers, *lengths[dim + 1 :])
    return jnp.moveaxis(pieces, dim, 0)


def sent_and_summed(array, axis, dim):
    pieces = cut_along(array, dim, lax.axis_size(axis))
    arrived = lax.all_to_all(pieces, axis, split_axis=0, concat_axis=0, tiled=True)
    return arrived.astype(jnp.float32).sum(axis=0)


def laid_out(pieces, dim):
    pieces = jnp.moveaxis(pieces, 0, dim)
    lengths = pieces.shape
    return pieces.reshape(*lengths[:dim], lengths[dim] * lengths[dim + 1], *lengths[dim + 2 :])


def copy_for_each(array, axis):
    copies = jnp.broadcast_to(array, (lax.axis_size(axis), *array.shape))
    return lax.all_to_all(copies, axis, split_axis=0, concat_axis=0, tiled=True)


def gather_directly(array, axis, dim):
    return laid_out(copy_for_each(array, axis), dim)


def shifted(value, axis, steps):
    count = lax.axis_size(axis)
    first, last = (max(0, -steps), min(count, count - steps))
    return lax.ppermute(value, axis, [(source, source + steps) for source in range(first, last)])


def per_device(
    impedance,
    incident,
    face_order,
    near_tiles,
    basis_right,
    rank_scale,
    rank_counts,
    coupling,
    basis_left,
):
    z_cols = impedance[0, 0]
    source = incident[0, 0]
    order_map = face_order[0, 0]
    tiles = near_tiles[0, 0]
    right_basis = basis_right[0, 0]
    left_basis = basis_left[0, 0]
    couple_rows = coupling[0]
    position = lax.axis_index("sub")
    cluster = position // 4
    rank_ids = jnp.arange(rank_scale.shape[1])
    kept = jnp.where(rank_ids < rank_counts[cluster], rank_scale[0], jnp.float32(0.0))
    trace_now = source
    for sweep_index in range(ITERS):
        whole = trace_now
        for bit_number in (0, 1):
            partner = from_partner(whole, "sub", bit_number)
            upper_half = position // (1 << bit_number) % 2 == 1
            whole = jnp.where(
                upper_half,
                jnp.concatenate([partner, whole], 1),
                jnp.concatenate([whole, partner], 1),
            )
        outgoing = jnp.dot(whole, z_cols, preferred_element_type=jnp.float32).astype(jnp.bfloat16)
        lower_out = outgoing[:, :FACE_Q]
        upper_out = outgoing[:, FACE_Q : 2 * FACE_Q]
        outer_out = outgoing[:, 2 * FACE_Q :]
        partial_sum = jnp.dot(outer_out, right_basis, preferred_element_type=jnp.float32)
        share = sent_and_summed(partial_sum.astype(jnp.bfloat16), "grp", 0)
        coefs = (share * kept).astype(jnp.bfloat16)
        block_rows = gather_directly(coefs[None], "sub", 0)
        sources = jnp.arange(block_rows.shape[0]) // 4
        chosen = jnp.take(couple_rows, sources, axis=0)
        chosen = jnp.where((sources != cluster)[:, None, None], chosen, jnp.zeros_like(chosen))
        far_part = jnp.einsum(
            "nkr,nrt->kt", block_rows, chosen, preferred_element_type=jnp.float32
        ).astype(jnp.bfloat16)
        far = gather_directly(far_part, "grp", 0)
        arrived = []
        for offset in (4, -4):
            sent = (upper_out, outer_out) if offset > 0 else (lower_out, outer_out)
            arrived.append(shifted((sent[0], sent[1]), "sub", offset))
        upper_below, outer_below = arrived[0]
        lower_above, outer_above = arrived[1]
        lower_in = jnp.take(upper_below, order_map, axis=1)
        outer_in = jnp.dot(outer_out, tiles[0], preferred_element_type=jnp.float32)
        outer_in = outer_in + jnp.dot(outer_below, tiles[1], preferred_element_type=jnp.float32)
        outer_in = outer_in + jnp.dot(outer_above, tiles[2], preferred_element_type=jnp.float32)
        outer_in = outer_in + jnp.dot(far, left_basis, preferred_element_type=jnp.float32)
        joined = jnp.concatenate(
            [lower_in.astype(jnp.float32), lower_above.astype(jnp.float32), outer_in], 1
        )
        trace_now = (joined + source.astype(jnp.float32)).astype(jnp.bfloat16)
    return trace_now[None, None]


def solution(mesh):
    placed = (
        P("sub", "grp", None, None),
        P("sub", "grp", None, None),
        P("sub", "grp", None),
        P("sub", "grp", None, None, None),
        P("sub", "grp", None, None),
        P("sub", None),
        P(),
        P("sub", None, None, None),
        P("sub", "grp", None, None),
    )
    return jax.shard_map(
        per_device,
        mesh=mesh,
        in_specs=placed,
        out_specs=P("sub", "grp", None, None),
        check_vma=False,
    )
```

profile of v0, /device:TPU:1, one launch (start us, length us, event | category | flops | bytes accessed | tf_op | source)
XLA Modules:
  0.0 253.9 jit_solution(7599356805764994689)
XLA Ops:
  0.0 12.5 %collective-permute-start = (bf16[96,512]{1,0:T(8,128)(2,1)}, bf16[96,512]{1,0:T(8,128)(2,1)S(1)}, u32[]{:S(2)}, u32[]{:S(2)}) collective-permute-start(bf16[96,512]{1,0:T(8,128)(2,1)} %bitcast.116), channel_id=1, source_target_pairs={{0,12},{12,0},{24,36},{36,24},{48,60},{60,48},{72,84},{84,72},{96,... | collective-permute-start | bytes 294920 | tf_op jit(solution)/shard_map/ppermute | solution.py:13
  14.0 3.2 %gather_fusion.1 = bf16[64,128,128]{2,1,0:T(8,128)(2,1)} fusion(bf16[16,128,128]{2,1,0:T(8,128)(2,1)} %bitcast.115, s32[1024]{0:T(1024)S(1)} %pad_clamp_fusion), kind=kCustom, calls=%fused_computation.1.clone | custom fusion | bytes 4194560 | tf_op jit(solution)/shard_map/jit(_take)/gather | solution.py:91
  17.8 3.3 %select_select_fusion = bf16[64,128,128]{2,1,0:T(8,128)(2,1)} fusion(bf16[64,128,128]{2,1,0:T(8,128)(2,1)} %gather_fusion.1, pred[64]{0:T(512)(128)(4,1)S(1)} %get-tuple-element.13, pred[64]{0:T(512)(128)(4,1)S(1)} %get-tuple-element.14), kind=kLoop, calls=%fused_computation.10 | loop fusion | flops 2097152 | bytes 4194432 | tf_op jit(solution)/shard_map/jit(_where)/select_n | solution.py:92
  21.3 2.1 collective-permute-start.1
  24.0 5.8 %collective-permute-done.1 = bf16[96,1024]{1,0:T(8,128)(2,1)S(1)} collective-permute-done((bf16[96,1024]{1,0:T(8,128)(2,1)S(1)}, bf16[96,1024]{1,0:T(8,128)(2,1)S(1)}, u32[]{:S(2)}, u32[]{:S(2)}) %collective-permute-start.1) | collective-permute-done | bytes 196640 | tf_op jit(solution)/shard_map/ppermute | solution.py:13
  30.3 1.3 collective-permute-start.4
  31.6 1.3 collective-permute-start.5
  33.6 3.6 %all-to-all-start = ((bf16[12,8,128]{2,1,0:T(8,128)(2,1)}), bf16[12,8,128]{2,1,0:T(8,128)(2,1)S(1)}, u32[]{:S(2)}, u32[]{:S(2)}) async-start(bf16[12,8,128]{2,1,0:T(8,128)(2,1)} %fusion.19), calls=%async_computation | async-start | bytes 49152 | tf_op jit(solution)/shard_map/all_to_all | solution.py:24
  37.4 5.8 %all-to-all-done = bf16[12,8,128]{2,1,0:T(8,128)(2,1)S(1)} async-done(((bf16[12,8,128]{2,1,0:T(8,128)(2,1)}), bf16[12,8,128]{2,1,0:T(8,128)(2,1)S(1)}, u32[]{:S(2)}, u32[]{:S(2)}) %all-to-all-start) | async-done | bytes 24608 | tf_op jit(solution)/shard_map/all_to_all | solution.py:24
  43.9 23.2 %all-to-all-start.1 = ((bf16[64,1,8,128]{3,2,1,0:T(8,128)(2,1)}), bf16[64,1,8,128]{3,2,1,0:T(8,128)(2,1)S(1)}, u32[]{:S(2)}, u32[]{:S(2)}) async-start(bf16[64,1,8,128]{3,2,1,0:T(8,128)(2,1)} %broadcast_in_dim.65), calls=%async_computation.1 | async-start | bytes 262144 | tf_op jit(solution)/shard_map/all_to_all | solution.py:36
  67.2 4.2 %collective-permute-start.2 = (bf16[96,192]{1,0:T(8,128)(2,1)S(1)}, bf16[96,192]{1,0:T(8,128)(2,1)S(1)}, u32[]{:S(2)}, u32[]{:S(2)}) collective-permute-start(bf16[96,192]{1,0:T(8,128)(2,1)S(1)} %get-tuple-element.11), channel_id=1, source_target_pairs={{0,48},{12,60},{24,72},{36,84},{48,96},{60,108},{72,120},{84,132},... | collective-permute-start | bytes 110600 | tf_op jit(solution)/shard_map/ppermute | solution.py:46
  71.4 1.3 collective-permute-start.3
  73.0 0.8 gather_fusion
  73.9 7.9 %all-to-all-done.1 = bf16[64,1,8,128]{3,2,1,0:T(8,128)(2,1)S(1)} async-done(((bf16[64,1,8,128]{3,2,1,0:T(8,128)(2,1)}), bf16[64,1,8,128]{3,2,1,0:T(8,128)(2,1)S(1)}, u32[]{:S(2)}, u32[]{:S(2)}) %all-to-all-start.1) | async-done | bytes 131104 | tf_op jit(solution)/shard_map/all_to_all | solution.py:36
  81.8 2.0 fusion.22
  84.4 3.5 %all-to-all-start.2 = ((bf16[12,8,128]{2,1,0:T(8,128)(2,1)}), bf16[12,8,128]{2,1,0:T(8,128)(2,1)S(1)}, u32[]{:S(2)}, u32[]{:S(2)}) async-start(bf16[12,8,128]{2,1,0:T(8,128)(2,1)} %broadcast_in_dim.67), calls=%async_computation.2 | async-start | bytes 49152 | tf_op jit(solution)/shard_map/all_to_all | solution.py:36
  87.9 5.9 %all-to-all-done.2 = bf16[12,8,128]{2,1,0:T(8,128)(2,1)S(1)} async-done(((bf16[12,8,128]{2,1,0:T(8,128)(2,1)}), bf16[12,8,128]{2,1,0:T(8,128)(2,1)S(1)}, u32[]{:S(2)}, u32[]{:S(2)}) %all-to-all-start.2) | async-done | bytes 24608 | tf_op jit(solution)/shard_map/all_to_all | solution.py:36
  94.2 3.5 %collective-permute-start.6 = (bf16[96,512]{1,0:T(8,128)(2,1)S(1)}, bf16[96,512]{1,0:T(8,128)(2,1)S(1)}, u32[]{:S(2)}, u32[]{:S(2)}) collective-permute-start(bf16[96,512]{1,0:T(8,128)(2,1)S(1)} %fusion.43), channel_id=1, source_target_pairs={{0,12},{12,0},{24,36},{36,24},{48,60},{60,48},{72,84},{84,72},{96,... | collective-permute-start | bytes 294920 | tf_op jit(solution)/shard_map/ppermute | solution.py:13
  97.7 0.9 collective-permute-done.6
  98.7 2.3 collective-permute-start.7
  101.0 5.7 %collective-permute-done.7 = bf16[96,1024]{1,0:T(8,128)(2,1)S(1)} collective-permute-done((bf16[96,1024]{1,0:T(8,128)(2,1)S(1)}, bf16[96,1024]{1,0:T(8,128)(2,1)S(1)}, u32[]{:S(2)}, u32[]{:S(2)}) %collective-permute-start.7) | collective-permute-done | bytes 196640 | tf_op jit(solution)/shard_map/ppermute | solution.py:13
  107.9 3.5 %all-to-all-start.3 = ((bf16[12,8,128]{2,1,0:T(8,128)(2,1)}), bf16[12,8,128]{2,1,0:T(8,128)(2,1)S(1)}, u32[]{:S(2)}, u32[]{:S(2)}) async-start(bf16[12,8,128]{2,1,0:T(8,128)(2,1)} %fusion.20), calls=%async_computation.3 | async-start | bytes 49152 | tf_op jit(solution)/shard_map/all_to_all | solution.py:24
  111.6 2.4 collective-permute-start.10
  114.0 1.3 collective-permute-start.11
  115.3 2.0 all-to-all-done.3
  118.0 18.6 %all-to-all-start.4 = ((bf16[64,1,8,128]{3,2,1,0:T(8,128)(2,1)}), bf16[64,1,8,128]{3,2,1,0:T(8,128)(2,1)S(1)}, u32[]{:S(2)}, u32[]{:S(2)}) async-start(bf16[64,1,8,128]{3,2,1,0:T(8,128)(2,1)} %broadcast_in_dim.68), calls=%async_computation.4 | async-start | bytes 262144 | tf_op jit(solution)/shard_map/all_to_all | solution.py:36
  136.7 4.2 %collective-permute-start.8 = (bf16[96,192]{1,0:T(8,128)(2,1)S(1)}, bf16[96,192]{1,0:T(8,128)(2,1)S(1)}, u32[]{:S(2)}, u32[]{:S(2)}) collective-permute-start(bf16[96,192]{1,0:T(8,128)(2,1)S(1)} %get-tuple-element.9), channel_id=1, source_target_pairs={{0,48},{12,60},{24,72},{36,84},{48,96},{60,108},{72,120},{84,132},... | collective-permute-start | bytes 110600 | tf_op jit(solution)/shard_map/ppermute | solution.py:46
  140.9 1.3 collective-permute-start.9
  142.4 0.8 gather_fusion.2
  143.3 8.1 %all-to-all-done.4 = bf16[64,1,8,128]{3,2,1,0:T(8,128)(2,1)S(1)} async-done(((bf16[64,1,8,128]{3,2,1,0:T(8,128)(2,1)}), bf16[64,1,8,128]{3,2,1,0:T(8,128)(2,1)S(1)}, u32[]{:S(2)}, u32[]{:S(2)}) %all-to-all-start.4) | async-done | bytes 131104 | tf_op jit(solution)/shard_map/all_to_all | solution.py:36
  151.4 2.0 fusion.23
  154.0 7.2 %all-to-all-start.5 = ((bf16[12,8,128]{2,1,0:T(8,128)(2,1)}), bf16[12,8,128]{2,1,0:T(8,128)(2,1)S(1)}, u32[]{:S(2)}, u32[]{:S(2)}) async-start(bf16[12,8,128]{2,1,0:T(8,128)(2,1)} %broadcast_in_dim.69), calls=%async_computation.5 | async-start | bytes 49152 | tf_op jit(solution)/shard_map/all_to_all | solution.py:36
  161.2 5.9 %all-to-all-done.5 = bf16[12,8,128]{2,1,0:T(8,128)(2,1)S(1)} async-done(((bf16[12,8,128]{2,1,0:T(8,128)(2,1)}), bf16[12,8,128]{2,1,0:T(8,128)(2,1)S(1)}, u32[]{:S(2)}, u32[]{:S(2)}) %all-to-all-start.5) | async-done | bytes 24608 | tf_op jit(solution)/shard_map/all_to_all | solution.py:36
  167.5 3.8 %collective-permute-start.12 = (bf16[96,512]{1,0:T(8,128)(2,1)S(1)}, bf16[96,512]{1,0:T(8,128)(2,1)S(1)}, u32[]{:S(2)}, u32[]{:S(2)}) collective-permute-start(bf16[96,512]{1,0:T(8,128)(2,1)S(1)} %fusion.44), channel_id=1, source_target_pairs={{0,12},{12,0},{24,36},{36,24},{48,60},{60,48},{72,84},{84,72},{96,... | collective-permute-start | bytes 294920 | tf_op jit(solution)/shard_map/ppermute | solution.py:13
  171.3 0.9 collective-permute-done.12
  172.3 2.5 collective-permute-start.13
  174.8 5.6 %collective-permute-done.13 = bf16[96,1024]{1,0:T(8,128)(2,1)S(1)} collective-permute-done((bf16[96,1024]{1,0:T(8,128)(2,1)S(1)}, bf16[96,1024]{1,0:T(8,128)(2,1)S(1)}, u32[]{:S(2)}, u32[]{:S(2)}) %collective-permute-start.13) | collective-permute-done | bytes 196640 | tf_op jit(solution)/shard_map/ppermute | solution.py:13
  181.7 2.7 %collective-permute-start.16 = (bf16[96,128]{1,0:T(8,128)(2,1)S(1)}, bf16[96,128]{1,0:T(8,128)(2,1)S(1)}, u32[]{:S(2)}, u32[]{:S(2)}) collective-permute-start(bf16[96,128]{1,0:T(8,128)(2,1)S(1)} %slice.73), channel_id=1, source_target_pairs={{0,48},{12,60},{24,72},{36,84},{48,96},{60,108},{72,120},{84,132},... | collective-permute-start | bytes 73736 | tf_op jit(solution)/shard_map/ppermute | solution.py:46
  184.4 1.3 collective-permute-start.17
  185.7 3.5 %all-to-all-start.6 = ((bf16[12,8,128]{2,1,0:T(8,128)(2,1)}), bf16[12,8,128]{2,1,0:T(8,128)(2,1)S(1)}, u32[]{:S(2)}, u32[]{:S(2)}) async-start(bf16[12,8,128]{2,1,0:T(8,128)(2,1)} %fusion.21), calls=%async_computation.6 | async-start | bytes 49152 | tf_op jit(solution)/shard_map/all_to_all | solution.py:24
  189.3 4.9 %collective-permute-start.14 = (bf16[96,192]{1,0:T(8,128)(2,1)S(1)}, bf16[96,192]{1,0:T(8,128)(2,1)S(1)}, u32[]{:S(2)}, u32[]{:S(2)}) collective-permute-start(bf16[96,192]{1,0:T(8,128)(2,1)S(1)} %get-tuple-element.6), channel_id=1, source_target_pairs={{0,48},{12,60},{24,72},{36,84},{48,96},{60,108},{72,120},{84,132},... | collective-permute-start | bytes 110600 | tf_op jit(solution)/shard_map/ppermute | solution.py:46
  194.2 1.3 collective-permute-start.15
  196.2 26.1 %all-to-all-start.7 = ((bf16[64,1,8,128]{3,2,1,0:T(8,128)(2,1)}), bf16[64,1,8,128]{3,2,1,0:T(8,128)(2,1)S(1)}, u32[]{:S(2)}, u32[]{:S(2)}) async-start(bf16[64,1,8,128]{3,2,1,0:T(8,128)(2,1)} %broadcast_in_dim.70), calls=%async_computation.7 | async-start | bytes 262144 | tf_op jit(solution)/shard_map/all_to_all | solution.py:36
  222.6 0.8 gather_fusion.3
  223.5 13.6 %all-to-all-done.7 = bf16[64,1,8,128]{3,2,1,0:T(8,128)(2,1)S(1)} async-done(((bf16[64,1,8,128]{3,2,1,0:T(8,128)(2,1)}), bf16[64,1,8,128]{3,2,1,0:T(8,128)(2,1)S(1)}, u32[]{:S(2)}, u32[]{:S(2)}) %all-to-all-start.7) | async-done | bytes 131104 | tf_op jit(solution)/shard_map/all_to_all | solution.py:36
  237.1 2.0 fusion.24
  239.7 7.2 %all-to-all-start.8 = ((bf16[12,8,128]{2,1,0:T(8,128)(2,1)}), bf16[12,8,128]{2,1,0:T(8,128)(2,1)S(1)}, u32[]{:S(2)}, u32[]{:S(2)}) async-start(bf16[12,8,128]{2,1,0:T(8,128)(2,1)} %broadcast_in_dim.71), calls=%async_computation.8 | async-start | bytes 49152 | tf_op jit(solution)/shard_map/all_to_all | solution.py:36
  246.9 5.9 %all-to-all-done.8 = bf16[12,8,128]{2,1,0:T(8,128)(2,1)S(1)} async-done(((bf16[12,8,128]{2,1,0:T(8,128)(2,1)}), bf16[12,8,128]{2,1,0:T(8,128)(2,1)S(1)}, u32[]{:S(2)}, u32[]{:S(2)}) %all-to-all-start.8) | async-done | bytes 24608 | tf_op jit(solution)/shard_map/all_to_all | solution.py:36
  (90 shorter events, 14.0 us)
Async XLA Ops:
  0.0 29.8 %copy-start = (bf16[1,1,2048,512]{3,2,1,0:T(8,128)(2,1)S(1)}, bf16[1,1,2048,512]{3,2,1,0:T(8,128)(2,1)}, u32[]{:S(2)}) copy-start(bf16[1,1,2048,512]{3,2,1,0:T(8,128)(2,1)} %param.13) | copy-start | bytes 6291460
  0.0 21.2 %collective-permute-start = (bf16[96,512]{1,0:T(8,128)(2,1)}, bf16[96,512]{1,0:T(8,128)(2,1)S(1)}, u32[]{:S(2)}, u32[]{:S(2)}) collective-permute-start(bf16[96,512]{1,0:T(8,128)(2,1)} %bitcast.116), channel_id=1, source_target_pairs={{0,12},{12,0},{24,36},{36,24},{48,60},{60,48},{72,84},{84,72},{96,... | collective-permute-start | bytes 294920 | tf_op jit(solution)/shard_map/ppermute | solution.py:13
  14.0 3.2 %copy-start.5 = (s32[16]{0:T(128)S(1)}, s32[16]{0:T(128)}, u32[]{:S(2)}) copy-start(s32[16]{0:T(128)} %param.19) | copy-start | bytes 196
  17.8 3.3 %copy-start.1 = (bf16[1,1,96,512]{3,2,1,0:T(8,128)(2,1)S(1)}, bf16[1,1,96,512]{3,2,1,0:T(8,128)(2,1)}, u32[]{:S(2)}) copy-start(bf16[1,1,96,512]{3,2,1,0:T(8,128)(2,1)} %param.14) | copy-start | bytes 294916
  17.8 5.5 %copy-start.6 = (f32[1,128]{1,0:T(1,128)S(1)}, f32[1,128]{1,0:T(1,128)}, u32[]{:S(2)}) copy-start(f32[1,128]{1,0:T(1,128)} %param.18) | copy-start | bytes 1540
  21.2 11.7 %copy-start.3 = (bf16[1,1,128,128]{3,2,1,0:T(8,128)(2,1)S(1)}, bf16[1,1,128,128]{3,2,1,0:T(8,128)(2,1)}, u32[]{:S(2)}) copy-start(bf16[1,1,128,128]{3,2,1,0:T(8,128)(2,1)} %param.17) | copy-start | bytes 98308
  21.3 45.8 %copy-start.2 = (bf16[1,1,3,128,128]{4,3,2,1,0:T(8,128)(2,1)S(1)}, bf16[1,1,3,128,128]{4,3,2,1,0:T(8,128)(2,1)}, u32[]{:S(2)}) copy-start(bf16[1,1,3,128,128]{4,3,2,1,0:T(8,128)(2,1)} %param.16) | copy-start | bytes 294916
  21.3 8.5 %collective-permute-start.1 = (bf16[96,1024]{1,0:T(8,128)(2,1)S(1)}, bf16[96,1024]{1,0:T(8,128)(2,1)S(1)}, u32[]{:S(2)}, u32[]{:S(2)}) collective-permute-start(bf16[96,1024]{1,0:T(8,128)(2,1)S(1)} %maximum_select_fusion.6), channel_id=1, source_target_pairs={{0,24},{12,36},{24,0},{36,12},{48,72},{60,84},{72,48},{84,60},{96,... | collective-permute-start | bytes 589832 | tf_op jit(solution)/shard_map/ppermute | solution.py:13
  30.3 42.4 %collective-permute-start.4 = (bf16[96,128]{1,0:T(8,128)(2,1)S(1)}, bf16[96,128]{1,0:T(8,128)(2,1)S(1)}, u32[]{:S(2)}, u32[]{:S(2)}) collective-permute-start(bf16[96,128]{1,0:T(8,128)(2,1)S(1)} %slice.67), channel_id=1, source_target_pairs={{0,48},{12,60},{24,72},{36,84},{48,96},{60,108},{72,120},{84,132},... | collective-permute-start | bytes 73736 | tf_op jit(solution)/shard_map/ppermute | solution.py:46
  31.6 62.4 %collective-permute-start.5 = (bf16[96,128]{1,0:T(8,128)(2,1)S(1)}, bf16[96,128]{1,0:T(8,128)(2,1)S(1)}, u32[]{:S(2)}, u32[]{:S(2)}) collective-permute-start(bf16[96,128]{1,0:T(8,128)(2,1)S(1)} %slice.67), channel_id=1, source_target_pairs={{48,0},{60,12},{72,24},{84,36},{96,48},{108,60},{120,72},{132,84},... | collective-permute-start | bytes 73736 | tf_op jit(solution)/shard_map/ppermute | solution.py:46
  33.6 60.2 %copy-start.4 = (bf16[1,1,128,128]{3,2,1,0:T(8,128)(2,1)S(1)}, bf16[1,1,128,128]{3,2,1,0:T(8,128)(2,1)}, u32[]{:S(2)}) copy-start(bf16[1,1,128,128]{3,2,1,0:T(8,128)(2,1)} %param.21) | copy-start | bytes 98308
  33.6 9.5 %all-to-all-start = ((bf16[12,8,128]{2,1,0:T(8,128)(2,1)}), bf16[12,8,128]{2,1,0:T(8,128)(2,1)S(1)}, u32[]{:S(2)}, u32[]{:S(2)}) async-start(bf16[12,8,128]{2,1,0:T(8,128)(2,1)} %fusion.19), calls=%async_computation | async-start | bytes 49152 | tf_op jit(solution)/shard_map/all_to_all | solution.py:24
  43.9 37.9 %all-to-all-start.1 = ((bf16[64,1,8,128]{3,2,1,0:T(8,128)(2,1)}), bf16[64,1,8,128]{3,2,1,0:T(8,128)(2,1)S(1)}, u32[]{:S(2)}, u32[]{:S(2)}) async-start(bf16[64,1,8,128]{3,2,1,0:T(8,128)(2,1)} %broadcast_in_dim.65), calls=%async_computation.1 | async-start | bytes 262144 | tf_op jit(solution)/shard_map/all_to_all | solution.py:36
  67.2 5.6 %collective-permute-start.2 = (bf16[96,192]{1,0:T(8,128)(2,1)S(1)}, bf16[96,192]{1,0:T(8,128)(2,1)S(1)}, u32[]{:S(2)}, u32[]{:S(2)}) collective-permute-start(bf16[96,192]{1,0:T(8,128)(2,1)S(1)} %get-tuple-element.11), channel_id=1, source_target_pairs={{0,48},{12,60},{24,72},{36,84},{48,96},{60,108},{72,120},{84,132},... | collective-permute-start | bytes 110600 | tf_op jit(solution)/shard_map/ppermute | solution.py:46
  71.4 16.5 %collective-permute-start.3 = (bf16[96,192]{1,0:T(8,128)(2,1)S(1)}, bf16[96,192]{1,0:T(8,128)(2,1)S(1)}, u32[]{:S(2)}, u32[]{:S(2)}) collective-permute-start(bf16[96,192]{1,0:T(8,128)(2,1)S(1)} %get-tuple-element.12), channel_id=1, source_target_pairs={{48,0},{60,12},{72,24},{84,36},{96,48},{108,60},{120,72},{132,84},... | collective-permute-start | bytes 110600 | tf_op jit(solution)/shard_map/ppermute | solution.py:46
  84.4 9.4 %all-to-all-start.2 = ((bf16[12,8,128]{2,1,0:T(8,128)(2,1)}), bf16[12,8,128]{2,1,0:T(8,128)(2,1)S(1)}, u32[]{:S(2)}, u32[]{:S(2)}) async-start(bf16[12,8,128]{2,1,0:T(8,128)(2,1)} %broadcast_in_dim.67), calls=%async_computation.2 | async-start | bytes 49152 | tf_op jit(solution)/shard_map/all_to_all | solution.py:36
  94.2 4.4 %collective-permute-start.6 = (bf16[96,512]{1,0:T(8,128)(2,1)S(1)}, bf16[96,512]{1,0:T(8,128)(2,1)S(1)}, u32[]{:S(2)}, u32[]{:S(2)}) collective-permute-start(bf16[96,512]{1,0:T(8,128)(2,1)S(1)} %fusion.43), channel_id=1, source_target_pairs={{0,12},{12,0},{24,36},{36,24},{48,60},{60,48},{72,84},{84,72},{96,... | collective-permute-start | bytes 294920 | tf_op jit(solution)/shard_map/ppermute | solution.py:13
  98.7 8.0 %collective-permute-start.7 = (bf16[96,1024]{1,0:T(8,128)(2,1)S(1)}, bf16[96,1024]{1,0:T(8,128)(2,1)S(1)}, u32[]{:S(2)}, u32[]{:S(2)}) collective-permute-start(bf16[96,1024]{1,0:T(8,128)(2,1)S(1)} %maximum_select_fusion.7), channel_id=1, source_target_pairs={{0,24},{12,36},{24,0},{36,12},{48,72},{60,84},{72,48},{84,60},{96,... | collective-permute-start | bytes 589832 | tf_op jit(solution)/shard_map/ppermute | solution.py:13
  107.9 9.4 %all-to-all-start.3 = ((bf16[12,8,128]{2,1,0:T(8,128)(2,1)}), bf16[12,8,128]{2,1,0:T(8,128)(2,1)S(1)}, u32[]{:S(2)}, u32[]{:S(2)}) async-start(bf16[12,8,128]{2,1,0:T(8,128)(2,1)} %fusion.20), calls=%async_computation.3 | async-start | bytes 49152 | tf_op jit(solution)/shard_map/all_to_all | solution.py:24
  111.6 30.6 %collective-permute-start.10 = (bf16[96,128]{1,0:T(8,128)(2,1)S(1)}, bf16[96,128]{1,0:T(8,128)(2,1)S(1)}, u32[]{:S(2)}, u32[]{:S(2)}) collective-permute-start(bf16[96,128]{1,0:T(8,128)(2,1)S(1)} %slice.70), channel_id=1, source_target_pairs={{0,48},{12,60},{24,72},{36,84},{48,96},{60,108},{72,120},{84,132},... | collective-permute-start | bytes 73736 | tf_op jit(solution)/shard_map/ppermute | solution.py:46
  114.0 53.3 %collective-permute-start.11 = (bf16[96,128]{1,0:T(8,128)(2,1)S(1)}, bf16[96,128]{1,0:T(8,128)(2,1)S(1)}, u32[]{:S(2)}, u32[]{:S(2)}) collective-permute-start(bf16[96,128]{1,0:T(8,128)(2,1)S(1)} %slice.70), channel_id=1, source_target_pairs={{48,0},{60,12},{72,24},{84,36},{96,48},{108,60},{120,72},{132,84},... | collective-permute-start | bytes 73736 | tf_op jit(solution)/shard_map/ppermute | solution.py:46
  118.0 33.4 %all-to-all-start.4 = ((bf16[64,1,8,128]{3,2,1,0:T(8,128)(2,1)}), bf16[64,1,8,128]{3,2,1,0:T(8,128)(2,1)S(1)}, u32[]{:S(2)}, u32[]{:S(2)}) async-start(bf16[64,1,8,128]{3,2,1,0:T(8,128)(2,1)} %broadcast_in_dim.68), calls=%async_computation.4 | async-start | bytes 262144 | tf_op jit(solution)/shard_map/all_to_all | solution.py:36
  136.7 5.6 %collective-permute-start.8 = (bf16[96,192]{1,0:T(8,128)(2,1)S(1)}, bf16[96,192]{1,0:T(8,128)(2,1)S(1)}, u32[]{:S(2)}, u32[]{:S(2)}) collective-permute-start(bf16[96,192]{1,0:T(8,128)(2,1)S(1)} %get-tuple-element.9), channel_id=1, source_target_pairs={{0,48},{12,60},{24,72},{36,84},{48,96},{60,108},{72,120},{84,132},... | collective-permute-start | bytes 110600 | tf_op jit(solution)/shard_map/ppermute | solution.py:46
  140.9 20.3 %collective-permute-start.9 = (bf16[96,192]{1,0:T(8,128)(2,1)S(1)}, bf16[96,192]{1,0:T(8,128)(2,1)S(1)}, u32[]{:S(2)}, u32[]{:S(2)}) collective-permute-start(bf16[96,192]{1,0:T(8,128)(2,1)S(1)} %get-tuple-element.10), channel_id=1, source_target_pairs={{48,0},{60,12},{72,24},{84,36},{96,48},{108,60},{120,72},{132,84},... | collective-permute-start | bytes 110600 | tf_op jit(solution)/shard_map/ppermute | solution.py:46
  154.0 13.1 %all-to-all-start.5 = ((bf16[12,8,128]{2,1,0:T(8,128)(2,1)}), bf16[12,8,128]{2,1,0:T(8,128)(2,1)S(1)}, u32[]{:S(2)}, u32[]{:S(2)}) async-start(bf16[12,8,128]{2,1,0:T(8,128)(2,1)} %broadcast_in_dim.69), calls=%async_computation.5 | async-start | bytes 49152 | tf_op jit(solution)/shard_map/all_to_all | solution.py:36
  167.5 4.7 %collective-permute-start.12 = (bf16[96,512]{1,0:T(8,128)(2,1)S(1)}, bf16[96,512]{1,0:T(8,128)(2,1)S(1)}, u32[]{:S(2)}, u32[]{:S(2)}) collective-permute-start(bf16[96,512]{1,0:T(8,128)(2,1)S(1)} %fusion.44), channel_id=1, source_target_pairs={{0,12},{12,0},{24,36},{36,24},{48,60},{60,48},{72,84},{84,72},{96,... | collective-permute-start | bytes 294920 | tf_op jit(solution)/shard_map/ppermute | solution.py:13
  172.3 8.0 %collective-permute-start.13 = (bf16[96,1024]{1,0:T(8,128)(2,1)S(1)}, bf16[96,1024]{1,0:T(8,128)(2,1)S(1)}, u32[]{:S(2)}, u32[]{:S(2)}) collective-permute-start(bf16[96,1024]{1,0:T(8,128)(2,1)S(1)} %maximum_select_fusion.8), channel_id=1, source_target_pairs={{0,24},{12,36},{24,0},{36,12},{48,72},{60,84},{72,48},{84,60},{96,... | collective-permute-start | bytes 589832 | tf_op jit(solution)/shard_map/ppermute | solution.py:13
  181.7 40.6 %collective-permute-start.16 = (bf16[96,128]{1,0:T(8,128)(2,1)S(1)}, bf16[96,128]{1,0:T(8,128)(2,1)S(1)}, u32[]{:S(2)}, u32[]{:S(2)}) collective-permute-start(bf16[96,128]{1,0:T(8,128)(2,1)S(1)} %slice.73), channel_id=1, source_target_pairs={{0,48},{12,60},{24,72},{36,84},{48,96},{60,108},{72,120},{84,132},... | collective-permute-start | bytes 73736 | tf_op jit(solution)/shard_map/ppermute | solution.py:46
  184.4 68.6 %collective-permute-start.17 = (bf16[96,128]{1,0:T(8,128)(2,1)S(1)}, bf16[96,128]{1,0:T(8,128)(2,1)S(1)}, u32[]{:S(2)}, u32[]{:S(2)}) collective-permute-start(bf16[96,128]{1,0:T(8,128)(2,1)S(1)} %slice.73), channel_id=1, source_target_pairs={{48,0},{60,12},{72,24},{84,36},{96,48},{108,60},{120,72},{132,84},... | collective-permute-start | bytes 73736 | tf_op jit(solution)/shard_map/ppermute | solution.py:46
  185.7 9.8 %all-to-all-start.6 = ((bf16[12,8,128]{2,1,0:T(8,128)(2,1)}), bf16[12,8,128]{2,1,0:T(8,128)(2,1)S(1)}, u32[]{:S(2)}, u32[]{:S(2)}) async-start(bf16[12,8,128]{2,1,0:T(8,128)(2,1)} %fusion.21), calls=%async_computation.6 | async-start | bytes 49152 | tf_op jit(solution)/shard_map/all_to_all | solution.py:24
  189.3 33.2 %collective-permute-start.14 = (bf16[96,192]{1,0:T(8,128)(2,1)S(1)}, bf16[96,192]{1,0:T(8,128)(2,1)S(1)}, u32[]{:S(2)}, u32[]{:S(2)}) collective-permute-start(bf16[96,192]{1,0:T(8,128)(2,1)S(1)} %get-tuple-element.6), channel_id=1, source_target_pairs={{0,48},{12,60},{24,72},{36,84},{48,96},{60,108},{72,120},{84,132},... | collective-permute-start | bytes 110600 | tf_op jit(solution)/shard_map/ppermute | solution.py:46
  194.2 52.7 %collective-permute-start.15 = (bf16[96,192]{1,0:T(8,128)(2,1)S(1)}, bf16[96,192]{1,0:T(8,128)(2,1)S(1)}, u32[]{:S(2)}, u32[]{:S(2)}) collective-permute-start(bf16[96,192]{1,0:T(8,128)(2,1)S(1)} %get-tuple-element.8), channel_id=1, source_target_pairs={{48,0},{60,12},{72,24},{84,36},{96,48},{108,60},{120,72},{132,84},... | collective-permute-start | bytes 110600 | tf_op jit(solution)/shard_map/ppermute | solution.py:46
  196.2 41.0 %all-to-all-start.7 = ((bf16[64,1,8,128]{3,2,1,0:T(8,128)(2,1)}), bf16[64,1,8,128]{3,2,1,0:T(8,128)(2,1)S(1)}, u32[]{:S(2)}, u32[]{:S(2)}) async-start(bf16[64,1,8,128]{3,2,1,0:T(8,128)(2,1)} %broadcast_in_dim.70), calls=%async_computation.7 | async-start | bytes 262144 | tf_op jit(solution)/shard_map/all_to_all | solution.py:36
  239.7 13.1 %all-to-all-start.8 = ((bf16[12,8,128]{2,1,0:T(8,128)(2,1)}), bf16[12,8,128]{2,1,0:T(8,128)(2,1)S(1)}, u32[]{:S(2)}, u32[]{:S(2)}) async-start(bf16[12,8,128]{2,1,0:T(8,128)(2,1)} %broadcast_in_dim.71), calls=%async_computation.8 | async-start | bytes 49152 | tf_op jit(solution)/shard_map/all_to_all | solution.py:36
where the time goes:
time: 255 us; the launch traced here: 254 us
  starting transfers between devices  150 us (59%)
  waiting for transfers between devices  74.1 us (29%)
  matrix products  11.1 us (4%)
  local copies, waits for them, and re-layouts  11 us (4%)
  other arithmetic  6.68 us (3%)
    all_to_all x6, starting transfers between devices, copy_for_each(): return lax.all_to_all(copies, axis, split_axis=0, concat_axis=0, tiled=True)  85.7 us
    all_to_all x6, waiting for transfers between devices, copy_for_each(): return lax.all_to_all(copies, axis, split_axis=0, concat_axis=0, tiled=True)  47.3 us
    ppermute x12, starting transfers between devices, shifted(): lax.ppermute(value, axis, [(source, source + steps) for source in range(f...  27.4 us
    ppermute x6, starting transfers between devices, from_partner(): return lax.ppermute(value, axis, pairs)  26.6 us
    ppermute x6, waiting for transfers between devices, from_partner(): return lax.ppermute(value, axis, pairs)  18.9 us
    all_to_all x3, starting transfers between devices, sent_and_summed(): lax.all_to_all(pieces, axis, split_axis=0, concat_axis=0, tiled=True)  10.6 us
    all_to_all x3, waiting for transfers between devices, sent_and_summed(): lax.all_to_all(pieces, axis, split_axis=0, concat_axis=0, tiled=True)  7.83 us
    dot_general x3, matrix products, per_device(): jnp.einsum('nkr,nrt->kt', block_rows, chosen, preferred_element_type=jnp....  5.9 us
  transfers between devices with their start and end apart: 27, of which 13 were waited for; matrix products, arithmetic and copies ran while one was open for 10% of the time, Pallas kernels for 0%

commit v1 on v0

v1 whole, which is shorter than its diff:
```python
import jax
import jax.numpy as jnp
from jax import lax
from jax.sharding import Mesh, PartitionSpec as P

FACE_Q = 192
ITERS = 3
F32, BF16 = jnp.float32, jnp.bfloat16

LAYER = ("zh", "yh")
QUARTER = ("yl", "core")
SUB = LAYER + QUARTER
GRP = ("zl", "x")


def dot(a, b):
    return jnp.dot(a, b, preferred_element_type=F32)


def side_by_side(pieces):
    return jnp.concatenate([pieces[i] for i in range(pieces.shape[0])], axis=-1)


def copies_to(value, axes):
    copies = jnp.broadcast_to(value, (lax.axis_size(axes), *value.shape))
    return lax.all_to_all(copies, axes, 0, 0, tiled=True)


def shifted(value, steps):
    count = lax.axis_size(SUB)
    first, last = max(0, -steps), min(count, count - steps)
    return lax.ppermute(value, SUB, [(s, s + steps) for s in range(first, last)])


def per_device(
    impedance,
    incident,
    face_order,
    near_tiles,
    basis_right,
    rank_scale,
    rank_counts,
    coupling,
    basis_left,
):
    z_cols = impedance[0, 0]
    source = incident[0, 0]
    tiles = near_tiles[0, 0]
    right_basis = basis_right[0, 0]
    left_basis = basis_left[0, 0]
    n_layers, rank, _ = coupling.shape[1:]
    n_exc, width = source.shape
    layer = lax.axis_index(LAYER)
    quarter = lax.axis_index(QUARTER)
    n_q = lax.axis_size(QUARTER)
    n_g = lax.axis_size(GRP)
    rows = n_exc // n_q

    near = lax.all_gather(source, QUARTER)
    y_now = dot(side_by_side(near), z_cols)

    kept = jnp.where(jnp.arange(rank) < rank_counts[layer], rank_scale[0], F32(0.0))
    others = (jnp.arange(n_layers) != layer)[:, None, None]
    own = jnp.where(others, coupling[0], jnp.zeros_like(coupling[0]))
    own = jnp.concatenate([own.reshape(n_layers * rank, rank), left_basis], 0)
    of_all = copies_to(own, QUARTER)
    couple = side_by_side(of_all[:, : n_layers * rank])
    left = of_all[:, n_layers * rank :]
    z_outer = z_cols.reshape(n_q, width, width)[:, 2 * FACE_Q :]
    far_to_y = jnp.einsum("qrt,qtc->qrc", left, z_outer, preferred_element_type=F32)
    far_to_y = far_to_y.reshape(n_q * rank, width).astype(BF16)
    reorder = jax.nn.one_hot(face_order[0, 0], FACE_Q, axis=0, dtype=BF16)

    for sweep in range(ITERS):
        outgoing = y_now.astype(BF16)
        outer_out = outgoing[:, 2 * FACE_Q :]
        partial = (dot(outer_out, right_basis) * kept).astype(BF16)
        parts = jnp.broadcast_to(
            partial.reshape(n_q, 1, rows, rank), (n_q, n_g, rows, rank)
        ).reshape(n_q * n_g, rows, rank)
        arrived = lax.all_to_all(parts, QUARTER + GRP, 0, 0, tiled=True)
        below = shifted(outgoing[:, FACE_Q:], 4)
        above = shifted(jnp.concatenate([outgoing[:, :FACE_Q], outer_out], 1), -4)
        coefs = arrived.astype(F32).sum(0).astype(BF16)
        of_layers = copies_to(coefs, LAYER)
        lower_in = dot(below[:, :FACE_Q], reorder)
        lower_above = above[:, :FACE_Q].astype(F32)
        outer_in = dot(outer_out, tiles[0]) + dot(below[:, FACE_Q:], tiles[1])
        outer_in = outer_in + dot(above[:, FACE_Q:], tiles[2])
        near = jnp.concatenate([lower_in, lower_above, outer_in], 1) + source.astype(F32)
        far = dot(side_by_side(of_layers), couple).astype(BF16)
        if sweep < ITERS - 1:
            both = jnp.concatenate([near.astype(BF16), far], 0)
            both = lax.all_gather(both, QUARTER)
            far = both[:, n_exc:].reshape(n_exc, width)
            y_now = dot(side_by_side(both[:, :n_exc]), z_cols) + dot(far, far_to_y)
        else:
            far = lax.all_gather(far, QUARTER).reshape(n_exc, width)
            far = lax.dynamic_slice_in_dim(far, quarter * rank, rank, 1)
            far = dot(far, left_basis)
            outer = near[:, 2 * FACE_Q :] + far
            trace = jnp.concatenate([near[:, : 2 * FACE_Q], outer], 1)
    return trace.astype(BF16)[None, None]


def solution(mesh):
    finer = Mesh(mesh.devices.reshape(4, 4, 2, 2, 3, 4), SUB + GRP)
    placed = (
        P(SUB, GRP, None, None),
        P(SUB, GRP, None, None),
        P(SUB, GRP, None),
        P(SUB, GRP, None, None, None),
        P(SUB, GRP, None, None),
        P(SUB, None),
        P(),
        P(SUB, None, None, None),
        P(SUB, GRP, None, None),
    )
    return jax.shard_map(
        per_device,
        mesh=finer,
        in_specs=placed,
        out_specs=P(SUB, GRP, None, None),
        check_vma=False,
    )
```

time: 255 us -> 231 us (0.906)
  starting transfers between devices: 150 us -> 78.6 us
  blocking collectives: 0 us -> 44.2 us
  waiting for transfers between devices: 74.1 us -> 85.4 us
  matrix products: 11.1 us -> 7.48 us
  other arithmetic: 6.68 us -> 3.93 us
    all_gather x0 -> x4, blocking collectives: none -> 44.2 us  [the longest x2 20.4 us: per_device(): both = lax.all_gather(both, QUARTER)]
    ppermute x18 -> x6, starting transfers between devices: 54.1 us -> 16.1 us  [shifted(): lax.ppermute(value, SUB, [(s, s + steps) for s in range(first, last)])]
    all_to_all x9 -> x7, starting transfers between devices: 96.3 us -> 62.5 us  [the longest x4 46.2 us: copies_to(): return lax.all_to_all(copies, axes, 0, 0, tiled=True)]
    all_to_all x9 -> x7, waiting for transfers between devices: 55.2 us -> 80.8 us  [the longest x4 64.9 us: copies_to(): return lax.all_to_all(copies, axes, 0, 0, tiled=True)]
    ppermute x18 -> x6, waiting for transfers between devices: 19 us -> 4.62 us  [shifted(): lax.ppermute(value, SUB, [(s, s + steps) for s in range(first, last)])]
    gather x7 -> x0, local copies, waits for them, and re-layouts: 5.91 us -> none  [the longest x1 3.23 us: per_device(): chosen = jnp.take(couple_rows, sources, axis=0)]
    select_n x6 -> x1, other arithmetic: 4.18 us -> 0.34 us  [per_device(): own = jnp.where(others, coupling[0], jnp.zeros_like(coupling[0]))]
    dot_general x21 -> x25, matrix products: 11.1 us -> 7.48 us  [the longest x24 7.2 us: dot(): return jnp.dot(a, b, preferred_element_type=F32)]
  transfers between devices with their start and end apart: 27 -> 13, of which waited for: 13 -> 8; matrix products, arithmetic and copies ran while one was open for 10% -> 3% of each run, Pallas kernels for 0% -> 0%
where the time goes in v1:
time: 231 us; the launch traced here: 230 us
  waiting for transfers between devices  85.4 us (37%)
  starting transfers between devices  78.6 us (34%)
  blocking collectives  44.2 us (19%)
  local copies, waits for them, and re-layouts  9.47 us (4%)
  matrix products  7.48 us (3%)
  other arithmetic  3.93 us (2%)
    all_to_all x4, waiting for transfers between devices, copies_to(): return lax.all_to_all(copies, axes, 0, 0, tiled=True)  64.9 us
    all_to_all x4, starting transfers between devices, copies_to(): return lax.all_to_all(copies, axes, 0, 0, tiled=True)  46.2 us
    all_gather x2, blocking collectives, per_device(): both = lax.all_gather(both, QUARTER)  20.4 us
    all_gather x1, blocking collectives, per_device(): near = lax.all_gather(source, QUARTER)  16.8 us
    all_to_all x3, starting transfers between devices, per_device(): arrived = lax.all_to_all(parts, QUARTER + GRP, 0, 0, tiled=True)  16.2 us
    ppermute x6, starting transfers between devices, shifted(): lax.ppermute(value, SUB, [(s, s + steps) for s in range(first, last)])  16.1 us
    all_to_all x3, waiting for transfers between devices, per_device(): arrived = lax.all_to_all(parts, QUARTER + GRP, 0, 0, tiled=True)  15.9 us
    dot_general x24, matrix products, dot(): return jnp.dot(a, b, preferred_element_type=F32)  7.2 us
  transfers between devices with their start and end apart: 13, of which 8 were waited for; matrix products, arithmetic and copies ran while one was open for 3% of the time, Pallas kernels for 0%

profile of v1, /device:TPU:1, one launch (start us, length us, event | category | flops | bytes accessed | tf_op | source)
XLA Modules:
  0.0 229.8 jit_solution(10731758689723699160)
XLA Ops:
  0.0 16.8 %all-gather = bf16[4,1,96,512]{3,2,1,0:T(8,128)(2,1)S(1)} all-gather(bf16[1,1,96,512]{3,2,1,0:T(8,128)(2,1)} %param.10), channel_id=2, replica_groups=mesh['zh'=4,'yh'=4,'yl'=2,'core'=2,'zl'=3,'x'=4] {'yl','core'}, dimensions={0}, use_global_device_ids=true | all-gather | bytes 491520 | tf_op jit(solution)/shard_map/all_gather | solution.py:59
  16.9 2.1 fusion.18
  19.1 1.3 collective-permute-start.1
  20.5 4.9 %collective-permute-start = (bf16[96,320]{1,0:T(8,128)(2,1)S(1)}, bf16[96,320]{1,0:T(8,128)(2,1)S(1)}, u32[]{:S(2)}, u32[]{:S(2)}) collective-permute-start(bf16[96,320]{1,0:T(8,128)(2,1)S(1)} %slice.409), channel_id=1, source_target_pairs={{0,48},{12,60},{24,72},{36,84},{48,96},{60,108},{72,120},{84,132},... | collective-permute-start | bytes 184328 | tf_op jit(solution)/shard_map/ppermute | solution.py:32
  25.5 0.6 dynamic_slice.6
  26.0 0.6 fusion.92
  26.9 0.8 broadcast_in_dim.61
  27.6 5.0 %all-to-all-start = ((bf16[48,24,128]{2,1,0:T(8,128)(2,1)}), bf16[48,24,128]{2,1,0:T(8,128)(2,1)S(1)}, u32[]{:S(2)}, u32[]{:S(2)}) async-start(bf16[48,24,128]{2,1,0:T(8,128)(2,1)} %bitcast.14), calls=%async_computation | async-start | bytes 589824 | tf_op jit(solution)/shard_map/all_to_all | solution.py:81
  32.7 0.3 bitcast_select_fusion
  33.8 7.7 %all-to-all-done = bf16[48,24,128]{2,1,0:T(8,128)(2,1)S(1)} async-done(((bf16[48,24,128]{2,1,0:T(8,128)(2,1)}), bf16[48,24,128]{2,1,0:T(8,128)(2,1)S(1)}, u32[]{:S(2)}, u32[]{:S(2)}) %all-to-all-start) | async-done | bytes 294944 | tf_op jit(solution)/shard_map/all_to_all | solution.py:81
  41.6 0.7 broadcast_in_dim.62
  42.2 17.6 %all-to-all-start.1 = ((bf16[16,24,128]{2,1,0:T(8,128)(2,1)}), bf16[16,24,128]{2,1,0:T(8,128)(2,1)S(1)}, u32[]{:S(2)}, u32[]{:S(2)}) async-start(bf16[16,24,128]{2,1,0:T(8,128)(2,1)} %broadcast_in_dim.62), calls=%async_computation.1 | async-start | bytes 196608 | tf_op jit(solution)/shard_map/all_to_all | solution.py:26
  59.9 0.7 fusion.48
  60.6 13.0 %all-to-all-done.1 = bf16[16,24,128]{2,1,0:T(8,128)(2,1)S(1)} async-done(((bf16[16,24,128]{2,1,0:T(8,128)(2,1)}), bf16[16,24,128]{2,1,0:T(8,128)(2,1)S(1)}, u32[]{:S(2)}, u32[]{:S(2)}) %all-to-all-start.1) | async-done | bytes 98336 | tf_op jit(solution)/shard_map/all_to_all | solution.py:26
  73.6 1.7 broadcast_in_dim.67
  75.3 5.4 %all-to-all-start.2 = ((bf16[4,2176,128]{2,1,0:T(8,128)(2,1)}), bf16[4,2176,128]{2,1,0:T(8,128)(2,1)S(1)}, u32[]{:S(2)}, u32[]{:S(2)}) async-start(bf16[4,2176,128]{2,1,0:T(8,128)(2,1)} %broadcast_in_dim.67), calls=%async_computation.2 | async-start | bytes 4456448 | tf_op jit(solution)/shard_map/all_to_all | solution.py:26
  80.9 0.6 copy-done.20
  81.5 25.4 %all-to-all-done.2 = bf16[4,2176,128]{2,1,0:T(8,128)(2,1)S(1)} async-done(((bf16[4,2176,128]{2,1,0:T(8,128)(2,1)}), bf16[4,2176,128]{2,1,0:T(8,128)(2,1)S(1)}, u32[]{:S(2)}, u32[]{:S(2)}) %all-to-all-start.2) | async-done | bytes 2228256 | tf_op jit(solution)/shard_map/all_to_all | solution.py:26
  107.1 0.7 copy-done.21
  107.8 0.4 convolution_convert_fusion.3
  108.3 0.5 copy-done.10
  108.7 7.1 %all-gather.1 = bf16[480,512]{1,0:T(8,128)(2,1)S(1)} all-gather(bf16[120,512]{1,0:T(8,128)(2,1)S(1)} %pad_maximum_fusion.2), channel_id=3, replica_groups=mesh['zh'=4,'yh'=4,'yl'=2,'core'=2,'zl'=3,'x'=4] {'yl','core'}, dimensions={0}, use_global_device_ids=true | all-gather | bytes 614400 | tf_op jit(solution)/shard_map/all_gather | solution.py:94
  115.9 0.3 convolution_convert_fusion
  116.4 0.5 fusion.15
  117.1 0.8 broadcast_in_dim.69
  117.8 5.5 %all-to-all-start.3 = ((bf16[48,24,128]{2,1,0:T(8,128)(2,1)}), bf16[48,24,128]{2,1,0:T(8,128)(2,1)S(1)}, u32[]{:S(2)}, u32[]{:S(2)}) async-start(bf16[48,24,128]{2,1,0:T(8,128)(2,1)} %bitcast.47), calls=%async_computation.3 | async-start | bytes 589824 | tf_op jit(solution)/shard_map/all_to_all | solution.py:81
  123.6 2.4 %collective-permute-start.2 = (bf16[96,320]{1,0:T(8,128)(2,1)S(1)}, bf16[96,320]{1,0:T(8,128)(2,1)S(1)}, u32[]{:S(2)}, u32[]{:S(2)}) collective-permute-start(bf16[96,320]{1,0:T(8,128)(2,1)S(1)} %slice.443), channel_id=1, source_target_pairs={{0,48},{12,60},{24,72},{36,84},{48,96},{60,108},{72,120},{84,132},... | collective-permute-start | bytes 184328 | tf_op jit(solution)/shard_map/ppermute | solution.py:32
  126.2 1.3 collective-permute-start.3
  127.5 0.3 collective-permute-done.2
  128.1 4.3 %collective-permute-done.3 = bf16[96,320]{1,0:T(8,128)(2,1)S(1)} collective-permute-done((bf16[96,320]{1,0:T(8,128)(2,1)S(1)}, bf16[96,320]{1,0:T(8,128)(2,1)S(1)}, u32[]{:S(2)}, u32[]{:S(2)}) %collective-permute-start.3) | collective-permute-done | bytes 61472 | tf_op jit(solution)/shard_map/ppermute | solution.py:32
  132.7 0.7 broadcast_in_dim.70
  133.3 14.2 %all-to-all-start.4 = ((bf16[16,24,128]{2,1,0:T(8,128)(2,1)}), bf16[16,24,128]{2,1,0:T(8,128)(2,1)S(1)}, u32[]{:S(2)}, u32[]{:S(2)}) async-start(bf16[16,24,128]{2,1,0:T(8,128)(2,1)} %broadcast_in_dim.70), calls=%async_computation.4 | async-start | bytes 196608 | tf_op jit(solution)/shard_map/all_to_all | solution.py:26
  147.6 0.8 slice_convert_fusion.2
  148.5 12.8 %all-to-all-done.4 = bf16[16,24,128]{2,1,0:T(8,128)(2,1)S(1)} async-done(((bf16[16,24,128]{2,1,0:T(8,128)(2,1)}), bf16[16,24,128]{2,1,0:T(8,128)(2,1)S(1)}, u32[]{:S(2)}, u32[]{:S(2)}) %all-to-all-start.4) | async-done | bytes 98336 | tf_op jit(solution)/shard_map/all_to_all | solution.py:26
  161.6 0.4 convolution_convert_fusion.2
  162.0 13.3 %all-gather.2 = bf16[480,512]{1,0:T(8,128)(2,1)S(1)} all-gather(bf16[120,512]{1,0:T(8,128)(2,1)S(1)} %pad_maximum_fusion.3), channel_id=4, replica_groups=mesh['zh'=4,'yh'=4,'yl'=2,'core'=2,'zl'=3,'x'=4] {'yl','core'}, dimensions={0}, use_global_device_ids=true | all-gather | bytes 614400 | tf_op jit(solution)/shard_map/all_gather | solution.py:94
  175.5 0.5 fusion.12
  176.2 1.3 collective-permute-start.5
  177.8 4.9 %collective-permute-start.4 = (bf16[96,320]{1,0:T(8,128)(2,1)S(1)}, bf16[96,320]{1,0:T(8,128)(2,1)S(1)}, u32[]{:S(2)}, u32[]{:S(2)}) collective-permute-start(bf16[96,320]{1,0:T(8,128)(2,1)S(1)} %slice.471), channel_id=1, source_target_pairs={{0,48},{12,60},{24,72},{36,84},{48,96},{60,108},{72,120},{84,132},... | collective-permute-start | bytes 184328 | tf_op jit(solution)/shard_map/ppermute | solution.py:32
  182.7 0.8 broadcast_in_dim.72
  183.4 5.7 %all-to-all-start.5 = ((bf16[48,24,128]{2,1,0:T(8,128)(2,1)}), bf16[48,24,128]{2,1,0:T(8,128)(2,1)S(1)}, u32[]{:S(2)}, u32[]{:S(2)}) async-start(bf16[48,24,128]{2,1,0:T(8,128)(2,1)} %bitcast.72), calls=%async_computation.5 | async-start | bytes 589824 | tf_op jit(solution)/shard_map/all_to_all | solution.py:81
  189.7 8.2 %all-to-all-done.5 = bf16[48,24,128]{2,1,0:T(8,128)(2,1)S(1)} async-done(((bf16[48,24,128]{2,1,0:T(8,128)(2,1)}), bf16[48,24,128]{2,1,0:T(8,128)(2,1)S(1)}, u32[]{:S(2)}, u32[]{:S(2)}) %all-to-all-start.5) | async-done | bytes 294944 | tf_op jit(solution)/shard_map/all_to_all | solution.py:81
  198.0 0.7 broadcast_in_dim.73
  198.7 9.0 %all-to-all-start.6 = ((bf16[16,24,128]{2,1,0:T(8,128)(2,1)}), bf16[16,24,128]{2,1,0:T(8,128)(2,1)S(1)}, u32[]{:S(2)}, u32[]{:S(2)}) async-start(bf16[16,24,128]{2,1,0:T(8,128)(2,1)} %broadcast_in_dim.73), calls=%async_computation.6 | async-start | bytes 196608 | tf_op jit(solution)/shard_map/all_to_all | solution.py:26
  207.8 13.6 %all-to-all-done.6 = bf16[16,24,128]{2,1,0:T(8,128)(2,1)S(1)} async-done(((bf16[16,24,128]{2,1,0:T(8,128)(2,1)}), bf16[16,24,128]{2,1,0:T(8,128)(2,1)S(1)}, u32[]{:S(2)}, u32[]{:S(2)}) %all-to-all-start.6) | async-done | bytes 98336 | tf_op jit(solution)/shard_map/all_to_all | solution.py:26
  221.6 0.4 convolution_convert_fusion.1
  222.0 7.0 %all-gather.3 = bf16[96,512]{1,0:T(8,128)(2,1)S(1)} all-gather(bf16[24,512]{1,0:T(8,128)(2,1)S(1)} %convolution_convert_fusion.1), channel_id=5, replica_groups=mesh['zh'=4,'yh'=4,'yl'=2,'core'=2,'zl'=3,'x'=4] {'yl','core'}, dimensions={0}, use_global_device_ids=true | all-gather | bytes 122880 | tf_op jit(solution)/shard_map/all_gather | solution.py:98
  229.2 0.7 pad_maximum_fusion.4
  (147 shorter events, 4.9 us)
Async XLA Ops:
  0.0 26.7 %copy-start = (bf16[1,1,128,128]{3,2,1,0:T(8,128)(2,1)S(1)}, bf16[1,1,128,128]{3,2,1,0:T(8,128)(2,1)}, u32[]{:S(2)}) copy-start(bf16[1,1,128,128]{3,2,1,0:T(8,128)(2,1)} %param.13) | copy-start | bytes 98308
  16.8 8.6 %copy-start.22 = (s32[16]{0:T(128)S(1)}, s32[16]{0:T(128)}, u32[]{:S(2)}) copy-start(s32[16]{0:T(128)} %param.15) | copy-start | bytes 196
  16.8 9.2 %copy-start.23 = (f32[1,128]{1,0:T(1,128)S(1)}, f32[1,128]{1,0:T(1,128)}, u32[]{:S(2)}) copy-start(f32[1,128]{1,0:T(1,128)} %param.14) | copy-start | bytes 1540
  16.9 15.9 %copy-start.3 = (bf16[1,16,128,128]{3,2,1,0:T(8,128)(2,1)S(1)}, bf16[1,16,128,128]{3,2,1,0:T(8,128)(2,1)}, u32[]{:S(2)}) copy-start(bf16[1,16,128,128]{3,2,1,0:T(8,128)(2,1)} %param.16) | copy-start | bytes 1572868
  16.9 16.2 %copy-start.13 = (bf16[1,1,128,128]{3,2,1,0:T(8,128)(2,1)S(1)}, bf16[1,1,128,128]{3,2,1,0:T(8,128)(2,1)}, u32[]{:S(2)}) copy-start(bf16[1,1,128,128]{3,2,1,0:T(8,128)(2,1)} %param.17) | copy-start | bytes 98308
  19.0 14.1 %copy-start.2 = (bf16[1,1,3,128,128]{4,3,2,1,0:T(8,128)(2,1)S(1)}, bf16[1,1,3,128,128]{4,3,2,1,0:T(8,128)(2,1)}, u32[]{:S(2)}) copy-start(bf16[1,1,3,128,128]{4,3,2,1,0:T(8,128)(2,1)} %param.12) | copy-start | bytes 294916
  19.0 14.5 %copy-start.16 = (s32[1,1,192]{2,1,0:T(1,128)S(1)}, s32[1,1,192]{2,1,0:T(1,128)}, u32[]{:S(2)}) copy-start(s32[1,1,192]{2,1,0:T(1,128)} %param.11) | copy-start | bytes 2308
  19.1 14.5 %collective-permute-start.1 = (bf16[96,320]{1,0:T(8,128)(2,1)S(1)}, bf16[96,320]{1,0:T(8,128)(2,1)S(1)}, u32[]{:S(2)}, u32[]{:S(2)}) collective-permute-start(bf16[96,320]{1,0:T(8,128)(2,1)S(1)} %pad_maximum_fusion.5), channel_id=1, source_target_pairs={{48,0},{60,12},{72,24},{84,36},{96,48},{108,60},{120,72},{132,84},... | collective-permute-start | bytes 184328 | tf_op jit(solution)/shard_map/ppermute | solution.py:32
  20.5 12.7 %collective-permute-start = (bf16[96,320]{1,0:T(8,128)(2,1)S(1)}, bf16[96,320]{1,0:T(8,128)(2,1)S(1)}, u32[]{:S(2)}, u32[]{:S(2)}) collective-permute-start(bf16[96,320]{1,0:T(8,128)(2,1)S(1)} %slice.409), channel_id=1, source_target_pairs={{0,48},{12,60},{24,72},{36,84},{48,96},{60,108},{72,120},{84,132},... | collective-permute-start | bytes 184328 | tf_op jit(solution)/shard_map/ppermute | solution.py:32
  26.7 90.2 %copy-start.18 = (f32[128]{0:T(128)}, f32[128]{0:T(128)S(1)}, u32[]{:S(2)}) copy-start(f32[128]{0:T(128)S(1)} %fusion.92) | copy-start | bytes 1540
  27.6 32.2 %copy-start.1 = (bf16[1,1,96,512]{3,2,1,0:T(8,128)(2,1)S(1)}, bf16[1,1,96,512]{3,2,1,0:T(8,128)(2,1)}, u32[]{:S(2)}) copy-start(bf16[1,1,96,512]{3,2,1,0:T(8,128)(2,1)} %param.10) | copy-start | bytes 294916
  27.6 13.9 %all-to-all-start = ((bf16[48,24,128]{2,1,0:T(8,128)(2,1)}), bf16[48,24,128]{2,1,0:T(8,128)(2,1)S(1)}, u32[]{:S(2)}, u32[]{:S(2)}) async-start(bf16[48,24,128]{2,1,0:T(8,128)(2,1)} %bitcast.14), calls=%async_computation | async-start | bytes 589824 | tf_op jit(solution)/shard_map/all_to_all | solution.py:81
  42.2 31.4 %all-to-all-start.1 = ((bf16[16,24,128]{2,1,0:T(8,128)(2,1)}), bf16[16,24,128]{2,1,0:T(8,128)(2,1)S(1)}, u32[]{:S(2)}, u32[]{:S(2)}) async-start(bf16[16,24,128]{2,1,0:T(8,128)(2,1)} %broadcast_in_dim.62), calls=%async_computation.1 | async-start | bytes 196608 | tf_op jit(solution)/shard_map/all_to_all | solution.py:26
  75.3 31.7 %all-to-all-start.2 = ((bf16[4,2176,128]{2,1,0:T(8,128)(2,1)}), bf16[4,2176,128]{2,1,0:T(8,128)(2,1)S(1)}, u32[]{:S(2)}, u32[]{:S(2)}) async-start(bf16[4,2176,128]{2,1,0:T(8,128)(2,1)} %broadcast_in_dim.67), calls=%async_computation.2 | async-start | bytes 4456448 | tf_op jit(solution)/shard_map/all_to_all | solution.py:26
  80.9 0.6 copy-start.20
  106.9 0.9 copy-start.21
  107.1 1.2 copy-start.4
  107.1 1.2 copy-start.6
  107.1 1.2 copy-start.8
  107.8 0.9 copy-start.10
  107.8 8.1 %copy-start.11 = (bf16[1,1,2048,512]{3,2,1,0:T(8,128)(2,1)S(1)}, bf16[1,1,2048,512]{3,2,1,0:T(8,128)(2,1)}, u32[]{:S(2)}) copy-start(bf16[1,1,2048,512]{3,2,1,0:T(8,128)(2,1)} %param.9) | copy-start | bytes 6291460
  116.9 44.6 %copy-start.5 = (bf16[2048,128]{1,0:T(8,128)(2,1)S(1)}, bf16[2048,128]{1,0:T(8,128)(2,1)}, u32[]{:S(2)}) copy-start(bf16[2048,128]{1,0:T(8,128)(2,1)} %copy-done.4) | copy-start | bytes 1572868
  116.9 44.6 %copy-start.7 = (bf16[2048,128]{1,0:T(8,128)(2,1)S(1)}, bf16[2048,128]{1,0:T(8,128)(2,1)}, u32[]{:S(2)}) copy-start(bf16[2048,128]{1,0:T(8,128)(2,1)} %copy-done.6) | copy-start | bytes 1572868
  116.9 44.6 %copy-start.9 = (bf16[2048,128]{1,0:T(8,128)(2,1)S(1)}, bf16[2048,128]{1,0:T(8,128)(2,1)}, u32[]{:S(2)}) copy-start(bf16[2048,128]{1,0:T(8,128)(2,1)} %copy-done.8) | copy-start | bytes 1572868
  117.8 14.8 %all-to-all-start.3 = ((bf16[48,24,128]{2,1,0:T(8,128)(2,1)}), bf16[48,24,128]{2,1,0:T(8,128)(2,1)S(1)}, u32[]{:S(2)}, u32[]{:S(2)}) async-start(bf16[48,24,128]{2,1,0:T(8,128)(2,1)} %bitcast.47), calls=%async_computation.3 | async-start | bytes 589824 | tf_op jit(solution)/shard_map/all_to_all | solution.py:81
  123.6 4.1 %collective-permute-start.2 = (bf16[96,320]{1,0:T(8,128)(2,1)S(1)}, bf16[96,320]{1,0:T(8,128)(2,1)S(1)}, u32[]{:S(2)}, u32[]{:S(2)}) collective-permute-start(bf16[96,320]{1,0:T(8,128)(2,1)S(1)} %slice.443), channel_id=1, source_target_pairs={{0,48},{12,60},{24,72},{36,84},{48,96},{60,108},{72,120},{84,132},... | collective-permute-start | bytes 184328 | tf_op jit(solution)/shard_map/ppermute | solution.py:32
  126.2 6.3 %collective-permute-start.3 = (bf16[96,320]{1,0:T(8,128)(2,1)S(1)}, bf16[96,320]{1,0:T(8,128)(2,1)S(1)}, u32[]{:S(2)}, u32[]{:S(2)}) collective-permute-start(bf16[96,320]{1,0:T(8,128)(2,1)S(1)} %pad_maximum_fusion.6), channel_id=1, source_target_pairs={{48,0},{60,12},{72,24},{84,36},{96,48},{108,60},{120,72},{132,84},... | collective-permute-start | bytes 184328 | tf_op jit(solution)/shard_map/ppermute | solution.py:32
  132.4 0.9 copy-start.15
  133.3 28.0 %all-to-all-start.4 = ((bf16[16,24,128]{2,1,0:T(8,128)(2,1)}), bf16[16,24,128]{2,1,0:T(8,128)(2,1)S(1)}, u32[]{:S(2)}, u32[]{:S(2)}) async-start(bf16[16,24,128]{2,1,0:T(8,128)(2,1)} %broadcast_in_dim.70), calls=%async_computation.4 | async-start | bytes 196608 | tf_op jit(solution)/shard_map/all_to_all | solution.py:26
  162.0 13.6 %copy-start.12 = (bf16[1,1,2048,512]{3,2,1,0:T(8,128)(2,1)S(1)}, bf16[1,1,2048,512]{3,2,1,0:T(8,128)(2,1)}, u32[]{:S(2)}) copy-start(bf16[1,1,2048,512]{3,2,1,0:T(8,128)(2,1)} %param.9) | copy-start | bytes 6291460
  175.3 2.3 copy-start.19
  175.5 13.7 %copy-start.17 = (s32[1,1,192]{2,1,0:T(1,128)S(1)}, s32[1,1,192]{2,1,0:T(1,128)}, u32[]{:S(2)}) copy-start(s32[1,1,192]{2,1,0:T(1,128)} %param.11) | copy-start | bytes 2308
  176.2 12.9 %collective-permute-start.5 = (bf16[96,320]{1,0:T(8,128)(2,1)S(1)}, bf16[96,320]{1,0:T(8,128)(2,1)S(1)}, u32[]{:S(2)}, u32[]{:S(2)}) collective-permute-start(bf16[96,320]{1,0:T(8,128)(2,1)S(1)} %pad_maximum_fusion.7), channel_id=1, source_target_pairs={{48,0},{60,12},{72,24},{84,36},{96,48},{108,60},{120,72},{132,84},... | collective-permute-start | bytes 184328 | tf_op jit(solution)/shard_map/ppermute | solution.py:32
  177.8 11.4 %collective-permute-start.4 = (bf16[96,320]{1,0:T(8,128)(2,1)S(1)}, bf16[96,320]{1,0:T(8,128)(2,1)S(1)}, u32[]{:S(2)}, u32[]{:S(2)}) collective-permute-start(bf16[96,320]{1,0:T(8,128)(2,1)S(1)} %slice.471), channel_id=1, source_target_pairs={{0,48},{12,60},{24,72},{36,84},{48,96},{60,108},{72,120},{84,132},... | collective-permute-start | bytes 184328 | tf_op jit(solution)/shard_map/ppermute | solution.py:32
  183.4 14.5 %all-to-all-start.5 = ((bf16[48,24,128]{2,1,0:T(8,128)(2,1)}), bf16[48,24,128]{2,1,0:T(8,128)(2,1)S(1)}, u32[]{:S(2)}, u32[]{:S(2)}) async-start(bf16[48,24,128]{2,1,0:T(8,128)(2,1)} %bitcast.72), calls=%async_computation.5 | async-start | bytes 589824 | tf_op jit(solution)/shard_map/all_to_all | solution.py:81
  198.7 22.8 %all-to-all-start.6 = ((bf16[16,24,128]{2,1,0:T(8,128)(2,1)}), bf16[16,24,128]{2,1,0:T(8,128)(2,1)S(1)}, u32[]{:S(2)}, u32[]{:S(2)}) async-start(bf16[16,24,128]{2,1,0:T(8,128)(2,1)} %broadcast_in_dim.73), calls=%async_computation.6 | async-start | bytes 196608 | tf_op jit(solution)/shard_map/all_to_all | solution.py:26
  221.6 7.4 %copy-start.14 = (bf16[1,1,128,128]{3,2,1,0:T(8,128)(2,1)S(1)}, bf16[1,1,128,128]{3,2,1,0:T(8,128)(2,1)}, u32[]{:S(2)}) copy-start(bf16[1,1,128,128]{3,2,1,0:T(8,128)(2,1)} %param.17) | copy-start | bytes 98308

commit v2 on v1

--- a/solution.py
+++ b/solution.py
@@ -11,6 +11,8 @@
 QUARTER = ("yl", "core")
 SUB = LAYER + QUARTER
 GRP = ("zl", "x")
+FIRST = QUARTER + ("x",)
+SECOND = LAYER + ("zl",)
 
 
 def dot(a, b):
@@ -21,9 +23,13 @@
     return jnp.concatenate([pieces[i] for i in range(pieces.shape[0])], axis=-1)
 
 
-def copies_to(value, axes):
-    copies = jnp.broadcast_to(value, (lax.axis_size(axes), *value.shape))
-    return lax.all_to_all(copies, axes, 0, 0, tiled=True)
+def from_other(value, axis):
+    return lax.ppermute(value, axis, [(0, 1), (1, 0)])
+
+
+def in_order(flip, pair):
+    mine, other = pair
+    return jnp.where(flip, other, mine), jnp.where(flip, mine, other)
 
 
 def shifted(value, steps):
@@ -53,7 +59,7 @@
     layer = lax.axis_index(LAYER)
     quarter = lax.axis_index(QUARTER)
     n_q = lax.axis_size(QUARTER)
-    n_g = lax.axis_size(GRP)
+    n_x, n_zl = lax.axis_size("x"), lax.axis_size("zl")
     rows = n_exc // n_q
 
     near = lax.all_gather(source, QUARTER)
@@ -63,9 +69,21 @@
     others = (jnp.arange(n_layers) != layer)[:, None, None]
     own = jnp.where(others, coupling[0], jnp.zeros_like(coupling[0]))
     own = jnp.concatenate([own.reshape(n_layers * rank, rank), left_basis], 0)
-    of_all = copies_to(own, QUARTER)
+    yl, core = lax.axis_index("yl"), lax.axis_index("core")
+    chips = jnp.stack([own, from_other(own, "yl")])
+    of_all = jnp.stack([chips, from_other(chips, "core")], 1)
+    of_all = of_all.reshape(n_q, n_layers * rank + rank, rank)
     couple = side_by_side(of_all[:, : n_layers * rank])
     left = of_all[:, n_layers * rank :]
+
+    def by_quarter(blocks):
+        upper = in_order(core == 1, (blocks[0], blocks[1]))
+        lower = in_order(core == 1, (blocks[2], blocks[3]))
+        first = in_order(yl == 1, (upper[0], lower[0]))
+        second = in_order(yl == 1, (upper[1], lower[1]))
+        return first[0], second[0], first[1], second[1]
+
+    left = jnp.stack(by_quarter(left))
     z_outer = z_cols.reshape(n_q, width, width)[:, 2 * FACE_Q :]
     far_to_y = jnp.einsum("qrt,qtc->qrc", left, z_outer, preferred_element_type=F32)
     far_to_y = far_to_y.reshape(n_q * rank, width).astype(BF16)
@@ -76,19 +94,26 @@
         outer_out = outgoing[:, 2 * FACE_Q :]
         partial = (dot(outer_out, right_basis) * kept).astype(BF16)
         parts = jnp.broadcast_to(
-            partial.reshape(n_q, 1, rows, rank), (n_q, n_g, rows, rank)
-        ).reshape(n_q * n_g, rows, rank)
-        arrived = lax.all_to_all(parts, QUARTER + GRP, 0, 0, tiled=True)
+            partial.reshape(n_q, 1, rows, rank), (n_q, n_x, rows, rank)
+        ).reshape(n_q * n_x, rows, rank)
+        arrived = lax.all_to_all(parts, FIRST, 0, 0, tiled=True)
+        coefs = arrived.astype(F32).sum(0).astype(BF16)
+        copies = jnp.broadcast_to(coefs, (n_layers * n_zl, rows, rank))
+        copies, outgoing = lax.optimization_barrier((copies, outgoing))
+        outer_out = outgoing[:, 2 * FACE_Q :]
+        of_layers = lax.all_to_all(copies, SECOND, 0, 0, tiled=True)
+        of_layers = of_layers.reshape(n_layers, n_zl, rows, rank)
+        of_layers = of_layers.astype(F32).sum(1).astype(BF16)
         below = shifted(outgoing[:, FACE_Q:], 4)
         above = shifted(jnp.concatenate([outgoing[:, :FACE_Q], outer_out], 1), -4)
-        coefs = arrived.astype(F32).sum(0).astype(BF16)
-        of_layers = copies_to(coefs, LAYER)
         lower_in = dot(below[:, :FACE_Q], reorder)
         lower_above = above[:, :FACE_Q].astype(F32)
         outer_in = dot(outer_out, tiles[0]) + dot(below[:, FACE_Q:], tiles[1])
         outer_in = outer_in + dot(above[:, FACE_Q:], tiles[2])
         near = jnp.concatenate([lower_in, lower_above, outer_in], 1) + source.astype(F32)
-        far = dot(side_by_side(of_layers), couple).astype(BF16)
+        far = dot(of_layers.transpose(1, 0, 2).reshape(rows, -1), couple)
+        far = [far[:, k * rank : (k + 1) * rank] for k in range(n_q)]
+        far = jnp.concatenate(by_quarter(far), 1).astype(BF16)
         if sweep < ITERS - 1:
             both = jnp.concatenate([near.astype(BF16), far], 0)
             both = lax.all_gather(both, QUARTER)

time: 231 us -> 194 us (0.84)
  waiting for transfers between devices: 85.4 us -> 49.3 us
  starting transfers between devices: 78.6 us -> 66.9 us
  blocking collectives: 44.2 us -> 54.5 us
  other arithmetic: 3.93 us -> 7.74 us
  local copies, waits for them, and re-layouts: 9.47 us -> 7.03 us
    all_to_all x7 -> x5, waiting for transfers between devices: 80.8 us -> 27.8 us  [the longest x3 16 us: per_device(): of_layers = lax.all_to_all(copies, SECOND, 0, 0, tiled=True)]
    all_to_all x7 -> x5, starting transfers between devices: 62.5 us -> 43 us  [the longest x3 36.1 us: per_device(): of_layers = lax.all_to_all(copies, SECOND, 0, 0, tiled=True)]
    ppermute x6, waiting for transfers between devices: 4.62 us -> 21.6 us  [shifted(): lax.ppermute(value, SUB, [(s, s + steps) for s in range(first, last)])]
    all_to_all x0 -> x1, blocking collectives: none -> 9.09 us  [per_device(): arrived = lax.all_to_all(parts, FIRST, 0, 0, tiled=True)]
    ppermute x0 -> x2, starting transfers between devices: none -> 7.23 us  [from_other(): return lax.ppermute(value, axis, [(0, 1), (1, 0)])]
    all_gather x1, blocking collectives: 16.8 us -> 20.7 us  [per_device(): near = lax.all_gather(source, QUARTER)]
    another operation x0 -> x5, other arithmetic: none -> 3.52 us  [the longest x2 2.65 us: per_device(): of_all = jnp.stack([chips, from_other(chips, 'core')], 1)]
    all_gather x2, blocking collectives: 20.4 us -> 17.3 us  [per_device(): both = lax.all_gather(both, QUARTER)]
  transfers between devices with their start and end apart: 13 -> 13, of which waited for: 8 -> 9; matrix products, arithmetic and copies ran while one was open for 3% -> 5% of each run, Pallas kernels for 0% -> 0%
where the time goes in v2:
time: 194 us; the launch traced here: 193 us
  starting transfers between devices  66.9 us (34%)
  blocking collectives  54.5 us (28%)
  waiting for transfers between devices  49.3 us (25%)
  other arithmetic  7.74 us (4%)
  matrix products  7.47 us (4%)
  local copies, waits for them, and re-layouts  7.03 us (4%)
    all_to_all x3, starting transfers between devices, per_device(): of_layers = lax.all_to_all(copies, SECOND, 0, 0, tiled=True)  36.1 us
    ppermute x6, waiting for transfers between devices, shifted(): lax.ppermute(value, SUB, [(s, s + steps) for s in range(first, last)])  21.6 us
    all_gather x1, blocking collectives, per_device(): near = lax.all_gather(source, QUARTER)  20.7 us
    all_gather x2, blocking collectives, per_device(): both = lax.all_gather(both, QUARTER)  17.3 us
    ppermute x6, starting transfers between devices, shifted(): lax.ppermute(value, SUB, [(s, s + steps) for s in range(first, last)])  16.6 us
    all_to_all x3, waiting for transfers between devices, per_device(): of_layers = lax.all_to_all(copies, SECOND, 0, 0, tiled=True)  16 us
    all_to_all x2, waiting for transfers between devices, per_device(): arrived = lax.all_to_all(parts, FIRST, 0, 0, tiled=True)  11.8 us
    all_to_all x1, blocking collectives, per_device(): arrived = lax.all_to_all(parts, FIRST, 0, 0, tiled=True)  9.09 us
  transfers between devices with their start and end apart: 13, of which 9 were waited for; matrix products, arithmetic and copies ran while one was open for 5% of the time, Pallas kernels for 0%

profile of v2, /device:TPU:1, one launch (start us, length us, event | category | flops | bytes accessed | tf_op | source)
XLA Modules:
  0.0 193.4 jit_solution(8067601846642193820)
XLA Ops:
  0.1 1.4 bitcast_select_fusion
  1.5 0.8 fusion.124
  2.3 4.0 %collective-permute-start.2 = (bf16[2176,128]{1,0:T(8,128)(2,1)S(1)}, bf16[2176,128]{1,0:T(8,128)(2,1)S(1)}, u32[]{:S(2)}, u32[]{:S(2)}) collective-permute-start(bf16[2176,128]{1,0:T(8,128)(2,1)S(1)} %get-tuple-element.28), channel_id=1, source_target_pairs={{0,24},{24,0},{1,25},{25,1},{2,26},{26,2},{3,27},{27,3},{4,28},{28... | collective-permute-start | bytes 1671176 | tf_op jit(solution)/shard_map/ppermute | solution.py:27
  6.4 20.7 %all-gather = bf16[4,1,96,512]{3,2,1,0:T(8,128)(2,1)S(1)} all-gather(bf16[1,1,96,512]{3,2,1,0:T(8,128)(2,1)S(1)} %copy-done.1), channel_id=2, replica_groups=mesh['zh'=4,'yh'=4,'yl'=2,'core'=2,'zl'=3,'x'=4] {'yl','core'}, dimensions={0}, use_global_device_ids=true | all-gather | bytes 491520 | tf_op jit(solution)/shard_map/all_gather | solution.py:65
  27.1 0.6 dynamic_slice.6
  27.7 0.6 fusion.114
  28.4 2.1 %fusion.18 = bf16[96,512]{1,0:T(8,128)(2,1)S(1)} fusion(bf16[1,1,2048,512]{3,2,1,0:T(8,128)(2,1)} %param.9, bf16[96,512]{1,0:T(8,128)(2,1)S(1)} %get-tuple-element.40, bf16[96,512]{1,0:T(8,128)(2,1)S(1)} %get-tuple-element.38, bf16[96,512]{1,0:T(8,128)(2,1)S(1)} %get-tuple-element.39, bf16[96,512]{1,0:T(8,128)(2,1)S(1)} %get-tuple-element.37), kind=kOutput, calls=%fused_computation.13 | convolution fusion | flops 202948608 | bytes 2588672 | tf_op jit(solution)/shard_map/dot_general | solution.py:19
  30.6 0.7 broadcast_in_dim.58
  31.3 3.5 %all-to-all-start = ((bf16[16,24,128]{2,1,0:T(8,128)(2,1)}), bf16[16,24,128]{2,1,0:T(8,128)(2,1)S(1)}, u32[]{:S(2)}, u32[]{:S(2)}) async-start(bf16[16,24,128]{2,1,0:T(8,128)(2,1)} %bitcast.9), calls=%async_computation | async-start | bytes 196608 | tf_op jit(solution)/shard_map/all_to_all | solution.py:99
  34.8 5.9 %all-to-all-done = bf16[16,24,128]{2,1,0:T(8,128)(2,1)S(1)} async-done(((bf16[16,24,128]{2,1,0:T(8,128)(2,1)}), bf16[16,24,128]{2,1,0:T(8,128)(2,1)S(1)}, u32[]{:S(2)}, u32[]{:S(2)}) %all-to-all-start) | async-done | bytes 98336 | tf_op jit(solution)/shard_map/all_to_all | solution.py:99
  40.7 0.8 broadcast_in_dim.59
  41.4 0.7 slice.227
  42.2 17.8 %all-to-all-start.1 = ((bf16[48,24,128]{2,1,0:T(8,128)(2,1)}), bf16[48,24,128]{2,1,0:T(8,128)(2,1)S(1)}, u32[]{:S(2)}, u32[]{:S(2)}) async-start(bf16[48,24,128]{2,1,0:T(8,128)(2,1)} %broadcast_in_dim.59), calls=%async_computation.1 | async-start | bytes 589824 | tf_op jit(solution)/shard_map/all_to_all | solution.py:104
  60.1 1.3 collective-permute-start.1
  61.4 4.9 %collective-permute-start = (bf16[96,320]{1,0:T(8,128)(2,1)}, bf16[96,320]{1,0:T(8,128)(2,1)S(1)}, u32[]{:S(2)}, u32[]{:S(2)}) collective-permute-start(bf16[96,320]{1,0:T(8,128)(2,1)} %slice.227), channel_id=1, source_target_pairs={{0,48},{12,60},{24,72},{36,84},{48,96},{60,108},{72,120},{84,132},... | collective-permute-start | bytes 184328 | tf_op jit(solution)/shard_map/ppermute | solution.py:38
  66.4 0.8 copy-done.3
  67.3 1.2 fusion.125
  68.5 3.2 %collective-permute-start.3 = (bf16[2,2176,128]{2,1,0:T(8,128)(2,1)S(1)}, bf16[2,2176,128]{2,1,0:T(8,128)(2,1)}, u32[]{:S(2)}, u32[]{:S(2)}) collective-permute-start(bf16[2,2176,128]{2,1,0:T(8,128)(2,1)S(1)} %get-tuple-element.26), channel_id=1, source_target_pairs={{0,12},{12,0},{1,13},{13,1},{2,14},{14,2},{3,15},{15,3},{4,16},{16... | collective-permute-start | bytes 3342344 | tf_op jit(solution)/shard_map/ppermute | solution.py:27
  72.4 8.3 %all-to-all-done.1 = bf16[48,24,128]{2,1,0:T(8,128)(2,1)S(1)} async-done(((bf16[48,24,128]{2,1,0:T(8,128)(2,1)}), bf16[48,24,128]{2,1,0:T(8,128)(2,1)S(1)}, u32[]{:S(2)}, u32[]{:S(2)}) %all-to-all-start.1) | async-done | bytes 294944 | tf_op jit(solution)/shard_map/all_to_all | solution.py:104
  80.7 0.7 reduce_sum.73
  81.4 1.5 pad_maximum_fusion
  83.0 0.7 copy-done.7
  83.7 0.4 fusion.66
  84.1 8.6 %all-gather.1 = bf16[480,512]{1,0:T(8,128)(2,1)S(1)} all-gather(bf16[120,512]{1,0:T(8,128)(2,1)S(1)} %maximum_maximum_fusion), channel_id=3, replica_groups=mesh['zh'=4,'yh'=4,'yl'=2,'core'=2,'zl'=3,'x'=4] {'yl','core'}, dimensions={0}, use_global_device_ids=true | all-gather | bytes 614400 | tf_op jit(solution)/shard_map/all_gather | solution.py:119
  93.3 0.5 fusion.15
  94.0 9.1 %all_to_all.30 = bf16[16,24,128]{2,1,0:T(8,128)(2,1)S(1)} all-to-all(bf16[16,24,128]{2,1,0:T(8,128)(2,1)S(1)} %bitcast.172), channel_id=1, replica_groups=mesh['zh'=4,'yh'=4,'yl'=2,'core'=2,'zl'=3,'x'=4] {'yl','core','x'}, dimensions={0} | all-to-all | bytes 196608 | tf_op jit(solution)/shard_map/all_to_all | solution.py:99
  103.1 0.8 broadcast_in_dim.66
  104.1 8.9 %all-to-all-start.3 = ((bf16[48,24,128]{2,1,0:T(8,128)(2,1)}), bf16[48,24,128]{2,1,0:T(8,128)(2,1)S(1)}, u32[]{:S(2)}, u32[]{:S(2)}) async-start(bf16[48,24,128]{2,1,0:T(8,128)(2,1)} %broadcast_in_dim.66), calls=%async_computation.3 | async-start | bytes 589824 | tf_op jit(solution)/shard_map/all_to_all | solution.py:104
  113.0 3.9 %collective-permute-start.4 = (bf16[96,320]{1,0:T(8,128)(2,1)S(1)}, bf16[96,320]{1,0:T(8,128)(2,1)S(1)}, u32[]{:S(2)}, u32[]{:S(2)}) collective-permute-start(bf16[96,320]{1,0:T(8,128)(2,1)S(1)} %slice.256), channel_id=1, source_target_pairs={{0,48},{12,60},{24,72},{36,84},{48,96},{60,108},{72,120},{84,132},... | collective-permute-start | bytes 184328 | tf_op jit(solution)/shard_map/ppermute | solution.py:38
  117.1 1.3 collective-permute-start.5
  118.8 10.6 %collective-permute-done.5 = bf16[96,320]{1,0:T(8,128)(2,1)S(1)} collective-permute-done((bf16[96,320]{1,0:T(8,128)(2,1)S(1)}, bf16[96,320]{1,0:T(8,128)(2,1)S(1)}, u32[]{:S(2)}, u32[]{:S(2)}) %collective-permute-start.5) | collective-permute-done | bytes 61472 | tf_op jit(solution)/shard_map/ppermute | solution.py:38
  129.9 3.8 %all-to-all-done.3 = bf16[48,24,128]{2,1,0:T(8,128)(2,1)S(1)} async-done(((bf16[48,24,128]{2,1,0:T(8,128)(2,1)}), bf16[48,24,128]{2,1,0:T(8,128)(2,1)S(1)}, u32[]{:S(2)}, u32[]{:S(2)}) %all-to-all-start.3) | async-done | bytes 294944 | tf_op jit(solution)/shard_map/all_to_all | solution.py:104
  133.7 0.4 fusion.63
  134.2 8.6 %all-gather.2 = bf16[480,512]{1,0:T(8,128)(2,1)S(1)} all-gather(bf16[120,512]{1,0:T(8,128)(2,1)S(1)} %maximum_maximum_fusion.1), channel_id=4, replica_groups=mesh['zh'=4,'yh'=4,'yl'=2,'core'=2,'zl'=3,'x'=4] {'yl','core'}, dimensions={0}, use_global_device_ids=true | all-gather | bytes 614400 | tf_op jit(solution)/shard_map/all_gather | solution.py:119
  143.1 0.5 fusion.12
  143.7 0.7 broadcast_in_dim.68
  144.4 3.5 %all-to-all-start.4 = ((bf16[16,24,128]{2,1,0:T(8,128)(2,1)}), bf16[16,24,128]{2,1,0:T(8,128)(2,1)S(1)}, u32[]{:S(2)}, u32[]{:S(2)}) async-start(bf16[16,24,128]{2,1,0:T(8,128)(2,1)} %bitcast.49), calls=%async_computation.4 | async-start | bytes 196608 | tf_op jit(solution)/shard_map/all_to_all | solution.py:99
  147.8 5.9 %all-to-all-done.4 = bf16[16,24,128]{2,1,0:T(8,128)(2,1)S(1)} async-done(((bf16[16,24,128]{2,1,0:T(8,128)(2,1)}), bf16[16,24,128]{2,1,0:T(8,128)(2,1)S(1)}, u32[]{:S(2)}, u32[]{:S(2)}) %all-to-all-start.4) | async-done | bytes 98336 | tf_op jit(solution)/shard_map/all_to_all | solution.py:99
  153.7 0.8 broadcast_in_dim.69
  154.7 9.3 %all-to-all-start.5 = ((bf16[48,24,128]{2,1,0:T(8,128)(2,1)}), bf16[48,24,128]{2,1,0:T(8,128)(2,1)S(1)}, u32[]{:S(2)}, u32[]{:S(2)}) async-start(bf16[48,24,128]{2,1,0:T(8,128)(2,1)} %broadcast_in_dim.69), calls=%async_computation.5 | async-start | bytes 589824 | tf_op jit(solution)/shard_map/all_to_all | solution.py:104
  164.1 3.9 %collective-permute-start.6 = (bf16[96,320]{1,0:T(8,128)(2,1)S(1)}, bf16[96,320]{1,0:T(8,128)(2,1)S(1)}, u32[]{:S(2)}, u32[]{:S(2)}) collective-permute-start(bf16[96,320]{1,0:T(8,128)(2,1)S(1)} %slice.273), channel_id=1, source_target_pairs={{0,48},{12,60},{24,72},{36,84},{48,96},{60,108},{72,120},{84,132},... | collective-permute-start | bytes 184328 | tf_op jit(solution)/shard_map/ppermute | solution.py:38
  168.1 1.3 collective-permute-start.7
  169.4 0.3 collective-permute-done.6
  170.0 10.4 %collective-permute-done.7 = bf16[96,320]{1,0:T(8,128)(2,1)S(1)} collective-permute-done((bf16[96,320]{1,0:T(8,128)(2,1)S(1)}, bf16[96,320]{1,0:T(8,128)(2,1)S(1)}, u32[]{:S(2)}, u32[]{:S(2)}) %collective-permute-start.7) | collective-permute-done | bytes 61472 | tf_op jit(solution)/shard_map/ppermute | solution.py:38
  180.8 4.0 %all-to-all-done.5 = bf16[48,24,128]{2,1,0:T(8,128)(2,1)S(1)} async-done(((bf16[48,24,128]{2,1,0:T(8,128)(2,1)}), bf16[48,24,128]{2,1,0:T(8,128)(2,1)S(1)}, u32[]{:S(2)}, u32[]{:S(2)}) %all-to-all-start.5) | async-done | bytes 294944 | tf_op jit(solution)/shard_map/all_to_all | solution.py:104
  184.8 0.4 fusion.60
  185.2 7.4 %all_gather.24 = bf16[4,24,512]{2,1,0:T(8,128)(2,1)S(1)} all-gather(bf16[1,24,512]{2,1,0:T(8,128)(2,1)S(1)} %pad_maximum_fusion.8), channel_id=1, replica_groups=mesh['zh'=4,'yh'=4,'yl'=2,'core'=2,'zl'=3,'x'=4] {'yl','core'}, dimensions={0}, use_global_device_ids=true | all-gather | bytes 122880 | tf_op jit(solution)/shard_map/all_gather | solution.py:123
  192.8 0.7 pad_maximum_fusion.4
  (83 shorter events, 5.0 us)
Async XLA Ops:
  0.0 30.5 %copy-start = (bf16[1,1,128,128]{3,2,1,0:T(8,128)(2,1)S(1)}, bf16[1,1,128,128]{3,2,1,0:T(8,128)(2,1)}, u32[]{:S(2)}) copy-start(bf16[1,1,128,128]{3,2,1,0:T(8,128)(2,1)} %param.13) | copy-start | bytes 98308
  0.0 6.4 %copy-start.1 = (bf16[1,1,96,512]{3,2,1,0:T(8,128)(2,1)S(1)}, bf16[1,1,96,512]{3,2,1,0:T(8,128)(2,1)}, u32[]{:S(2)}) copy-start(bf16[1,1,96,512]{3,2,1,0:T(8,128)(2,1)} %param.10) | copy-start | bytes 294916
  0.0 27.1 %copy-start.9 = (s32[16]{0:T(128)S(1)}, s32[16]{0:T(128)}, u32[]{:S(2)}) copy-start(s32[16]{0:T(128)} %param.15) | copy-start | bytes 196
  0.0 27.7 %copy-start.10 = (f32[1,128]{1,0:T(1,128)S(1)}, f32[1,128]{1,0:T(1,128)}, u32[]{:S(2)}) copy-start(f32[1,128]{1,0:T(1,128)} %param.14) | copy-start | bytes 1540
  2.3 64.1 %collective-permute-start.2 = (bf16[2176,128]{1,0:T(8,128)(2,1)S(1)}, bf16[2176,128]{1,0:T(8,128)(2,1)S(1)}, u32[]{:S(2)}, u32[]{:S(2)}) collective-permute-start(bf16[2176,128]{1,0:T(8,128)(2,1)S(1)} %get-tuple-element.28), channel_id=1, source_target_pairs={{0,24},{24,0},{1,25},{25,1},{2,26},{26,2},{3,27},{27,3},{4,28},{28... | collective-permute-start | bytes 1671176 | tf_op jit(solution)/shard_map/ppermute | solution.py:27
  28.4 37.9 %copy-start.2 = (bf16[1,1,3,128,128]{4,3,2,1,0:T(8,128)(2,1)S(1)}, bf16[1,1,3,128,128]{4,3,2,1,0:T(8,128)(2,1)}, u32[]{:S(2)}) copy-start(bf16[1,1,3,128,128]{4,3,2,1,0:T(8,128)(2,1)} %param.12) | copy-start | bytes 294916
  31.3 9.4 %all-to-all-start = ((bf16[16,24,128]{2,1,0:T(8,128)(2,1)}), bf16[16,24,128]{2,1,0:T(8,128)(2,1)S(1)}, u32[]{:S(2)}, u32[]{:S(2)}) async-start(bf16[16,24,128]{2,1,0:T(8,128)(2,1)} %bitcast.9), calls=%async_computation | async-start | bytes 196608 | tf_op jit(solution)/shard_map/all_to_all | solution.py:99
  42.2 29.5 %copy-start.8 = (s32[1,1,192]{2,1,0:T(1,128)S(1)}, s32[1,1,192]{2,1,0:T(1,128)}, u32[]{:S(2)}) copy-start(s32[1,1,192]{2,1,0:T(1,128)} %param.11) | copy-start | bytes 2308
  42.2 38.5 %all-to-all-start.1 = ((bf16[48,24,128]{2,1,0:T(8,128)(2,1)}), bf16[48,24,128]{2,1,0:T(8,128)(2,1)S(1)}, u32[]{:S(2)}, u32[]{:S(2)}) async-start(bf16[48,24,128]{2,1,0:T(8,128)(2,1)} %broadcast_in_dim.59), calls=%async_computation.1 | async-start | bytes 589824 | tf_op jit(solution)/shard_map/all_to_all | solution.py:104
  60.1 11.7 %collective-permute-start.1 = (bf16[96,320]{1,0:T(8,128)(2,1)S(1)}, bf16[96,320]{1,0:T(8,128)(2,1)S(1)}, u32[]{:S(2)}, u32[]{:S(2)}) collective-permute-start(bf16[96,320]{1,0:T(8,128)(2,1)S(1)} %pad_maximum_fusion.5), channel_id=1, source_target_pairs={{48,0},{60,12},{72,24},{84,36},{96,48},{108,60},{120,72},{132,84},... | collective-permute-start | bytes 184328 | tf_op jit(solution)/shard_map/ppermute | solution.py:38
  61.4 10.3 %collective-permute-start = (bf16[96,320]{1,0:T(8,128)(2,1)}, bf16[96,320]{1,0:T(8,128)(2,1)S(1)}, u32[]{:S(2)}, u32[]{:S(2)}) collective-permute-start(bf16[96,320]{1,0:T(8,128)(2,1)} %slice.227), channel_id=1, source_target_pairs={{0,48},{12,60},{24,72},{36,84},{48,96},{60,108},{72,120},{84,132},... | collective-permute-start | bytes 184328 | tf_op jit(solution)/shard_map/ppermute | solution.py:38
  66.4 0.8 copy-start.3
  68.5 12.9 %collective-permute-start.3 = (bf16[2,2176,128]{2,1,0:T(8,128)(2,1)S(1)}, bf16[2,2176,128]{2,1,0:T(8,128)(2,1)}, u32[]{:S(2)}, u32[]{:S(2)}) collective-permute-start(bf16[2,2176,128]{2,1,0:T(8,128)(2,1)S(1)} %get-tuple-element.26), channel_id=1, source_target_pairs={{0,12},{12,0},{1,13},{13,1},{2,14},{14,2},{3,15},{15,3},{4,16},{16... | collective-permute-start | bytes 3342344 | tf_op jit(solution)/shard_map/ppermute | solution.py:27
  82.8 0.9 copy-start.7
  83.7 9.1 %copy-start.4 = (bf16[1,1,2048,512]{3,2,1,0:T(8,128)(2,1)S(1)}, bf16[1,1,2048,512]{3,2,1,0:T(8,128)(2,1)}, u32[]{:S(2)}) copy-start(bf16[1,1,2048,512]{3,2,1,0:T(8,128)(2,1)} %param.9) | copy-start | bytes 6291460
  104.1 29.6 %all-to-all-start.3 = ((bf16[48,24,128]{2,1,0:T(8,128)(2,1)}), bf16[48,24,128]{2,1,0:T(8,128)(2,1)S(1)}, u32[]{:S(2)}, u32[]{:S(2)}) async-start(bf16[48,24,128]{2,1,0:T(8,128)(2,1)} %broadcast_in_dim.66), calls=%async_computation.3 | async-start | bytes 589824 | tf_op jit(solution)/shard_map/all_to_all | solution.py:104
  113.0 5.6 %collective-permute-start.4 = (bf16[96,320]{1,0:T(8,128)(2,1)S(1)}, bf16[96,320]{1,0:T(8,128)(2,1)S(1)}, u32[]{:S(2)}, u32[]{:S(2)}) collective-permute-start(bf16[96,320]{1,0:T(8,128)(2,1)S(1)} %slice.256), channel_id=1, source_target_pairs={{0,48},{12,60},{24,72},{36,84},{48,96},{60,108},{72,120},{84,132},... | collective-permute-start | bytes 184328 | tf_op jit(solution)/shard_map/ppermute | solution.py:38
  117.1 12.3 %collective-permute-start.5 = (bf16[96,320]{1,0:T(8,128)(2,1)S(1)}, bf16[96,320]{1,0:T(8,128)(2,1)S(1)}, u32[]{:S(2)}, u32[]{:S(2)}) collective-permute-start(bf16[96,320]{1,0:T(8,128)(2,1)S(1)} %pad_maximum_fusion.6), channel_id=1, source_target_pairs={{48,0},{60,12},{72,24},{84,36},{96,48},{108,60},{120,72},{132,84},... | collective-permute-start | bytes 184328 | tf_op jit(solution)/shard_map/ppermute | solution.py:38
  134.1 9.0 %copy-start.5 = (bf16[1,1,2048,512]{3,2,1,0:T(8,128)(2,1)S(1)}, bf16[1,1,2048,512]{3,2,1,0:T(8,128)(2,1)}, u32[]{:S(2)}) copy-start(bf16[1,1,2048,512]{3,2,1,0:T(8,128)(2,1)} %param.9) | copy-start | bytes 6291460
  144.4 9.4 %all-to-all-start.4 = ((bf16[16,24,128]{2,1,0:T(8,128)(2,1)}), bf16[16,24,128]{2,1,0:T(8,128)(2,1)S(1)}, u32[]{:S(2)}, u32[]{:S(2)}) async-start(bf16[16,24,128]{2,1,0:T(8,128)(2,1)} %bitcast.49), calls=%async_computation.4 | async-start | bytes 196608 | tf_op jit(solution)/shard_map/all_to_all | solution.py:99
  154.7 30.0 %all-to-all-start.5 = ((bf16[48,24,128]{2,1,0:T(8,128)(2,1)}), bf16[48,24,128]{2,1,0:T(8,128)(2,1)S(1)}, u32[]{:S(2)}, u32[]{:S(2)}) async-start(bf16[48,24,128]{2,1,0:T(8,128)(2,1)} %broadcast_in_dim.69), calls=%async_computation.5 | async-start | bytes 589824 | tf_op jit(solution)/shard_map/all_to_all | solution.py:104
  164.1 5.6 %collective-permute-start.6 = (bf16[96,320]{1,0:T(8,128)(2,1)S(1)}, bf16[96,320]{1,0:T(8,128)(2,1)S(1)}, u32[]{:S(2)}, u32[]{:S(2)}) collective-permute-start(bf16[96,320]{1,0:T(8,128)(2,1)S(1)} %slice.273), channel_id=1, source_target_pairs={{0,48},{12,60},{24,72},{36,84},{48,96},{60,108},{72,120},{84,132},... | collective-permute-start | bytes 184328 | tf_op jit(solution)/shard_map/ppermute | solution.py:38
  168.1 12.3 %collective-permute-start.7 = (bf16[96,320]{1,0:T(8,128)(2,1)S(1)}, bf16[96,320]{1,0:T(8,128)(2,1)S(1)}, u32[]{:S(2)}, u32[]{:S(2)}) collective-permute-start(bf16[96,320]{1,0:T(8,128)(2,1)S(1)} %pad_maximum_fusion.7), channel_id=1, source_target_pairs={{48,0},{60,12},{72,24},{84,36},{96,48},{108,60},{120,72},{132,84},... | collective-permute-start | bytes 184328 | tf_op jit(solution)/shard_map/ppermute | solution.py:38
  184.8 7.9 %copy-start.6 = (bf16[1,1,128,128]{3,2,1,0:T(8,128)(2,1)S(1)}, bf16[1,1,128,128]{3,2,1,0:T(8,128)(2,1)}, u32[]{:S(2)}) copy-start(bf16[1,1,128,128]{3,2,1,0:T(8,128)(2,1)} %param.17) | copy-start | bytes 98308

commit v3 on v1

--- a/solution.py
+++ b/solution.py
@@ -21,15 +21,23 @@
     return jnp.concatenate([pieces[i] for i in range(pieces.shape[0])], axis=-1)
 
 
-def copies_to(value, axes):
-    copies = jnp.broadcast_to(value, (lax.axis_size(axes), *value.shape))
-    return lax.all_to_all(copies, axes, 0, 0, tiled=True)
+def from_other(value, axis):
+    return lax.ppermute(value, axis, [(0, 1), (1, 0)])
 
 
-def shifted(value, steps):
-    count = lax.axis_size(SUB)
-    first, last = max(0, -steps), min(count, count - steps)
-    return lax.ppermute(value, SUB, [(s, s + steps) for s in range(first, last)])
+def in_order(flip, pair):
+    mine, other = pair
+    return jnp.where(flip, other, mine), jnp.where(flip, mine, other)
+
+
+def with_neighbours(value, first):
+    n_q = lax.axis_size(QUARTER)
+    pairs = []
+    for lower in range(first, lax.axis_size(LAYER) - 1, 2):
+        for q in range(n_q):
+            here, there = lower * n_q + q, (lower + 1) * n_q + q
+            pairs += [(here, there), (there, here)]
+    return lax.ppermute(value, SUB, pairs)
 
 
 def per_device(
@@ -56,20 +64,31 @@
     n_g = lax.axis_size(GRP)
     rows = n_exc // n_q
 
-    near = lax.all_gather(source, QUARTER)
-    y_now = dot(side_by_side(near), z_cols)
+    yl, core = lax.axis_index("yl"), lax.axis_index("core")
+    even = layer % 2 == 0
+
+    flat = side_by_side(left_basis.reshape(-1, rank * rank // width, rank))
+    both = lax.all_gather(jnp.concatenate([source, flat], 0), QUARTER)
+    own, both = lax.optimization_barrier((coupling[0], both))
+    own = own.reshape(n_layers * rank, rank)
+    other = from_other(own, "yl")
+    y_now = dot(side_by_side(both[:, :n_exc]), z_cols)
+    left = both[:, n_exc:].reshape(n_q, -1, width // rank, rank)
+    left = left.transpose(0, 2, 1, 3).reshape(n_q, rank, rank)
 
     kept = jnp.where(jnp.arange(rank) < rank_counts[layer], rank_scale[0], F32(0.0))
     others = (jnp.arange(n_layers) != layer)[:, None, None]
-    own = jnp.where(others, coupling[0], jnp.zeros_like(coupling[0]))
-    own = jnp.concatenate([own.reshape(n_layers * rank, rank), left_basis], 0)
-    of_all = copies_to(own, QUARTER)
-    couple = side_by_side(of_all[:, : n_layers * rank])
-    left = of_all[:, n_layers * rank :]
     z_outer = z_cols.reshape(n_q, width, width)[:, 2 * FACE_Q :]
     far_to_y = jnp.einsum("qrt,qtc->qrc", left, z_outer, preferred_element_type=F32)
     far_to_y = far_to_y.reshape(n_q * rank, width).astype(BF16)
     reorder = jax.nn.one_hot(face_order[0, 0], FACE_Q, axis=0, dtype=BF16)
+
+    def by_quarter(blocks):
+        upper = in_order(core == 1, (blocks[0], blocks[1]))
+        lower = in_order(core == 1, (blocks[2], blocks[3]))
+        first = in_order(yl == 1, (upper[0], lower[0]))
+        second = in_order(yl == 1, (upper[1], lower[1]))
+        return first[0], second[0], first[1], second[1]
 
     for sweep in range(ITERS):
         outgoing = y_now.astype(BF16)
@@ -78,19 +97,34 @@
         parts = jnp.broadcast_to(
             partial.reshape(n_q, 1, rows, rank), (n_q, n_g, rows, rank)
         ).reshape(n_q * n_g, rows, rank)
+        up = outgoing[:, FACE_Q:]
+        down = jnp.concatenate([outgoing[:, :FACE_Q], outer_out], 1)
         arrived = lax.all_to_all(parts, QUARTER + GRP, 0, 0, tiled=True)
-        below = shifted(outgoing[:, FACE_Q:], 4)
-        above = shifted(jnp.concatenate([outgoing[:, :FACE_Q], outer_out], 1), -4)
         coefs = arrived.astype(F32).sum(0).astype(BF16)
-        of_layers = copies_to(coefs, LAYER)
+        if sweep == 0:
+            other, coefs = lax.optimization_barrier((other, coefs))
+            chips = jnp.stack([own, other])
+            of_all = jnp.stack([chips, from_other(chips, "core")], 1)
+            couple = side_by_side(of_all.reshape(n_q, n_layers * rank, rank))
+        one = with_neighbours(jnp.where(even, up, down), 0)
+        two = with_neighbours(jnp.where(even, down, up), 1)
+        below, above = jnp.where(even, two, one), jnp.where(even, one, two)
         lower_in = dot(below[:, :FACE_Q], reorder)
         lower_above = above[:, :FACE_Q].astype(F32)
         outer_in = dot(outer_out, tiles[0]) + dot(below[:, FACE_Q:], tiles[1])
         outer_in = outer_in + dot(above[:, FACE_Q:], tiles[2])
         near = jnp.concatenate([lower_in, lower_above, outer_in], 1) + source.astype(F32)
-        far = dot(side_by_side(of_layers), couple).astype(BF16)
         if sweep < ITERS - 1:
-            both = jnp.concatenate([near.astype(BF16), far], 0)
+            near = near.astype(BF16)
+        copies = jnp.broadcast_to(coefs, (n_layers, rows, rank))
+        copies, near = lax.optimization_barrier((copies, near))
+        of_layers = lax.all_to_all(copies, LAYER, 0, 0, tiled=True)
+        of_layers = jnp.where(others, of_layers, jnp.zeros_like(of_layers))
+        far = dot(of_layers.transpose(1, 0, 2).reshape(rows, -1), couple)
+        far = [far[:, k * rank : (k + 1) * rank] for k in range(n_q)]
+        far = jnp.concatenate(by_quarter(far), 1).astype(BF16)
+        if sweep < ITERS - 1:
+            both = jnp.concatenate([near, far], 0)
             both = lax.all_gather(both, QUARTER)
             far = both[:, n_exc:].reshape(n_exc, width)
             y_now = dot(side_by_side(both[:, :n_exc]), z_cols) + dot(far, far_to_y)

time: 231 us -> 201 us (0.87)
  waiting for transfers between devices: 85.4 us -> 46.4 us
  blocking collectives: 44.2 us -> 66.1 us
  starting transfers between devices: 78.6 us -> 64.9 us
  local copies, waits for them, and re-layouts: 9.47 us -> 6.74 us
  other arithmetic: 3.93 us -> 6.48 us
    all_to_all x4 -> x2, waiting for transfers between devices: 64.9 us -> 25.9 us  [per_device(): of_layers = lax.all_to_all(copies, LAYER, 0, 0, tiled=True)]
    all_to_all x0 -> x1, blocking collectives: none -> 25.4 us  [per_device(): of_layers = lax.all_to_all(copies, LAYER, 0, 0, tiled=True)]
    all_to_all x4 -> x2, starting transfers between devices: 46.2 us -> 35.2 us  [per_device(): of_layers = lax.all_to_all(copies, LAYER, 0, 0, tiled=True)]
    all_gather x2, blocking collectives: 20.4 us -> 16.8 us  [per_device(): both = lax.all_gather(both, QUARTER)]
    ppermute x6 -> x8, waiting for transfers between devices: 4.62 us -> 1.54 us  [the longest x6 1.53 us: with_neighbours(): return lax.ppermute(value, SUB, pairs)]
    all_to_all x3, waiting for transfers between devices: 15.9 us -> 18.9 us  [per_device(): arrived = lax.all_to_all(parts, QUARTER + GRP, 0, 0, tiled=True)]
    another operation x0 -> x4, other arithmetic: none -> 2.63 us  [the longest x2 2.6 us: per_device(): of_all = jnp.stack([chips, from_other(chips, 'core')], 1)]
    broadcast_in_dim x5 -> x3, local copies, waits for them, and re-layouts: 3.71 us -> 1.33 us  [per_device(): copies = jnp.broadcast_to(coefs, (n_layers, rows, rank))]
  transfers between devices with their start and end apart: 13 -> 13, of which waited for: 8 -> 6; matrix products, arithmetic and copies ran while one was open for 3% -> 7% of each run, Pallas kernels for 0% -> 0%
where the time goes in v3:
time: 201 us; the launch traced here: 200 us
  blocking collectives  66.1 us (33%)
  starting transfers between devices  64.9 us (32%)
  waiting for transfers between devices  46.4 us (23%)
  matrix products  9.19 us (5%)
  local copies, waits for them, and re-layouts  6.74 us (3%)
  other arithmetic  6.48 us (3%)
    all_to_all x2, starting transfers between devices, per_device(): of_layers = lax.all_to_all(copies, LAYER, 0, 0, tiled=True)  35.2 us
    all_to_all x2, waiting for transfers between devices, per_device(): of_layers = lax.all_to_all(copies, LAYER, 0, 0, tiled=True)  25.9 us
    all_to_all x1, blocking collectives, per_device(): of_layers = lax.all_to_all(copies, LAYER, 0, 0, tiled=True)  25.4 us
    all_to_all x3, waiting for transfers between devices, per_device(): arrived = lax.all_to_all(parts, QUARTER + GRP, 0, 0, tiled=True)  18.9 us
    all_gather x1, blocking collectives, per_device(): both = lax.all_gather(jnp.concatenate([source, flat], 0), QUARTER)  16.9 us
    all_gather x2, blocking collectives, per_device(): both = lax.all_gather(both, QUARTER)  16.8 us
    all_to_all x3, starting transfers between devices, per_device(): arrived = lax.all_to_all(parts, QUARTER + GRP, 0, 0, tiled=True)  15.7 us
    ppermute x6, starting transfers between devices, with_neighbours(): return lax.ppermute(value, SUB, pairs)  8.83 us
  transfers between devices with their start and end apart: 13, of which 6 were waited for; matrix products, arithmetic and copies ran while one was open for 7% of the time, Pallas kernels for 0%

profile of v3, /device:TPU:1, one launch (start us, length us, event | category | flops | bytes accessed | tf_op | source)
XLA Modules:
  0.0 200.3 jit_solution(4618098440958505410)
XLA Ops:
  0.0 0.8 slice_bitcast_fusion.20
  0.8 0.9 maximum_maximum_fusion
  1.7 16.9 %all-gather = bf16[512,512]{1,0:T(8,128)(2,1)S(1)} all-gather(bf16[128,512]{1,0:T(8,128)(2,1)S(1)} %maximum_maximum_fusion), channel_id=2, replica_groups=mesh['zh'=4,'yh'=4,'yl'=2,'core'=2,'zl'=3,'x'=4] {'yl','core'}, dimensions={0}, use_global_device_ids=true | all-gather | bytes 655360 | tf_op jit(solution)/shard_map/all_gather | solution.py:71
  18.5 2.8 %collective-permute-start = (bf16[2048,128]{1,0:T(8,128)(2,1)}, bf16[2048,128]{1,0:T(8,128)(2,1)S(1)}, u32[]{:S(2)}, u32[]{:S(2)}) collective-permute-start(bf16[2048,128]{1,0:T(8,128)(2,1)} %bitcast.180), channel_id=1, source_target_pairs={{0,24},{24,0},{1,25},{25,1},{2,26},{26,2},{3,27},{27,3},{4,28},{28... | collective-permute-start | bytes 1572872 | tf_op jit(solution)/shard_map/ppermute | solution.py:25
  21.4 1.2 dynamic_slice.6
  22.6 1.3 fusion.105
  23.9 2.0 %fusion.18 = bf16[96,512]{1,0:T(8,128)(2,1)S(1)} fusion(bf16[1,1,2048,512]{3,2,1,0:T(8,128)(2,1)} %param.9, bf16[96,512]{1,0:T(8,128)(2,1)S(1)} %get-tuple-element.32, bf16[96,512]{1,0:T(8,128)(2,1)S(1)} %get-tuple-element.33, bf16[96,512]{1,0:T(8,128)(2,1)S(1)} %get-tuple-element.34, bf16[96,512]{1,0:T(8,128)(2,1)S(1)} %get-tuple-element.31), kind=kOutput, calls=%fused_computation.13 | convolution fusion | flops 202948608 | bytes 2588672 | tf_op jit(solution)/shard_map/dot_general | solution.py:17
  26.2 0.8 broadcast_in_dim.57
  26.9 4.6 %all-to-all-start = ((bf16[48,24,128]{2,1,0:T(8,128)(2,1)}), bf16[48,24,128]{2,1,0:T(8,128)(2,1)S(1)}, u32[]{:S(2)}, u32[]{:S(2)}) async-start(bf16[48,24,128]{2,1,0:T(8,128)(2,1)} %bitcast.17), calls=%async_computation | async-start | bytes 589824 | tf_op jit(solution)/shard_map/all_to_all | solution.py:102
  31.7 1.9 collective-permute-start.2
  33.6 0.7 collective-permute-start.1
  34.3 1.3 convolution_convert_fusion
  35.7 0.8 fusion.80
  36.5 1.5 collective-permute-done.2
  38.0 2.7 %all-to-all-done = bf16[48,24,128]{2,1,0:T(8,128)(2,1)S(1)} async-done(((bf16[48,24,128]{2,1,0:T(8,128)(2,1)}), bf16[48,24,128]{2,1,0:T(8,128)(2,1)S(1)}, u32[]{:S(2)}, u32[]{:S(2)}) %all-to-all-start) | async-done | bytes 294944 | tf_op jit(solution)/shard_map/all_to_all | solution.py:102
  40.8 0.8 copy-done.4
  41.6 1.2 fusion.116
  42.8 2.3 %collective-permute-start.3 = (bf16[2,2048,128]{2,1,0:T(8,128)(2,1)S(1)}, bf16[2,2048,128]{2,1,0:T(8,128)(2,1)}, u32[]{:S(2)}, u32[]{:S(2)}) collective-permute-start(bf16[2,2048,128]{2,1,0:T(8,128)(2,1)S(1)} %get-tuple-element.30), channel_id=1, source_target_pairs={{0,12},{12,0},{1,13},{13,1},{2,14},{14,2},{3,15},{15,3},{4,16},{16... | collective-permute-start | bytes 3145736 | tf_op jit(solution)/shard_map/ppermute | solution.py:25
  45.3 0.2 convolution_add_fusion.6
  45.8 0.7 broadcast_in_dim.58
  46.5 22.9 %all-to-all-start.1 = ((bf16[16,24,128]{2,1,0:T(8,128)(2,1)}), bf16[16,24,128]{2,1,0:T(8,128)(2,1)S(1)}, u32[]{:S(2)}, u32[]{:S(2)}) async-start(bf16[16,24,128]{2,1,0:T(8,128)(2,1)} %broadcast_in_dim.58), calls=%async_computation.1 | async-start | bytes 196608 | tf_op jit(solution)/shard_map/all_to_all | solution.py:121
  69.4 1.4 pad_maximum_fusion
  71.0 12.2 %all-to-all-done.1 = bf16[16,24,128]{2,1,0:T(8,128)(2,1)S(1)} async-done(((bf16[16,24,128]{2,1,0:T(8,128)(2,1)}), bf16[16,24,128]{2,1,0:T(8,128)(2,1)S(1)}, u32[]{:S(2)}, u32[]{:S(2)}) %all-to-all-start.1) | async-done | bytes 98336 | tf_op jit(solution)/shard_map/all_to_all | solution.py:121
  83.2 0.4 fusion.59
  83.6 8.6 %all-gather.1 = bf16[480,512]{1,0:T(8,128)(2,1)S(1)} all-gather(bf16[120,512]{1,0:T(8,128)(2,1)S(1)} %maximum_maximum_fusion.1), channel_id=3, replica_groups=mesh['zh'=4,'yh'=4,'yl'=2,'core'=2,'zl'=3,'x'=4] {'yl','core'}, dimensions={0}, use_global_device_ids=true | all-gather | bytes 614400 | tf_op jit(solution)/shard_map/all_gather | solution.py:128
  92.2 0.2 fusion.117
  92.5 0.5 fusion.15
  93.2 2.4 %collective-permute-start.5 = (bf16[96,320]{1,0:T(8,128)(2,1)S(1)}, bf16[96,320]{1,0:T(8,128)(2,1)S(1)}, u32[]{:S(2)}, u32[]{:S(2)}) collective-permute-start(bf16[96,320]{1,0:T(8,128)(2,1)S(1)} %get-tuple-element.45), channel_id=1, source_target_pairs={{0,48},{48,0},{12,60},{60,12},{24,72},{72,24},{36,84},{84,36},{96,... | collective-permute-start | bytes 184328 | tf_op jit(solution)/shard_map/ppermute | solution.py:40
  95.6 0.7 collective-permute-start.4
  96.4 0.8 broadcast_in_dim.61
  97.2 5.4 %all-to-all-start.2 = ((bf16[48,24,128]{2,1,0:T(8,128)(2,1)}), bf16[48,24,128]{2,1,0:T(8,128)(2,1)S(1)}, u32[]{:S(2)}, u32[]{:S(2)}) async-start(bf16[48,24,128]{2,1,0:T(8,128)(2,1)} %bitcast.44), calls=%async_computation.2 | async-start | bytes 589824 | tf_op jit(solution)/shard_map/all_to_all | solution.py:102
  103.4 8.1 %all-to-all-done.2 = bf16[48,24,128]{2,1,0:T(8,128)(2,1)S(1)} async-done(((bf16[48,24,128]{2,1,0:T(8,128)(2,1)}), bf16[48,24,128]{2,1,0:T(8,128)(2,1)S(1)}, u32[]{:S(2)}, u32[]{:S(2)}) %all-to-all-start.2) | async-done | bytes 294944 | tf_op jit(solution)/shard_map/all_to_all | solution.py:102
  111.5 25.4 %all_to_all.30 = bf16[16,24,128]{2,1,0:T(8,128)(2,1)S(1)} all-to-all(bf16[16,24,128]{2,1,0:T(8,128)(2,1)S(1)} %broadcast_in_dim.62), channel_id=1, replica_groups=mesh['zh'=4,'yh'=4,'yl'=2,'core'=2,'zl'=3,'x'=4] {'zh','yh'}, dimensions={0} | all-to-all | bytes 196608 | tf_op jit(solution)/shard_map/all_to_all | solution.py:121
  136.9 0.4 fusion.56
  137.3 8.3 %all-gather.2 = bf16[480,512]{1,0:T(8,128)(2,1)S(1)} all-gather(bf16[120,512]{1,0:T(8,128)(2,1)S(1)} %maximum_maximum_fusion.2), channel_id=4, replica_groups=mesh['zh'=4,'yh'=4,'yl'=2,'core'=2,'zl'=3,'x'=4] {'yl','core'}, dimensions={0}, use_global_device_ids=true | all-gather | bytes 614400 | tf_op jit(solution)/shard_map/all_gather | solution.py:128
  145.7 0.2 fusion.118
  145.9 0.5 fusion.12
  146.6 2.5 %collective-permute-start.7 = (bf16[96,320]{1,0:T(8,128)(2,1)S(1)}, bf16[96,320]{1,0:T(8,128)(2,1)S(1)}, u32[]{:S(2)}, u32[]{:S(2)}) collective-permute-start(bf16[96,320]{1,0:T(8,128)(2,1)S(1)} %get-tuple-element.43), channel_id=1, source_target_pairs={{0,48},{48,0},{12,60},{60,12},{24,72},{72,24},{36,84},{84,36},{96,... | collective-permute-start | bytes 184328 | tf_op jit(solution)/shard_map/ppermute | solution.py:40
  149.2 0.7 collective-permute-start.6
  150.0 0.8 broadcast_in_dim.64
  150.7 5.7 %all-to-all-start.4 = ((bf16[48,24,128]{2,1,0:T(8,128)(2,1)}), bf16[48,24,128]{2,1,0:T(8,128)(2,1)S(1)}, u32[]{:S(2)}, u32[]{:S(2)}) async-start(bf16[48,24,128]{2,1,0:T(8,128)(2,1)} %bitcast.53), calls=%async_computation.4 | async-start | bytes 589824 | tf_op jit(solution)/shard_map/all_to_all | solution.py:102
  157.2 8.1 %all-to-all-done.4 = bf16[48,24,128]{2,1,0:T(8,128)(2,1)S(1)} async-done(((bf16[48,24,128]{2,1,0:T(8,128)(2,1)}), bf16[48,24,128]{2,1,0:T(8,128)(2,1)S(1)}, u32[]{:S(2)}, u32[]{:S(2)}) %all-to-all-start.4) | async-done | bytes 294944 | tf_op jit(solution)/shard_map/all_to_all | solution.py:102
  165.4 0.7 broadcast_in_dim.65
  166.0 12.3 %all-to-all-start.5 = ((bf16[16,24,128]{2,1,0:T(8,128)(2,1)}), bf16[16,24,128]{2,1,0:T(8,128)(2,1)S(1)}, u32[]{:S(2)}, u32[]{:S(2)}) async-start(bf16[16,24,128]{2,1,0:T(8,128)(2,1)} %broadcast_in_dim.65), calls=%async_computation.5 | async-start | bytes 196608 | tf_op jit(solution)/shard_map/all_to_all | solution.py:121
  178.3 13.7 %all-to-all-done.5 = bf16[16,24,128]{2,1,0:T(8,128)(2,1)S(1)} async-done(((bf16[16,24,128]{2,1,0:T(8,128)(2,1)}), bf16[16,24,128]{2,1,0:T(8,128)(2,1)S(1)}, u32[]{:S(2)}, u32[]{:S(2)}) %all-to-all-start.5) | async-done | bytes 98336 | tf_op jit(solution)/shard_map/all_to_all | solution.py:121
  192.1 0.4 fusion.53
  192.5 7.0 %all_gather.28 = bf16[4,24,512]{2,1,0:T(8,128)(2,1)S(1)} all-gather(bf16[1,24,512]{2,1,0:T(8,128)(2,1)S(1)} %pad_maximum_fusion.7), channel_id=1, replica_groups=mesh['zh'=4,'yh'=4,'yl'=2,'core'=2,'zl'=3,'x'=4] {'yl','core'}, dimensions={0}, use_global_device_ids=true | all-gather | bytes 122880 | tf_op jit(solution)/shard_map/all_gather | solution.py:132
  199.7 0.7 pad_maximum_fusion.3
  (77 shorter events, 3.6 us)
Async XLA Ops:
  0.0 26.0 %copy-start = (bf16[1,1,128,128]{3,2,1,0:T(8,128)(2,1)S(1)}, bf16[1,1,128,128]{3,2,1,0:T(8,128)(2,1)}, u32[]{:S(2)}) copy-start(bf16[1,1,128,128]{3,2,1,0:T(8,128)(2,1)} %param.13) | copy-start | bytes 98308
  18.5 22.3 %collective-permute-start = (bf16[2048,128]{1,0:T(8,128)(2,1)}, bf16[2048,128]{1,0:T(8,128)(2,1)S(1)}, u32[]{:S(2)}, u32[]{:S(2)}) collective-permute-start(bf16[2048,128]{1,0:T(8,128)(2,1)} %bitcast.180), channel_id=1, source_target_pairs={{0,24},{24,0},{1,25},{25,1},{2,26},{26,2},{3,27},{27,3},{4,28},{28... | collective-permute-start | bytes 1572872 | tf_op jit(solution)/shard_map/ppermute | solution.py:25
  26.0 9.7 %copy-start.2 = (bf16[1,1,3,128,128]{4,3,2,1,0:T(8,128)(2,1)S(1)}, bf16[1,1,3,128,128]{4,3,2,1,0:T(8,128)(2,1)}, u32[]{:S(2)}) copy-start(bf16[1,1,3,128,128]{4,3,2,1,0:T(8,128)(2,1)} %param.12) | copy-start | bytes 294916
  26.0 15.6 %copy-start.3 = (bf16[1,16,128,128]{3,2,1,0:T(8,128)(2,1)S(1)}, bf16[1,16,128,128]{3,2,1,0:T(8,128)(2,1)}, u32[]{:S(2)}) copy-start(bf16[1,16,128,128]{3,2,1,0:T(8,128)(2,1)} %param.16) | copy-start | bytes 1572868
  26.9 13.8 %all-to-all-start = ((bf16[48,24,128]{2,1,0:T(8,128)(2,1)}), bf16[48,24,128]{2,1,0:T(8,128)(2,1)S(1)}, u32[]{:S(2)}, u32[]{:S(2)}) async-start(bf16[48,24,128]{2,1,0:T(8,128)(2,1)} %bitcast.17), calls=%async_computation | async-start | bytes 589824 | tf_op jit(solution)/shard_map/all_to_all | solution.py:102
  31.7 6.3 %collective-permute-start.2 = (bf16[96,320]{1,0:T(8,128)(2,1)S(1)}, bf16[96,320]{1,0:T(8,128)(2,1)S(1)}, u32[]{:S(2)}, u32[]{:S(2)}) collective-permute-start(bf16[96,320]{1,0:T(8,128)(2,1)S(1)} %get-tuple-element.47), channel_id=1, source_target_pairs={{0,48},{48,0},{12,60},{60,12},{24,72},{72,24},{36,84},{84,36},{96,... | collective-permute-start | bytes 184328 | tf_op jit(solution)/shard_map/ppermute | solution.py:40
  33.6 4.4 %collective-permute-start.1 = (bf16[96,320]{1,0:T(8,128)(2,1)S(1)}, bf16[96,320]{1,0:T(8,128)(2,1)S(1)}, u32[]{:S(2)}, u32[]{:S(2)}) collective-permute-start(bf16[96,320]{1,0:T(8,128)(2,1)S(1)} %get-tuple-element.48), channel_id=1, source_target_pairs={{48,96},{96,48},{60,108},{108,60},{72,120},{120,72},{84,132},{132,... | collective-permute-start | bytes 184328 | tf_op jit(solution)/shard_map/ppermute | solution.py:40
  35.7 9.5 %copy-start.9 = (s32[1,1,192]{2,1,0:T(1,128)S(1)}, s32[1,1,192]{2,1,0:T(1,128)}, u32[]{:S(2)}) copy-start(s32[1,1,192]{2,1,0:T(1,128)} %param.11) | copy-start | bytes 2308
  38.0 7.7 %copy-start.1 = (bf16[1,1,96,512]{3,2,1,0:T(8,128)(2,1)S(1)}, bf16[1,1,96,512]{3,2,1,0:T(8,128)(2,1)}, u32[]{:S(2)}) copy-start(bf16[1,1,96,512]{3,2,1,0:T(8,128)(2,1)} %param.10) | copy-start | bytes 294916
  40.8 4.5 %copy-start.5 = (f32[96,128]{1,0:T(8,128)S(1)}, f32[96,128]{1,0:T(8,128)}, u32[]{:S(2)}) copy-start(f32[96,128]{1,0:T(8,128)} %fusion.80) | copy-start | bytes 147460
  40.8 0.8 copy-start.4
  42.8 26.6 %collective-permute-start.3 = (bf16[2,2048,128]{2,1,0:T(8,128)(2,1)S(1)}, bf16[2,2048,128]{2,1,0:T(8,128)(2,1)}, u32[]{:S(2)}, u32[]{:S(2)}) collective-permute-start(bf16[2,2048,128]{2,1,0:T(8,128)(2,1)S(1)} %get-tuple-element.30), channel_id=1, source_target_pairs={{0,12},{12,0},{1,13},{13,1},{2,14},{14,2},{3,15},{15,3},{4,16},{16... | collective-permute-start | bytes 3145736 | tf_op jit(solution)/shard_map/ppermute | solution.py:25
  46.5 36.7 %all-to-all-start.1 = ((bf16[16,24,128]{2,1,0:T(8,128)(2,1)}), bf16[16,24,128]{2,1,0:T(8,128)(2,1)S(1)}, u32[]{:S(2)}, u32[]{:S(2)}) async-start(bf16[16,24,128]{2,1,0:T(8,128)(2,1)} %broadcast_in_dim.58), calls=%async_computation.1 | async-start | bytes 196608 | tf_op jit(solution)/shard_map/all_to_all | solution.py:121
  83.6 8.9 %copy-start.6 = (bf16[1,1,2048,512]{3,2,1,0:T(8,128)(2,1)S(1)}, bf16[1,1,2048,512]{3,2,1,0:T(8,128)(2,1)}, u32[]{:S(2)}) copy-start(bf16[1,1,2048,512]{3,2,1,0:T(8,128)(2,1)} %param.9) | copy-start | bytes 6291460
  93.2 9.4 %collective-permute-start.5 = (bf16[96,320]{1,0:T(8,128)(2,1)S(1)}, bf16[96,320]{1,0:T(8,128)(2,1)S(1)}, u32[]{:S(2)}, u32[]{:S(2)}) collective-permute-start(bf16[96,320]{1,0:T(8,128)(2,1)S(1)} %get-tuple-element.45), channel_id=1, source_target_pairs={{0,48},{48,0},{12,60},{60,12},{24,72},{72,24},{36,84},{84,36},{96,... | collective-permute-start | bytes 184328 | tf_op jit(solution)/shard_map/ppermute | solution.py:40
  95.6 7.0 %collective-permute-start.4 = (bf16[96,320]{1,0:T(8,128)(2,1)S(1)}, bf16[96,320]{1,0:T(8,128)(2,1)S(1)}, u32[]{:S(2)}, u32[]{:S(2)}) collective-permute-start(bf16[96,320]{1,0:T(8,128)(2,1)S(1)} %get-tuple-element.46), channel_id=1, source_target_pairs={{48,96},{96,48},{60,108},{108,60},{72,120},{120,72},{84,132},{132,... | collective-permute-start | bytes 184328 | tf_op jit(solution)/shard_map/ppermute | solution.py:40
  97.2 14.3 %all-to-all-start.2 = ((bf16[48,24,128]{2,1,0:T(8,128)(2,1)}), bf16[48,24,128]{2,1,0:T(8,128)(2,1)S(1)}, u32[]{:S(2)}, u32[]{:S(2)}) async-start(bf16[48,24,128]{2,1,0:T(8,128)(2,1)} %bitcast.44), calls=%async_computation.2 | async-start | bytes 589824 | tf_op jit(solution)/shard_map/all_to_all | solution.py:102
  137.3 8.6 %copy-start.7 = (bf16[1,1,2048,512]{3,2,1,0:T(8,128)(2,1)S(1)}, bf16[1,1,2048,512]{3,2,1,0:T(8,128)(2,1)}, u32[]{:S(2)}) copy-start(bf16[1,1,2048,512]{3,2,1,0:T(8,128)(2,1)} %param.9) | copy-start | bytes 6291460
  146.6 9.8 %collective-permute-start.7 = (bf16[96,320]{1,0:T(8,128)(2,1)S(1)}, bf16[96,320]{1,0:T(8,128)(2,1)S(1)}, u32[]{:S(2)}, u32[]{:S(2)}) collective-permute-start(bf16[96,320]{1,0:T(8,128)(2,1)S(1)} %get-tuple-element.43), channel_id=1, source_target_pairs={{0,48},{48,0},{12,60},{60,12},{24,72},{72,24},{36,84},{84,36},{96,... | collective-permute-start | bytes 184328 | tf_op jit(solution)/shard_map/ppermute | solution.py:40
  149.2 7.3 %collective-permute-start.6 = (bf16[96,320]{1,0:T(8,128)(2,1)S(1)}, bf16[96,320]{1,0:T(8,128)(2,1)S(1)}, u32[]{:S(2)}, u32[]{:S(2)}) collective-permute-start(bf16[96,320]{1,0:T(8,128)(2,1)S(1)} %get-tuple-element.44), channel_id=1, source_target_pairs={{48,96},{96,48},{60,108},{108,60},{72,120},{120,72},{84,132},{132,... | collective-permute-start | bytes 184328 | tf_op jit(solution)/shard_map/ppermute | solution.py:40
  150.7 14.6 %all-to-all-start.4 = ((bf16[48,24,128]{2,1,0:T(8,128)(2,1)}), bf16[48,24,128]{2,1,0:T(8,128)(2,1)S(1)}, u32[]{:S(2)}, u32[]{:S(2)}) async-start(bf16[48,24,128]{2,1,0:T(8,128)(2,1)} %bitcast.53), calls=%async_computation.4 | async-start | bytes 589824 | tf_op jit(solution)/shard_map/all_to_all | solution.py:102
  166.0 26.1 %all-to-all-start.5 = ((bf16[16,24,128]{2,1,0:T(8,128)(2,1)}), bf16[16,24,128]{2,1,0:T(8,128)(2,1)S(1)}, u32[]{:S(2)}, u32[]{:S(2)}) async-start(bf16[16,24,128]{2,1,0:T(8,128)(2,1)} %broadcast_in_dim.65), calls=%async_computation.5 | async-start | bytes 196608 | tf_op jit(solution)/shard_map/all_to_all | solution.py:121
  178.3 21.2 %copy-start.8 = (bf16[1,1,128,128]{3,2,1,0:T(8,128)(2,1)S(1)}, bf16[1,1,128,128]{3,2,1,0:T(8,128)(2,1)}, u32[]{:S(2)}) copy-start(bf16[1,1,128,128]{3,2,1,0:T(8,128)(2,1)} %param.17) | copy-start | bytes 98308

commit v4 on v3

v4 whole, which is shorter than its diff:
```python
import jax
import jax.numpy as jnp
from jax import lax
from jax.sharding import Mesh, PartitionSpec as P

FACE_Q = 192
ITERS = 3
F32, BF16 = jnp.float32, jnp.bfloat16

LAYER = ("zh", "yh")
QUARTER = ("yl", "core")
SUB = LAYER + QUARTER
GRP = ("zl", "x")


def dot(a, b):
    return jnp.dot(a, b, preferred_element_type=F32)


def side_by_side(pieces):
    return jnp.concatenate([pieces[i] for i in range(pieces.shape[0])], axis=-1)


def from_other(value, axis):
    return lax.ppermute(value, axis, [(0, 1), (1, 0)])


def in_order(flip, pair):
    mine, other = pair
    return jnp.where(flip, other, mine), jnp.where(flip, mine, other)


def to_neighbours(value):
    count, step = lax.axis_size(SUB), lax.axis_size(QUARTER)
    pairs = [(s, s + step) for s in range(0, count - step, 2)]
    pairs += [(s, s - step) for s in range(step + 1, count, 2)]
    return lax.ppermute(value, SUB, pairs)


def per_device(
    impedance,
    incident,
    face_order,
    near_tiles,
    basis_right,
    rank_scale,
    rank_counts,
    coupling,
    basis_left,
):
    z_cols = impedance[0, 0]
    source = incident[0, 0]
    tiles = near_tiles[0, 0]
    right_basis = basis_right[0, 0]
    left_basis = basis_left[0, 0]
    n_layers, rank, _ = coupling.shape[1:]
    n_exc, width = source.shape
    layer = lax.axis_index(LAYER)
    quarter = lax.axis_index(QUARTER)
    n_q = lax.axis_size(QUARTER)
    rows = n_exc // n_q
    half = width - FACE_Q

    yl, core = lax.axis_index("yl"), lax.axis_index("core")
    n_x = lax.axis_size("yl") * lax.axis_size(GRP)
    first = core == 0

    flat = side_by_side(left_basis.reshape(-1, rank * rank // width, rank))
    both = lax.all_gather(jnp.concatenate([source, flat], 0), QUARTER)
    own, both = lax.optimization_barrier((coupling[0], both))
    own = own.reshape(n_layers * rank, rank)
    other = from_other(own, "yl")
    y_first = dot(side_by_side(both[:, :n_exc]), z_cols)
    left = both[:, n_exc:].reshape(n_q, -1, width // rank, rank)
    left = left.transpose(0, 2, 1, 3).reshape(n_q, rank, rank)

    kept = jnp.where(jnp.arange(rank) < rank_counts[layer], rank_scale[0], F32(0.0))
    scaled = (right_basis.astype(F32) * kept).astype(BF16)
    order = jnp.pad(face_order[0, 0].astype(BF16), (0, 16 * rank - FACE_Q))
    shared = [scaled, tiles.reshape(3 * rank, rank), order.reshape(16, rank)]
    shared = lax.all_gather(jnp.concatenate(shared, 0), "core")
    scaled = shared[:, :rank]
    passed = jnp.where(first, shared[:, 2 * rank : 3 * rank], shared[:, 3 * rank : 4 * rank])
    order = shared[:, 4 * rank :].reshape(2, -1)[:, :FACE_Q].astype(jnp.int32)
    same = jnp.broadcast_to(jnp.arange(FACE_Q, dtype=jnp.int32), order.shape)
    order = jnp.where(first, order, same)
    reorder = (jnp.arange(FACE_Q)[None, :, None] == order[:, None, :]).astype(BF16)

    others = (jnp.arange(n_layers) != layer)[:, None, None]
    z_quarters = z_cols.reshape(n_q, width, width)
    z_outer = z_quarters[:, 2 * FACE_Q :]
    far_to_y = jnp.einsum("qrt,qtc->qrc", left, z_outer, preferred_element_type=F32)
    far_to_y = far_to_y.reshape(n_q * rank, width).astype(BF16)
    z_near = []
    for chip in (0, 2):
        for face in (0, FACE_Q):
            for q in (chip, chip + 1):
                z_near += [z_quarters[q, face : face + FACE_Q], z_outer[q]]
    z_near = jnp.concatenate(z_near, 0)
    y_now = y_first

    def by_quarter(blocks):
        upper = in_order(core == 1, (blocks[0], blocks[1]))
        lower = in_order(core == 1, (blocks[2], blocks[3]))
        ones = in_order(yl == 1, (upper[0], lower[0]))
        twos = in_order(yl == 1, (upper[1], lower[1]))
        return ones[0], twos[0], ones[1], twos[1]

    for sweep in range(ITERS):
        outgoing = y_now.astype(BF16)
        pair = lax.all_gather(outgoing, "core")
        outer = pair[:, :, 2 * FACE_Q :]
        partial = dot(outer[0], scaled[0]) + dot(outer[1], scaled[1])
        partial = partial.astype(BF16).reshape(n_q // 2, 2, 1, rows, rank)
        partial = jnp.where(first, partial[:, 0], partial[:, 1])
        parts = jnp.broadcast_to(partial, (n_q // 2, 2 * n_x // n_q, rows, rank))
        parts = parts.reshape(n_x, rows, rank)
        arrived = lax.all_to_all(parts, ("yl",) + GRP, 0, 0, tiled=True)
        coefs = arrived.astype(F32).sum(0).astype(BF16)
        faces = jnp.where(first, pair[:, :, FACE_Q : 2 * FACE_Q], pair[:, :, :FACE_Q])
        faces = jnp.concatenate([faces[0], outer[0], faces[1], outer[1]], 1)
        faces = to_neighbours(faces)
        if sweep == 0:
            other, coefs = lax.optimization_barrier((other, coefs))
            chips = jnp.stack([own, other])
            of_all = jnp.stack([chips, from_other(chips, "core")], 1)
            couple = side_by_side(of_all.reshape(n_q, n_layers * rank, rank))
        by_own = dot(outgoing[:, 2 * FACE_Q :], tiles[0])
        near = []
        for k in (0, 1):
            face = faces[:, k * half : k * half + FACE_Q]
            trace = faces[:, k * half + FACE_Q : (k + 1) * half]
            near += [
                dot(face, reorder[k]),
                dot(trace, passed[k]) + jnp.where(core == k, by_own, F32(0.0)),
            ]
        near = jnp.concatenate(near, 1).astype(BF16)
        copies = jnp.broadcast_to(coefs, (n_layers, rows, rank))
        of_layers = lax.all_to_all(copies, LAYER, 0, 0, tiled=True)
        of_layers = jnp.where(others, of_layers, jnp.zeros_like(of_layers))
        far = dot(of_layers.transpose(1, 0, 2).reshape(rows, -1), couple)
        far = [far[:, k * rank : (k + 1) * rank] for k in range(n_q)]
        far = jnp.concatenate(by_quarter(far), 1).astype(BF16)
        if sweep < ITERS - 1:
            far = jnp.pad(far, ((0, 0), (0, 2 * half - width)))
            both = lax.all_gather(jnp.concatenate([near, far], 0), QUARTER)
            far = both[:, n_exc:, :width].reshape(n_exc, width)
            y_now = y_first + dot(side_by_side(both[:, :n_exc]), z_near)
            y_now = y_now + dot(far, far_to_y)
        else:
            near = lax.all_gather(near, "core").astype(F32)
            near = jnp.where(first, near[:, :, :half], near[:, :, half:])
            far = lax.all_gather(far, QUARTER).reshape(n_exc, width)
            far = lax.dynamic_slice_in_dim(far, quarter * rank, rank, 1)
            far = dot(far, left_basis)
            outer_in = near[0, :, FACE_Q:] + near[1, :, FACE_Q:] + far
            faces_in = [near[0, :, :FACE_Q], near[1, :, :FACE_Q]]
            trace = jnp.concatenate([*faces_in, outer_in], 1) + source.astype(F32)
    return trace.astype(BF16)[None, None]


def solution(mesh):
    finer = Mesh(mesh.devices.reshape(4, 4, 2, 2, 3, 4), SUB + GRP)
    placed = (
        P(SUB, GRP, None, None),
        P(SUB, GRP, None, None),
        P(SUB, GRP, None),
        P(SUB, GRP, None, None, None),
        P(SUB, GRP, None, None),
        P(SUB, None),
        P(),
        P(SUB, None, None, None),
        P(SUB, GRP, None, None),
    )
    return jax.shard_map(
        per_device,
        mesh=finer,
        in_specs=placed,
        out_specs=P(SUB, GRP, None, None),
        check_vma=False,
    )
```

time: 201 us -> 205 us (1.020)
  blocking collectives: 66.1 us -> 56.8 us
  matrix products: 9.19 us -> 14.8 us
  other arithmetic: 6.48 us -> 10.1 us
  starting transfers between devices: 64.9 us -> 61.5 us
  waiting for transfers between devices: 46.4 us -> 49.5 us
  local copies, waits for them, and re-layouts: 6.74 us -> 9.69 us
    all_to_all x1 -> x0, blocking collectives: 25.4 us -> none  [per_device(): of_layers = lax.all_to_all(copies, LAYER, 0, 0, tiled=True)]
    all_to_all x3, waiting for transfers between devices: 18.9 us -> 6.08 us  [per_device(): arrived = lax.all_to_all(parts, ('yl',) + GRP, 0, 0, tiled=True)]
    all_gather x2 -> x7, blocking collectives: 16.8 us -> 29.7 us  [the longest x2 18.1 us: per_device(): both = lax.all_gather(jnp.concatenate([near, far], 0), QUARTER)]
    all_to_all x2 -> x3, waiting for transfers between devices: 25.9 us -> 37.6 us  [per_device(): of_layers = lax.all_to_all(copies, LAYER, 0, 0, tiled=True)]
    dot_general x24 -> x30, matrix products: 7.85 us -> 14.5 us  [dot(): return jnp.dot(a, b, preferred_element_type=F32)]
    ppermute x6 -> x3, starting transfers between devices: 8.83 us -> 3.86 us  [to_neighbours(): return lax.ppermute(value, SUB, pairs)]
    ppermute x6 -> x3, waiting for transfers between devices: 1.53 us -> 5.8 us  [to_neighbours(): return lax.ppermute(value, SUB, pairs)]
    all_gather x1, blocking collectives: 7 us -> 10.3 us  [per_device(): far = lax.all_gather(far, QUARTER).reshape(n_exc, width)]
  transfers between devices with their start and end apart: 13 -> 11, of which waited for: 6 -> 6; matrix products, arithmetic and copies ran while one was open for 7% -> 12% of each run, Pallas kernels for 0% -> 0%
where the time goes in v4:
time: 205 us; the launch traced here: 203 us
  starting transfers between devices  61.5 us (30%)
  blocking collectives  56.8 us (28%)
  waiting for transfers between devices  49.5 us (24%)
  matrix products  14.8 us (7%)
  other arithmetic  10.1 us (5%)
  local copies, waits for them, and re-layouts  9.69 us (5%)
    all_to_all x3, waiting for transfers between devices, per_device(): of_layers = lax.all_to_all(copies, LAYER, 0, 0, tiled=True)  37.6 us
    all_to_all x3, starting transfers between devices, per_device(): of_layers = lax.all_to_all(copies, LAYER, 0, 0, tiled=True)  35.3 us
    all_gather x2, blocking collectives, per_device(): both = lax.all_gather(jnp.concatenate([near, far], 0), QUARTER)  18.1 us
    all_gather x1, blocking collectives, per_device(): both = lax.all_gather(jnp.concatenate([source, flat], 0), QUARTER)  16.9 us
    all_to_all x3, starting transfers between devices, per_device(): arrived = lax.all_to_all(parts, ('yl',) + GRP, 0, 0, tiled=True)  16.4 us
    dot_general x30, matrix products, dot(): return jnp.dot(a, b, preferred_element_type=F32)  14.5 us
    all_gather x1, blocking collectives, per_device(): far = lax.all_gather(far, QUARTER).reshape(n_exc, width)  10.3 us
    all_to_all x3, waiting for transfers between devices, per_device(): arrived = lax.all_to_all(parts, ('yl',) + GRP, 0, 0, tiled=True)  6.08 us
  transfers between devices with their start and end apart: 11, of which 6 were waited for; matrix products, arithmetic and copies ran while one was open for 12% of the time, Pallas kernels for 0%

profile of v4, /device:TPU:1, one launch (start us, length us, event | category | flops | bytes accessed | tf_op | source)
XLA Modules:
  0.0 203.2 jit_solution(13194488127944984939)
XLA Ops:
  0.0 0.7 slice_bitcast_fusion.70
  0.8 0.9 maximum_maximum_fusion
  1.7 16.9 %all-gather = bf16[512,512]{1,0:T(8,128)(2,1)S(1)} all-gather(bf16[128,512]{1,0:T(8,128)(2,1)S(1)} %maximum_maximum_fusion), channel_id=2, replica_groups=mesh['zh'=4,'yh'=4,'yl'=2,'core'=2,'zl'=3,'x'=4] {'yl','core'}, dimensions={0}, use_global_device_ids=true | all-gather | bytes 655360 | tf_op jit(solution)/shard_map/all_gather | solution.py:69
  18.5 2.8 %collective-permute-start.1 = (bf16[2048,128]{1,0:T(8,128)(2,1)}, bf16[2048,128]{1,0:T(8,128)(2,1)}, u32[]{:S(2)}, u32[]{:S(2)}) collective-permute-start(bf16[2048,128]{1,0:T(8,128)(2,1)} %bitcast.327), channel_id=1, source_target_pairs={{0,24},{24,0},{1,25},{25,1},{2,26},{26,2},{3,27},{27,3},{4,28},{28... | collective-permute-start | bytes 1572872 | tf_op jit(solution)/shard_map/ppermute | solution.py:25
  21.4 0.7 slice_bitcast_fusion.37
  22.0 0.7 convert_reduce_fusion
  22.7 1.3 dynamic_slice.6
  24.1 1.3 fusion.118
  25.3 0.8 fusion.66
  26.1 0.9 pad_maximum_fusion.5
  27.0 2.2 %all-gather.2 = bf16[1056,128]{1,0:T(8,128)(2,1)S(1)} all-gather(bf16[528,128]{1,0:T(8,128)(2,1)S(1)} %pad_maximum_fusion.5), channel_id=4, replica_groups=mesh['zh'=4,'yh'=4,'yl'=2,'core'=2,'zl'=3,'x'=4] {'core'}, dimensions={0}, use_global_device_ids=true | all-gather | bytes 405504 | tf_op jit(solution)/shard_map/all_gather | solution.py:81
  29.3 2.9 %fusion.124 = (bf16[96,512]{1,0:T(8,128)(2,1)S(1)}, f32[96,512]{1,0:T(8,128)}) fusion(bf16[1,1,2048,512]{3,2,1,0:T(8,128)(2,1)} %param.9, bf16[96,512]{1,0:T(8,128)(2,1)S(1)} %get-tuple-element.28, bf16[96,512]{1,0:T(8,128)(2,1)S(1)} %get-tuple-element.29, bf16[96,512]{1,0:T(8,128)(2,1)} %get-tuple-element.30, bf16[96,512]{1,0:T(8,128)(2,1)S(1)} %get-tuple-element.27), kind=kOutput, calls=%fused_computation.256 | convolution fusion | flops 202948608 | bytes 2785280 | tf_op jit(solution)/shard_map/dot_general | solution.py:17
  32.2 1.9 all-gather.1
  34.4 0.7 broadcast_in_dim.63
  35.1 3.8 %all-to-all-start = ((bf16[24,24,128]{2,1,0:T(8,128)(2,1)}), bf16[24,24,128]{2,1,0:T(8,128)(2,1)S(1)}, u32[]{:S(2)}, u32[]{:S(2)}) async-start(bf16[24,24,128]{2,1,0:T(8,128)(2,1)} %bitcast.33), calls=%async_computation | async-start | bytes 294912 | tf_op jit(solution)/shard_map/all_to_all | solution.py:118
  39.0 0.8 pad_maximum_fusion.6
  39.8 1.3 collective-permute-start
  41.6 1.5 copy-done.6
  43.5 3.2 %all-to-all-done = bf16[24,24,128]{2,1,0:T(8,128)(2,1)S(1)} async-done(((bf16[24,24,128]{2,1,0:T(8,128)(2,1)}), bf16[24,24,128]{2,1,0:T(8,128)(2,1)S(1)}, u32[]{:S(2)}, u32[]{:S(2)}) %all-to-all-start) | async-done | bytes 147488 | tf_op jit(solution)/shard_map/all_to_all | solution.py:118
  46.8 1.3 fusion.123
  48.1 3.2 %collective-permute-start.2 = (bf16[2,2048,128]{2,1,0:T(8,128)(2,1)S(1)}, bf16[2,2048,128]{2,1,0:T(8,128)(2,1)}, u32[]{:S(2)}, u32[]{:S(2)}) collective-permute-start(bf16[2,2048,128]{2,1,0:T(8,128)(2,1)S(1)} %get-tuple-element.18), channel_id=1, source_target_pairs={{0,12},{12,0},{1,13},{13,1},{2,14},{14,2},{3,15},{15,3},{4,16},{16... | collective-permute-start | bytes 3145736 | tf_op jit(solution)/shard_map/ppermute | solution.py:25
  51.4 1.0 fusion.7
  52.4 0.9 fusion.8
  53.3 1.1 convolution_convert_fusion.5
  54.4 1.6 convolution_convert_fusion.6
  56.6 15.5 %all-to-all-start.1 = ((bf16[16,24,128]{2,1,0:T(8,128)(2,1)}), bf16[16,24,128]{2,1,0:T(8,128)(2,1)S(1)}, u32[]{:S(2)}, u32[]{:S(2)}) async-start(bf16[16,24,128]{2,1,0:T(8,128)(2,1)} %broadcast_in_dim.64), calls=%async_computation.1 | async-start | bytes 196608 | tf_op jit(solution)/shard_map/all_to_all | solution.py:139
  72.1 1.4 pad_maximum_fusion
  73.6 12.2 %all-to-all-done.1 = bf16[16,24,128]{2,1,0:T(8,128)(2,1)S(1)} async-done(((bf16[16,24,128]{2,1,0:T(8,128)(2,1)}), bf16[16,24,128]{2,1,0:T(8,128)(2,1)S(1)}, u32[]{:S(2)}, u32[]{:S(2)}) %all-to-all-start.1) | async-done | bytes 98336 | tf_op jit(solution)/shard_map/all_to_all | solution.py:139
  86.7 8.7 %all-gather.3 = bf16[480,640]{1,0:T(8,128)(2,1)S(1)} all-gather(bf16[120,640]{1,0:T(8,128)(2,1)S(1)} %pad_maximum_fusion.3), channel_id=5, replica_groups=mesh['zh'=4,'yh'=4,'yl'=2,'core'=2,'zl'=3,'x'=4] {'yl','core'}, dimensions={0}, use_global_device_ids=true | all-gather | bytes 768000 | tf_op jit(solution)/shard_map/all_gather | solution.py:146
  96.3 1.9 all-gather.4
  99.3 4.8 %all-to-all-start.2 = ((bf16[24,24,128]{2,1,0:T(8,128)(2,1)}), bf16[24,24,128]{2,1,0:T(8,128)(2,1)S(1)}, u32[]{:S(2)}, u32[]{:S(2)}) async-start(bf16[24,24,128]{2,1,0:T(8,128)(2,1)} %bitcast.74), calls=%async_computation.2 | async-start | bytes 294912 | tf_op jit(solution)/shard_map/all_to_all | solution.py:118
  104.3 1.3 collective-permute-start.3
  105.7 5.8 %collective-permute-done.3 = bf16[96,640]{1,0:T(8,128)(2,1)S(1)} collective-permute-done((bf16[96,640]{1,0:T(8,128)(2,1)S(1)}, bf16[96,640]{1,0:T(8,128)(2,1)S(1)}, u32[]{:S(2)}, u32[]{:S(2)}) %collective-permute-start.3) | collective-permute-done | bytes 122912 | tf_op jit(solution)/shard_map/ppermute | solution.py:37
  113.1 10.5 %all-to-all-start.3 = ((bf16[16,24,128]{2,1,0:T(8,128)(2,1)}), bf16[16,24,128]{2,1,0:T(8,128)(2,1)S(1)}, u32[]{:S(2)}, u32[]{:S(2)}) async-start(bf16[16,24,128]{2,1,0:T(8,128)(2,1)} %broadcast_in_dim.66), calls=%async_computation.3 | async-start | bytes 196608 | tf_op jit(solution)/shard_map/all_to_all | solution.py:139
  123.6 1.0 fusion.10
  124.5 0.9 convolution_convert_fusion.4
  125.5 11.8 %all-to-all-done.3 = bf16[16,24,128]{2,1,0:T(8,128)(2,1)S(1)} async-done(((bf16[16,24,128]{2,1,0:T(8,128)(2,1)}), bf16[16,24,128]{2,1,0:T(8,128)(2,1)S(1)}, u32[]{:S(2)}, u32[]{:S(2)}) %all-to-all-start.3) | async-done | bytes 98336 | tf_op jit(solution)/shard_map/all_to_all | solution.py:139
  137.9 9.4 %all-gather.5 = bf16[480,640]{1,0:T(8,128)(2,1)S(1)} all-gather(bf16[120,640]{1,0:T(8,128)(2,1)S(1)} %pad_maximum_fusion.4), channel_id=7, replica_groups=mesh['zh'=4,'yh'=4,'yl'=2,'core'=2,'zl'=3,'x'=4] {'yl','core'}, dimensions={0}, use_global_device_ids=true | all-gather | bytes 768000 | tf_op jit(solution)/shard_map/all_gather | solution.py:146
  148.2 1.9 all-gather.6
  150.5 1.3 collective-permute-start.4
  151.9 0.7 broadcast_in_dim.67
  152.6 7.7 %all-to-all-start.4 = ((bf16[24,24,128]{2,1,0:T(8,128)(2,1)}), bf16[24,24,128]{2,1,0:T(8,128)(2,1)S(1)}, u32[]{:S(2)}, u32[]{:S(2)}) async-start(bf16[24,24,128]{2,1,0:T(8,128)(2,1)} %bitcast.96), calls=%async_computation.4 | async-start | bytes 294912 | tf_op jit(solution)/shard_map/all_to_all | solution.py:118
  161.3 3.5 %all_gather.64 = bf16[2,96,640]{2,1,0:T(8,128)(2,1)S(1)} all-gather(bf16[1,96,640]{2,1,0:T(8,128)(2,1)S(1)} %pad_maximum_fusion.9), channel_id=1, replica_groups=mesh['zh'=4,'yh'=4,'yl'=2,'core'=2,'zl'=3,'x'=4] {'core'}, dimensions={0}, use_global_device_ids=true | all-gather | bytes 368640 | tf_op jit(solution)/shard_map/all_gather | solution.py:151
  164.8 2.8 %all-to-all-done.4 = bf16[24,24,128]{2,1,0:T(8,128)(2,1)S(1)} async-done(((bf16[24,24,128]{2,1,0:T(8,128)(2,1)}), bf16[24,24,128]{2,1,0:T(8,128)(2,1)S(1)}, u32[]{:S(2)}, u32[]{:S(2)}) %all-to-all-start.4) | async-done | bytes 147488 | tf_op jit(solution)/shard_map/all_to_all | solution.py:118
  168.4 9.3 %all-to-all-start.5 = ((bf16[16,24,128]{2,1,0:T(8,128)(2,1)}), bf16[16,24,128]{2,1,0:T(8,128)(2,1)S(1)}, u32[]{:S(2)}, u32[]{:S(2)}) async-start(bf16[16,24,128]{2,1,0:T(8,128)(2,1)} %broadcast_in_dim.68), calls=%async_computation.5 | async-start | bytes 196608 | tf_op jit(solution)/shard_map/all_to_all | solution.py:139
  177.9 13.6 %all-to-all-done.5 = bf16[16,24,128]{2,1,0:T(8,128)(2,1)S(1)} async-done(((bf16[16,24,128]{2,1,0:T(8,128)(2,1)}), bf16[16,24,128]{2,1,0:T(8,128)(2,1)S(1)}, u32[]{:S(2)}, u32[]{:S(2)}) %all-to-all-start.5) | async-done | bytes 98336 | tf_op jit(solution)/shard_map/all_to_all | solution.py:139
  192.0 10.3 %all_gather.65 = bf16[4,24,512]{2,1,0:T(8,128)(2,1)S(1)} all-gather(bf16[1,24,512]{2,1,0:T(8,128)(2,1)S(1)} %pad_maximum_fusion.10), channel_id=1, replica_groups=mesh['zh'=4,'yh'=4,'yl'=2,'core'=2,'zl'=3,'x'=4] {'yl','core'}, dimensions={0}, use_global_device_ids=true | all-gather | bytes 122880 | tf_op jit(solution)/shard_map/all_gather | solution.py:153
  202.5 0.8 fusion.48
  (114 shorter events, 10.9 us)
Async XLA Ops:
  18.5 28.2 %collective-permute-start.1 = (bf16[2048,128]{1,0:T(8,128)(2,1)}, bf16[2048,128]{1,0:T(8,128)(2,1)}, u32[]{:S(2)}, u32[]{:S(2)}) collective-permute-start(bf16[2048,128]{1,0:T(8,128)(2,1)} %bitcast.327), channel_id=1, source_target_pairs={{0,24},{24,0},{1,25},{25,1},{2,26},{26,2},{3,27},{27,3},{4,28},{28... | collective-permute-start | bytes 1572872 | tf_op jit(solution)/shard_map/ppermute | solution.py:25
  27.0 14.1 %copy-start.1 = (bf16[1,1,3,128,128]{4,3,2,1,0:T(8,128)(2,1)S(1)}, bf16[1,1,3,128,128]{4,3,2,1,0:T(8,128)(2,1)}, u32[]{:S(2)}) copy-start(bf16[1,1,3,128,128]{4,3,2,1,0:T(8,128)(2,1)} %param.12) | copy-start | bytes 294916
  29.2 12.0 %copy-start = (bf16[1,1,2048,512]{3,2,1,0:T(8,128)(2,1)S(1)}, bf16[1,1,2048,512]{3,2,1,0:T(8,128)(2,1)}, u32[]{:S(2)}) copy-start(bf16[1,1,2048,512]{3,2,1,0:T(8,128)(2,1)} %param.9) | copy-start | bytes 6291460
  35.1 11.7 %all-to-all-start = ((bf16[24,24,128]{2,1,0:T(8,128)(2,1)}), bf16[24,24,128]{2,1,0:T(8,128)(2,1)S(1)}, u32[]{:S(2)}, u32[]{:S(2)}) async-start(bf16[24,24,128]{2,1,0:T(8,128)(2,1)} %bitcast.33), calls=%async_computation | async-start | bytes 294912 | tf_op jit(solution)/shard_map/all_to_all | solution.py:118
  39.8 11.6 %collective-permute-start = (bf16[96,640]{1,0:T(8,128)(2,1)}, bf16[96,640]{1,0:T(8,128)(2,1)}, u32[]{:S(2)}, u32[]{:S(2)}) collective-permute-start(bf16[96,640]{1,0:T(8,128)(2,1)} %pad_maximum_fusion.6), channel_id=1, source_target_pairs={{0,48},{24,72},{48,96},{72,120},{96,144},{120,168},{144,192},{168,... | collective-permute-start | bytes 368648 | tf_op jit(solution)/shard_map/ppermute | solution.py:37
  41.6 1.5 copy-start.6
  48.1 23.9 %collective-permute-start.2 = (bf16[2,2048,128]{2,1,0:T(8,128)(2,1)S(1)}, bf16[2,2048,128]{2,1,0:T(8,128)(2,1)}, u32[]{:S(2)}, u32[]{:S(2)}) collective-permute-start(bf16[2,2048,128]{2,1,0:T(8,128)(2,1)S(1)} %get-tuple-element.18), channel_id=1, source_target_pairs={{0,12},{12,0},{1,13},{13,1},{2,14},{14,2},{3,15},{15,3},{4,16},{16... | collective-permute-start | bytes 3145736 | tf_op jit(solution)/shard_map/ppermute | solution.py:25
  56.6 29.2 %all-to-all-start.1 = ((bf16[16,24,128]{2,1,0:T(8,128)(2,1)}), bf16[16,24,128]{2,1,0:T(8,128)(2,1)S(1)}, u32[]{:S(2)}, u32[]{:S(2)}) async-start(bf16[16,24,128]{2,1,0:T(8,128)(2,1)} %broadcast_in_dim.64), calls=%async_computation.1 | async-start | bytes 196608 | tf_op jit(solution)/shard_map/all_to_all | solution.py:139
  85.8 0.8 copy-start.4
  85.8 9.7 %copy-start.7 = (bf16[2560,512]{1,0:T(8,128)(2,1)S(1)}, bf16[2560,512]{1,0:T(8,128)(2,1)}, u32[]{:S(2)}) copy-start(bf16[2560,512]{1,0:T(8,128)(2,1)} %copy-done.6) | copy-start | bytes 7864324
  85.8 9.7 %copy-start.9 = (f32[96,512]{1,0:T(8,128)S(1)}, f32[96,512]{1,0:T(8,128)}, u32[]{:S(2)}) copy-start(f32[96,512]{1,0:T(8,128)} %get-tuple-element.62) | copy-start | bytes 589828
  99.3 13.0 %all-to-all-start.2 = ((bf16[24,24,128]{2,1,0:T(8,128)(2,1)}), bf16[24,24,128]{2,1,0:T(8,128)(2,1)S(1)}, u32[]{:S(2)}, u32[]{:S(2)}) async-start(bf16[24,24,128]{2,1,0:T(8,128)(2,1)} %bitcast.74), calls=%async_computation.2 | async-start | bytes 294912 | tf_op jit(solution)/shard_map/all_to_all | solution.py:118
  104.3 7.2 %collective-permute-start.3 = (bf16[96,640]{1,0:T(8,128)(2,1)S(1)}, bf16[96,640]{1,0:T(8,128)(2,1)S(1)}, u32[]{:S(2)}, u32[]{:S(2)}) collective-permute-start(bf16[96,640]{1,0:T(8,128)(2,1)S(1)} %pad_maximum_fusion.7), channel_id=1, source_target_pairs={{0,48},{24,72},{48,96},{72,120},{96,144},{120,168},{144,192},{168,... | collective-permute-start | bytes 368648 | tf_op jit(solution)/shard_map/ppermute | solution.py:37
  111.5 0.7 copy-start.5
  113.1 24.3 %all-to-all-start.3 = ((bf16[16,24,128]{2,1,0:T(8,128)(2,1)}), bf16[16,24,128]{2,1,0:T(8,128)(2,1)S(1)}, u32[]{:S(2)}, u32[]{:S(2)}) async-start(bf16[16,24,128]{2,1,0:T(8,128)(2,1)} %broadcast_in_dim.66), calls=%async_computation.3 | async-start | bytes 196608 | tf_op jit(solution)/shard_map/all_to_all | solution.py:139
  137.3 10.0 %copy-start.8 = (bf16[2560,512]{1,0:T(8,128)(2,1)S(1)}, bf16[2560,512]{1,0:T(8,128)(2,1)}, u32[]{:S(2)}) copy-start(bf16[2560,512]{1,0:T(8,128)(2,1)} %copy-done.6) | copy-start | bytes 7864324
  137.3 10.1 %copy-start.10 = (f32[96,512]{1,0:T(8,128)S(1)}, f32[96,512]{1,0:T(8,128)}, u32[]{:S(2)}) copy-start(f32[96,512]{1,0:T(8,128)} %get-tuple-element.62) | copy-start | bytes 589828
  150.5 10.0 %collective-permute-start.4 = (bf16[96,640]{1,0:T(8,128)(2,1)S(1)}, bf16[96,640]{1,0:T(8,128)(2,1)S(1)}, u32[]{:S(2)}, u32[]{:S(2)}) collective-permute-start(bf16[96,640]{1,0:T(8,128)(2,1)S(1)} %pad_maximum_fusion.8), channel_id=1, source_target_pairs={{0,48},{24,72},{48,96},{72,120},{96,144},{120,168},{144,192},{168,... | collective-permute-start | bytes 368648 | tf_op jit(solution)/shard_map/ppermute | solution.py:37
  152.6 15.1 %all-to-all-start.4 = ((bf16[24,24,128]{2,1,0:T(8,128)(2,1)}), bf16[24,24,128]{2,1,0:T(8,128)(2,1)S(1)}, u32[]{:S(2)}, u32[]{:S(2)}) async-start(bf16[24,24,128]{2,1,0:T(8,128)(2,1)} %bitcast.96), calls=%async_computation.4 | async-start | bytes 294912 | tf_op jit(solution)/shard_map/all_to_all | solution.py:118
  168.4 23.2 %all-to-all-start.5 = ((bf16[16,24,128]{2,1,0:T(8,128)(2,1)}), bf16[16,24,128]{2,1,0:T(8,128)(2,1)S(1)}, u32[]{:S(2)}, u32[]{:S(2)}) async-start(bf16[16,24,128]{2,1,0:T(8,128)(2,1)} %broadcast_in_dim.68), calls=%async_computation.5 | async-start | bytes 196608 | tf_op jit(solution)/shard_map/all_to_all | solution.py:139
  177.9 24.4 %copy-start.3 = (bf16[1,1,128,128]{3,2,1,0:T(8,128)(2,1)S(1)}, bf16[1,1,128,128]{3,2,1,0:T(8,128)(2,1)}, u32[]{:S(2)}) copy-start(bf16[1,1,128,128]{3,2,1,0:T(8,128)(2,1)} %param.17) | copy-start | bytes 98308
  177.9 24.6 %copy-start.2 = (bf16[1,1,96,512]{3,2,1,0:T(8,128)(2,1)S(1)}, bf16[1,1,96,512]{3,2,1,0:T(8,128)(2,1)}, u32[]{:S(2)}) copy-start(bf16[1,1,96,512]{3,2,1,0:T(8,128)(2,1)} %param.10) | copy-start | bytes 294916

commit v5 on v2

--- a/solution.py
+++ b/solution.py
@@ -62,19 +62,19 @@
     n_x, n_zl = lax.axis_size("x"), lax.axis_size("zl")
     rows = n_exc // n_q
 
-    near = lax.all_gather(source, QUARTER)
-    y_now = dot(side_by_side(near), z_cols)
+    yl, core = lax.axis_index("yl"), lax.axis_index("core")
+
+    both = jnp.pad(source, ((0, rank - n_exc), (0, 0)))
+    both = lax.all_gather(jnp.concatenate([both, left_basis], 1), QUARTER)
+    y_now = dot(side_by_side(both[:, :n_exc, :width]), z_cols)
+    left = both[:, :, width:]
 
     kept = jnp.where(jnp.arange(rank) < rank_counts[layer], rank_scale[0], F32(0.0))
     others = (jnp.arange(n_layers) != layer)[:, None, None]
-    own = jnp.where(others, coupling[0], jnp.zeros_like(coupling[0]))
-    own = jnp.concatenate([own.reshape(n_layers * rank, rank), left_basis], 0)
-    yl, core = lax.axis_index("yl"), lax.axis_index("core")
-    chips = jnp.stack([own, from_other(own, "yl")])
-    of_all = jnp.stack([chips, from_other(chips, "core")], 1)
-    of_all = of_all.reshape(n_q, n_layers * rank + rank, rank)
-    couple = side_by_side(of_all[:, : n_layers * rank])
-    left = of_all[:, n_layers * rank :]
+    z_outer = z_cols.reshape(n_q, width, width)[:, 2 * FACE_Q :]
+    far_to_y = jnp.einsum("qrt,qtc->qrc", left, z_outer, preferred_element_type=F32)
+    far_to_y = far_to_y.reshape(n_q * rank, width).astype(BF16)
+    reorder = jax.nn.one_hot(face_order[0, 0], FACE_Q, axis=0, dtype=BF16)
 
     def by_quarter(blocks):
         upper = in_order(core == 1, (blocks[0], blocks[1]))
@@ -82,12 +82,6 @@
         first = in_order(yl == 1, (upper[0], lower[0]))
         second = in_order(yl == 1, (upper[1], lower[1]))
         return first[0], second[0], first[1], second[1]
-
-    left = jnp.stack(by_quarter(left))
-    z_outer = z_cols.reshape(n_q, width, width)[:, 2 * FACE_Q :]
-    far_to_y = jnp.einsum("qrt,qtc->qrc", left, z_outer, preferred_element_type=F32)
-    far_to_y = far_to_y.reshape(n_q * rank, width).astype(BF16)
-    reorder = jax.nn.one_hot(face_order[0, 0], FACE_Q, axis=0, dtype=BF16)
 
     for sweep in range(ITERS):
         outgoing = y_now.astype(BF16)
@@ -100,10 +94,17 @@
         coefs = arrived.astype(F32).sum(0).astype(BF16)
         copies = jnp.broadcast_to(coefs, (n_layers * n_zl, rows, rank))
         copies, outgoing = lax.optimization_barrier((copies, outgoing))
+        if sweep == 0:
+            copies, own = lax.optimization_barrier((copies, coupling[0]))
+            own = own.reshape(n_layers * rank, rank)
+            across = from_other(own, "yl")
+            couple = [own, from_other(own, "core"), across, from_other(across, "core")]
+            couple = jnp.concatenate(couple, 1)
         outer_out = outgoing[:, 2 * FACE_Q :]
         of_layers = lax.all_to_all(copies, SECOND, 0, 0, tiled=True)
         of_layers = of_layers.reshape(n_layers, n_zl, rows, rank)
         of_layers = of_layers.astype(F32).sum(1).astype(BF16)
+        of_layers = jnp.where(others, of_layers, jnp.zeros_like(of_layers))
         below = shifted(outgoing[:, FACE_Q:], 4)
         above = shifted(jnp.concatenate([outgoing[:, :FACE_Q], outer_out], 1), -4)
         lower_in = dot(below[:, :FACE_Q], reorder)

time: 194 us -> 190 us (0.979)
  matrix products: 7.47 us -> 12.4 us
  other arithmetic: 7.74 us -> 3.78 us
  blocking collectives: 54.5 us -> 50.8 us
    ppermute x6, waiting for transfers between devices: 21.6 us -> 26.8 us  [shifted(): lax.ppermute(value, SUB, [(s, s + steps) for s in range(first, last)])]
    dot_general x24, matrix products: 7.19 us -> 11.1 us  [dot(): return jnp.dot(a, b, preferred_element_type=F32)]
    another operation x5 -> x2, other arithmetic: 3.52 us -> 0.03 us  [the longest x2 2.65 us: per_device(): of_all = jnp.stack([chips, from_other(chips, 'core')], 1)]
    all_gather x1, blocking collectives: 20.7 us -> 17.2 us  [per_device(): both = lax.all_gather(jnp.concatenate([both, left_basis], 1), QUARTER)]
    all_to_all x3, waiting for transfers between devices: 16 us -> 13.6 us  [per_device(): of_layers = lax.all_to_all(copies, SECOND, 0, 0, tiled=True)]
    ppermute x2 -> x3, starting transfers between devices: 7.23 us -> 8.7 us  [from_other(): return lax.ppermute(value, axis, [(0, 1), (1, 0)])]
  transfers between devices with their start and end apart: 13 -> 14, of which waited for: 9 -> 10; matrix products, arithmetic and copies ran while one was open for 5% -> 2% of each run, Pallas kernels for 0% -> 0%
where the time goes in v5:
time: 190 us; the launch traced here: 189 us
  starting transfers between devices  65.7 us (35%)
  blocking collectives  50.8 us (27%)
  waiting for transfers between devices  50.8 us (27%)
  matrix products  12.4 us (7%)
  local copies, waits for them, and re-layouts  5.32 us (3%)
  other arithmetic  3.78 us (2%)
    all_to_all x3, starting transfers between devices, per_device(): of_layers = lax.all_to_all(copies, SECOND, 0, 0, tiled=True)  34.4 us
    ppermute x6, waiting for transfers between devices, shifted(): lax.ppermute(value, SUB, [(s, s + steps) for s in range(first, last)])  26.8 us
    all_gather x2, blocking collectives, per_device(): both = lax.all_gather(both, QUARTER)  17.3 us
    all_gather x1, blocking collectives, per_device(): both = lax.all_gather(jnp.concatenate([both, left_basis], 1), QUARTER)  17.2 us
    ppermute x6, starting transfers between devices, shifted(): lax.ppermute(value, SUB, [(s, s + steps) for s in range(first, last)])  15.7 us
    all_to_all x3, waiting for transfers between devices, per_device(): of_layers = lax.all_to_all(copies, SECOND, 0, 0, tiled=True)  13.6 us
    dot_general x24, matrix products, dot(): return jnp.dot(a, b, preferred_element_type=F32)  11.1 us
    all_to_all x2, waiting for transfers between devices, per_device(): arrived = lax.all_to_all(parts, FIRST, 0, 0, tiled=True)  10.4 us
  transfers between devices with their start and end apart: 14, of which 10 were waited for; matrix products, arithmetic and copies ran while one was open for 2% of the time, Pallas kernels for 0%

profile of v5, /device:TPU:1, one launch (start us, length us, event | category | flops | bytes accessed | tf_op | source)
XLA Modules:
  0.0 189.4 jit_solution(8635559585258066787)
XLA Ops:
  0.0 0.9 fusion.54
  0.9 17.2 %all-gather = bf16[512,640]{1,0:T(8,128)(2,1)S(1)} all-gather(bf16[128,640]{1,0:T(8,128)(2,1)S(1)} %fusion.54), channel_id=2, replica_groups=mesh['zh'=4,'yh'=4,'yl'=2,'core'=2,'zl'=3,'x'=4] {'yl','core'}, dimensions={0}, use_global_device_ids=true | all-gather | bytes 819200 | tf_op jit(solution)/shard_map/all_gather | solution.py:68
  18.2 1.2 dynamic_slice.6
  19.4 1.3 fusion.110
  20.7 2.1 %fusion.18 = bf16[96,512]{1,0:T(8,128)(2,1)S(1)} fusion(bf16[1,1,2048,512]{3,2,1,0:T(8,128)(2,1)} %param.9, bf16[96,512]{1,0:T(8,128)(2,1)S(1)} %get-tuple-element.22, bf16[96,512]{1,0:T(8,128)(2,1)S(1)} %get-tuple-element.23, bf16[96,512]{1,0:T(8,128)(2,1)S(1)} %get-tuple-element.24, bf16[96,512]{1,0:T(8,128)(2,1)S(1)} %get-tuple-element.21), kind=kOutput, calls=%fused_computation.12 | convolution fusion | flops 202948608 | bytes 2588672 | tf_op jit(solution)/shard_map/dot_general | solution.py:19
  23.0 0.7 broadcast_in_dim.57
  23.7 3.5 %all-to-all-start = ((bf16[16,24,128]{2,1,0:T(8,128)(2,1)}), bf16[16,24,128]{2,1,0:T(8,128)(2,1)S(1)}, u32[]{:S(2)}, u32[]{:S(2)}) async-start(bf16[16,24,128]{2,1,0:T(8,128)(2,1)} %bitcast.12), calls=%async_computation | async-start | bytes 196608 | tf_op jit(solution)/shard_map/all_to_all | solution.py:93
  27.2 1.3 convolution_convert_fusion
  28.5 4.5 %all-to-all-done = bf16[16,24,128]{2,1,0:T(8,128)(2,1)S(1)} async-done(((bf16[16,24,128]{2,1,0:T(8,128)(2,1)}), bf16[16,24,128]{2,1,0:T(8,128)(2,1)S(1)}, u32[]{:S(2)}, u32[]{:S(2)}) %all-to-all-start) | async-done | bytes 98336 | tf_op jit(solution)/shard_map/all_to_all | solution.py:93
  33.1 0.8 broadcast_in_dim.58
  34.0 2.4 %collective-permute-start.3 = (bf16[2048,128]{1,0:T(8,128)(2,1)S(1)}, bf16[2048,128]{1,0:T(8,128)(2,1)S(1)}, u32[]{:S(2)}, u32[]{:S(2)}) collective-permute-start(bf16[2048,128]{1,0:T(8,128)(2,1)S(1)} %bitcast.164), channel_id=1, source_target_pairs={{0,24},{24,0},{1,25},{25,1},{2,26},{26,2},{3,27},{27,3},{4,28},{28... | collective-permute-start | bytes 1572872 | tf_op jit(solution)/shard_map/ppermute | solution.py:27
  36.3 2.6 %collective-permute-start.2 = (bf16[2048,128]{1,0:T(8,128)(2,1)S(1)}, bf16[2048,128]{1,0:T(8,128)(2,1)S(1)}, u32[]{:S(2)}, u32[]{:S(2)}) collective-permute-start(bf16[2048,128]{1,0:T(8,128)(2,1)S(1)} %bitcast.165), channel_id=1, source_target_pairs={{0,12},{12,0},{1,13},{13,1},{2,14},{14,2},{3,15},{15,3},{4,16},{16... | collective-permute-start | bytes 1572872 | tf_op jit(solution)/shard_map/ppermute | solution.py:27
  39.0 13.7 %all-to-all-start.1 = ((bf16[48,24,128]{2,1,0:T(8,128)(2,1)}), bf16[48,24,128]{2,1,0:T(8,128)(2,1)S(1)}, u32[]{:S(2)}, u32[]{:S(2)}) async-start(bf16[48,24,128]{2,1,0:T(8,128)(2,1)} %broadcast_in_dim.58), calls=%async_computation.1 | async-start | bytes 589824 | tf_op jit(solution)/shard_map/all_to_all | solution.py:104
  52.8 3.9 %collective-permute-start = (bf16[96,320]{1,0:T(8,128)(2,1)S(1)}, bf16[96,320]{1,0:T(8,128)(2,1)S(1)}, u32[]{:S(2)}, u32[]{:S(2)}) collective-permute-start(bf16[96,320]{1,0:T(8,128)(2,1)S(1)} %slice.201), channel_id=1, source_target_pairs={{0,48},{12,60},{24,72},{36,84},{48,96},{60,108},{72,120},{84,132},... | collective-permute-start | bytes 184328 | tf_op jit(solution)/shard_map/ppermute | solution.py:38
  56.8 1.3 collective-permute-start.1
  58.5 3.7 %collective-permute-start.4 = (bf16[2048,128]{1,0:T(8,128)(2,1)S(1)}, bf16[2048,128]{1,0:T(8,128)(2,1)}, u32[]{:S(2)}, u32[]{:S(2)}) collective-permute-start(bf16[2048,128]{1,0:T(8,128)(2,1)S(1)} %collective-permute-done.3), channel_id=1, source_target_pairs={{0,12},{12,0},{1,13},{13,1},{2,14},{14,2},{3,15},{15,3},{4,16},{16... | collective-permute-start | bytes 1572872 | tf_op jit(solution)/shard_map/ppermute | solution.py:27
  62.2 5.2 %collective-permute-done.1 = bf16[96,320]{1,0:T(8,128)(2,1)S(1)} collective-permute-done((bf16[96,320]{1,0:T(8,128)(2,1)S(1)}, bf16[96,320]{1,0:T(8,128)(2,1)S(1)}, u32[]{:S(2)}, u32[]{:S(2)}) %collective-permute-start.1) | collective-permute-done | bytes 61472 | tf_op jit(solution)/shard_map/ppermute | solution.py:38
  67.8 5.9 %all-to-all-done.1 = bf16[48,24,128]{2,1,0:T(8,128)(2,1)S(1)} async-done(((bf16[48,24,128]{2,1,0:T(8,128)(2,1)}), bf16[48,24,128]{2,1,0:T(8,128)(2,1)S(1)}, u32[]{:S(2)}, u32[]{:S(2)}) %all-to-all-start.1) | async-done | bytes 294944 | tf_op jit(solution)/shard_map/all_to_all | solution.py:104
  73.8 1.7 fusion.62
  75.5 8.8 %all-gather.1 = bf16[480,512]{1,0:T(8,128)(2,1)S(1)} all-gather(bf16[120,512]{1,0:T(8,128)(2,1)S(1)} %maximum_maximum_fusion), channel_id=3, replica_groups=mesh['zh'=4,'yh'=4,'yl'=2,'core'=2,'zl'=3,'x'=4] {'yl','core'}, dimensions={0}, use_global_device_ids=true | all-gather | bytes 614400 | tf_op jit(solution)/shard_map/all_gather | solution.py:120
  84.3 0.2 fusion.119
  84.5 0.5 fusion.15
  85.1 8.9 %all_to_all.30 = bf16[16,24,128]{2,1,0:T(8,128)(2,1)S(1)} all-to-all(bf16[16,24,128]{2,1,0:T(8,128)(2,1)S(1)} %bitcast.153), channel_id=1, replica_groups=mesh['zh'=4,'yh'=4,'yl'=2,'core'=2,'zl'=3,'x'=4] {'yl','core','x'}, dimensions={0} | all-to-all | bytes 196608 | tf_op jit(solution)/shard_map/all_to_all | solution.py:93
  94.1 0.7 broadcast_in_dim.62
  95.1 11.4 %all-to-all-start.3 = ((bf16[48,24,128]{2,1,0:T(8,128)(2,1)}), bf16[48,24,128]{2,1,0:T(8,128)(2,1)S(1)}, u32[]{:S(2)}, u32[]{:S(2)}) async-start(bf16[48,24,128]{2,1,0:T(8,128)(2,1)} %broadcast_in_dim.62), calls=%async_computation.3 | async-start | bytes 589824 | tf_op jit(solution)/shard_map/all_to_all | solution.py:104
  106.5 3.9 %collective-permute-start.5 = (bf16[96,320]{1,0:T(8,128)(2,1)S(1)}, bf16[96,320]{1,0:T(8,128)(2,1)S(1)}, u32[]{:S(2)}, u32[]{:S(2)}) collective-permute-start(bf16[96,320]{1,0:T(8,128)(2,1)S(1)} %slice.223), channel_id=1, source_target_pairs={{0,48},{12,60},{24,72},{36,84},{48,96},{60,108},{72,120},{84,132},... | collective-permute-start | bytes 184328 | tf_op jit(solution)/shard_map/ppermute | solution.py:38
  110.5 1.3 collective-permute-start.6
  111.8 0.3 collective-permute-done.5
  112.2 10.6 %collective-permute-done.6 = bf16[96,320]{1,0:T(8,128)(2,1)S(1)} collective-permute-done((bf16[96,320]{1,0:T(8,128)(2,1)S(1)}, bf16[96,320]{1,0:T(8,128)(2,1)S(1)}, u32[]{:S(2)}, u32[]{:S(2)}) %collective-permute-start.6) | collective-permute-done | bytes 61472 | tf_op jit(solution)/shard_map/ppermute | solution.py:38
  123.4 3.8 %all-to-all-done.3 = bf16[48,24,128]{2,1,0:T(8,128)(2,1)S(1)} async-done(((bf16[48,24,128]{2,1,0:T(8,128)(2,1)}), bf16[48,24,128]{2,1,0:T(8,128)(2,1)S(1)}, u32[]{:S(2)}, u32[]{:S(2)}) %all-to-all-start.3) | async-done | bytes 294944 | tf_op jit(solution)/shard_map/all_to_all | solution.py:104
  127.2 1.9 %fusion.59 = bf16[24,512]{1,0:T(8,128)(2,1)S(1)} fusion(bf16[2048,128]{1,0:T(8,128)(2,1)} %collective-permute-done.4, bf16[2048,128]{1,0:T(8,128)(2,1)} %copy-done.8, bf16[2048,128]{1,0:T(8,128)(2,1)} %copy-done.10, bf16[2048,128]{1,0:T(8,128)(2,1)} %bitcast.163, bf16[16,24,128]{2,1,0:T(8,128)(2,1)S(1)} %reduce_sum.75, pred[16]{0:T(512)(128)(4,1)S(1)} %iota_compare_fusion.5), kind=kOutput, calls=%fused_computation.69 | convolution fusion | flops 58769408 | bytes 2220048 | tf_op jit(solution)/shard_map/dot_general | solution.py:19
  129.2 8.5 %all-gather.2 = bf16[480,512]{1,0:T(8,128)(2,1)S(1)} all-gather(bf16[120,512]{1,0:T(8,128)(2,1)S(1)} %maximum_maximum_fusion.1), channel_id=4, replica_groups=mesh['zh'=4,'yh'=4,'yl'=2,'core'=2,'zl'=3,'x'=4] {'yl','core'}, dimensions={0}, use_global_device_ids=true | all-gather | bytes 614400 | tf_op jit(solution)/shard_map/all_gather | solution.py:120
  137.7 0.2 fusion.120
  137.9 0.5 fusion.12
  138.6 0.7 broadcast_in_dim.64
  139.2 3.5 %all-to-all-start.4 = ((bf16[16,24,128]{2,1,0:T(8,128)(2,1)}), bf16[16,24,128]{2,1,0:T(8,128)(2,1)S(1)}, u32[]{:S(2)}, u32[]{:S(2)}) async-start(bf16[16,24,128]{2,1,0:T(8,128)(2,1)} %bitcast.40), calls=%async_computation.4 | async-start | bytes 196608 | tf_op jit(solution)/shard_map/all_to_all | solution.py:93
  142.7 5.9 %all-to-all-done.4 = bf16[16,24,128]{2,1,0:T(8,128)(2,1)S(1)} async-done(((bf16[16,24,128]{2,1,0:T(8,128)(2,1)}), bf16[16,24,128]{2,1,0:T(8,128)(2,1)S(1)}, u32[]{:S(2)}, u32[]{:S(2)}) %all-to-all-start.4) | async-done | bytes 98336 | tf_op jit(solution)/shard_map/all_to_all | solution.py:93
  148.6 0.7 broadcast_in_dim.65
  149.6 9.3 %all-to-all-start.5 = ((bf16[48,24,128]{2,1,0:T(8,128)(2,1)}), bf16[48,24,128]{2,1,0:T(8,128)(2,1)S(1)}, u32[]{:S(2)}, u32[]{:S(2)}) async-start(bf16[48,24,128]{2,1,0:T(8,128)(2,1)} %broadcast_in_dim.65), calls=%async_computation.5 | async-start | bytes 589824 | tf_op jit(solution)/shard_map/all_to_all | solution.py:104
  158.9 3.9 %collective-permute-start.7 = (bf16[96,320]{1,0:T(8,128)(2,1)S(1)}, bf16[96,320]{1,0:T(8,128)(2,1)S(1)}, u32[]{:S(2)}, u32[]{:S(2)}) collective-permute-start(bf16[96,320]{1,0:T(8,128)(2,1)S(1)} %slice.240), channel_id=1, source_target_pairs={{0,48},{12,60},{24,72},{36,84},{48,96},{60,108},{72,120},{84,132},... | collective-permute-start | bytes 184328 | tf_op jit(solution)/shard_map/ppermute | solution.py:38
  162.9 1.3 collective-permute-start.8
  164.2 0.3 collective-permute-done.7
  164.9 10.4 %collective-permute-done.8 = bf16[96,320]{1,0:T(8,128)(2,1)S(1)} collective-permute-done((bf16[96,320]{1,0:T(8,128)(2,1)S(1)}, bf16[96,320]{1,0:T(8,128)(2,1)S(1)}, u32[]{:S(2)}, u32[]{:S(2)}) %collective-permute-start.8) | collective-permute-done | bytes 61472 | tf_op jit(solution)/shard_map/ppermute | solution.py:38
  175.3 0.2 convolution_add_fusion.1
  175.6 3.9 %all-to-all-done.5 = bf16[48,24,128]{2,1,0:T(8,128)(2,1)S(1)} async-done(((bf16[48,24,128]{2,1,0:T(8,128)(2,1)}), bf16[48,24,128]{2,1,0:T(8,128)(2,1)S(1)}, u32[]{:S(2)}, u32[]{:S(2)}) %all-to-all-start.5) | async-done | bytes 294944 | tf_op jit(solution)/shard_map/all_to_all | solution.py:104
  179.7 1.5 fusion.56
  181.2 7.4 %all_gather.28 = bf16[4,24,512]{2,1,0:T(8,128)(2,1)S(1)} all-gather(bf16[1,24,512]{2,1,0:T(8,128)(2,1)S(1)} %pad_maximum_fusion.5), channel_id=1, replica_groups=mesh['zh'=4,'yh'=4,'yl'=2,'core'=2,'zl'=3,'x'=4] {'yl','core'}, dimensions={0}, use_global_device_ids=true | all-gather | bytes 122880 | tf_op jit(solution)/shard_map/all_gather | solution.py:124
  188.7 0.7 pad_maximum_fusion.1
  (81 shorter events, 3.8 us)
Async XLA Ops:
  0.0 22.9 %copy-start = (bf16[1,1,128,128]{3,2,1,0:T(8,128)(2,1)S(1)}, bf16[1,1,128,128]{3,2,1,0:T(8,128)(2,1)}, u32[]{:S(2)}) copy-start(bf16[1,1,128,128]{3,2,1,0:T(8,128)(2,1)} %param.13) | copy-start | bytes 98308
  20.7 13.2 %copy-start.6 = (bf16[1,16,128,128]{3,2,1,0:T(8,128)(2,1)S(1)}, bf16[1,16,128,128]{3,2,1,0:T(8,128)(2,1)}, u32[]{:S(2)}) copy-start(bf16[1,16,128,128]{3,2,1,0:T(8,128)(2,1)} %param.16) | copy-start | bytes 1572868
  22.9 29.8 %copy-start.2 = (bf16[1,1,3,128,128]{4,3,2,1,0:T(8,128)(2,1)S(1)}, bf16[1,1,3,128,128]{4,3,2,1,0:T(8,128)(2,1)}, u32[]{:S(2)}) copy-start(bf16[1,1,3,128,128]{4,3,2,1,0:T(8,128)(2,1)} %param.12) | copy-start | bytes 294916
  22.9 35.5 %copy-start.5 = (s32[1,1,192]{2,1,0:T(1,128)S(1)}, s32[1,1,192]{2,1,0:T(1,128)}, u32[]{:S(2)}) copy-start(s32[1,1,192]{2,1,0:T(1,128)} %param.11) | copy-start | bytes 2308
  22.9 44.8 %copy-start.1 = (bf16[1,1,96,512]{3,2,1,0:T(8,128)(2,1)S(1)}, bf16[1,1,96,512]{3,2,1,0:T(8,128)(2,1)}, u32[]{:S(2)}) copy-start(bf16[1,1,96,512]{3,2,1,0:T(8,128)(2,1)} %param.10) | copy-start | bytes 294916
  23.7 9.4 %all-to-all-start = ((bf16[16,24,128]{2,1,0:T(8,128)(2,1)}), bf16[16,24,128]{2,1,0:T(8,128)(2,1)S(1)}, u32[]{:S(2)}, u32[]{:S(2)}) async-start(bf16[16,24,128]{2,1,0:T(8,128)(2,1)} %bitcast.12), calls=%async_computation | async-start | bytes 196608 | tf_op jit(solution)/shard_map/all_to_all | solution.py:93
  34.0 24.5 %collective-permute-start.3 = (bf16[2048,128]{1,0:T(8,128)(2,1)S(1)}, bf16[2048,128]{1,0:T(8,128)(2,1)S(1)}, u32[]{:S(2)}, u32[]{:S(2)}) collective-permute-start(bf16[2048,128]{1,0:T(8,128)(2,1)S(1)} %bitcast.164), channel_id=1, source_target_pairs={{0,24},{24,0},{1,25},{25,1},{2,26},{26,2},{3,27},{27,3},{4,28},{28... | collective-permute-start | bytes 1572872 | tf_op jit(solution)/shard_map/ppermute | solution.py:27
  36.3 37.4 %collective-permute-start.2 = (bf16[2048,128]{1,0:T(8,128)(2,1)S(1)}, bf16[2048,128]{1,0:T(8,128)(2,1)S(1)}, u32[]{:S(2)}, u32[]{:S(2)}) collective-permute-start(bf16[2048,128]{1,0:T(8,128)(2,1)S(1)} %bitcast.165), channel_id=1, source_target_pairs={{0,12},{12,0},{1,13},{13,1},{2,14},{14,2},{3,15},{15,3},{4,16},{16... | collective-permute-start | bytes 1572872 | tf_op jit(solution)/shard_map/ppermute | solution.py:27
  39.0 34.7 %all-to-all-start.1 = ((bf16[48,24,128]{2,1,0:T(8,128)(2,1)}), bf16[48,24,128]{2,1,0:T(8,128)(2,1)S(1)}, u32[]{:S(2)}, u32[]{:S(2)}) async-start(bf16[48,24,128]{2,1,0:T(8,128)(2,1)} %broadcast_in_dim.58), calls=%async_computation.1 | async-start | bytes 589824 | tf_op jit(solution)/shard_map/all_to_all | solution.py:104
  52.8 5.3 %collective-permute-start = (bf16[96,320]{1,0:T(8,128)(2,1)S(1)}, bf16[96,320]{1,0:T(8,128)(2,1)S(1)}, u32[]{:S(2)}, u32[]{:S(2)}) collective-permute-start(bf16[96,320]{1,0:T(8,128)(2,1)S(1)} %slice.201), channel_id=1, source_target_pairs={{0,48},{12,60},{24,72},{36,84},{48,96},{60,108},{72,120},{84,132},... | collective-permute-start | bytes 184328 | tf_op jit(solution)/shard_map/ppermute | solution.py:38
  56.8 10.7 %collective-permute-start.1 = (bf16[96,320]{1,0:T(8,128)(2,1)S(1)}, bf16[96,320]{1,0:T(8,128)(2,1)S(1)}, u32[]{:S(2)}, u32[]{:S(2)}) collective-permute-start(bf16[96,320]{1,0:T(8,128)(2,1)S(1)} %pad_maximum_fusion.2), channel_id=1, source_target_pairs={{48,0},{60,12},{72,24},{84,36},{96,48},{108,60},{120,72},{132,84},... | collective-permute-start | bytes 184328 | tf_op jit(solution)/shard_map/ppermute | solution.py:38
  58.5 15.2 %copy-start.8 = (bf16[2048,128]{1,0:T(8,128)(2,1)}, bf16[2048,128]{1,0:T(8,128)(2,1)S(1)}, u32[]{:S(2)}) copy-start(bf16[2048,128]{1,0:T(8,128)(2,1)S(1)} %collective-permute-done.3) | copy-start | bytes 1572868
  58.5 15.2 %collective-permute-start.4 = (bf16[2048,128]{1,0:T(8,128)(2,1)S(1)}, bf16[2048,128]{1,0:T(8,128)(2,1)}, u32[]{:S(2)}, u32[]{:S(2)}) collective-permute-start(bf16[2048,128]{1,0:T(8,128)(2,1)S(1)} %collective-permute-done.3), channel_id=1, source_target_pairs={{0,12},{12,0},{1,13},{13,1},{2,14},{14,2},{3,15},{15,3},{4,16},{16... | collective-permute-start | bytes 1572872 | tf_op jit(solution)/shard_map/ppermute | solution.py:27
  73.7 1.7 copy-start.10
  75.4 9.1 %copy-start.3 = (bf16[1,1,2048,512]{3,2,1,0:T(8,128)(2,1)S(1)}, bf16[1,1,2048,512]{3,2,1,0:T(8,128)(2,1)}, u32[]{:S(2)}) copy-start(bf16[1,1,2048,512]{3,2,1,0:T(8,128)(2,1)} %param.9) | copy-start | bytes 6291460
  95.1 32.1 %all-to-all-start.3 = ((bf16[48,24,128]{2,1,0:T(8,128)(2,1)}), bf16[48,24,128]{2,1,0:T(8,128)(2,1)S(1)}, u32[]{:S(2)}, u32[]{:S(2)}) async-start(bf16[48,24,128]{2,1,0:T(8,128)(2,1)} %broadcast_in_dim.62), calls=%async_computation.3 | async-start | bytes 589824 | tf_op jit(solution)/shard_map/all_to_all | solution.py:104
  106.5 5.6 %collective-permute-start.5 = (bf16[96,320]{1,0:T(8,128)(2,1)S(1)}, bf16[96,320]{1,0:T(8,128)(2,1)S(1)}, u32[]{:S(2)}, u32[]{:S(2)}) collective-permute-start(bf16[96,320]{1,0:T(8,128)(2,1)S(1)} %slice.223), channel_id=1, source_target_pairs={{0,48},{12,60},{24,72},{36,84},{48,96},{60,108},{72,120},{84,132},... | collective-permute-start | bytes 184328 | tf_op jit(solution)/shard_map/ppermute | solution.py:38
  110.5 12.3 %collective-permute-start.6 = (bf16[96,320]{1,0:T(8,128)(2,1)S(1)}, bf16[96,320]{1,0:T(8,128)(2,1)S(1)}, u32[]{:S(2)}, u32[]{:S(2)}) collective-permute-start(bf16[96,320]{1,0:T(8,128)(2,1)S(1)} %pad_maximum_fusion.3), channel_id=1, source_target_pairs={{48,0},{60,12},{72,24},{84,36},{96,48},{108,60},{120,72},{132,84},... | collective-permute-start | bytes 184328 | tf_op jit(solution)/shard_map/ppermute | solution.py:38
  138.4 41.2 %copy-start.7 = (bf16[1,16,128,128]{3,2,1,0:T(8,128)(2,1)S(1)}, bf16[1,16,128,128]{3,2,1,0:T(8,128)(2,1)}, u32[]{:S(2)}) copy-start(bf16[1,16,128,128]{3,2,1,0:T(8,128)(2,1)} %param.16) | copy-start | bytes 1572868
  138.4 41.2 %copy-start.9 = (bf16[2048,128]{1,0:T(8,128)(2,1)S(1)}, bf16[2048,128]{1,0:T(8,128)(2,1)}, u32[]{:S(2)}) copy-start(bf16[2048,128]{1,0:T(8,128)(2,1)} %copy-done.8) | copy-start | bytes 1572868
  138.4 41.2 %copy-start.11 = (bf16[2048,128]{1,0:T(8,128)(2,1)S(1)}, bf16[2048,128]{1,0:T(8,128)(2,1)}, u32[]{:S(2)}) copy-start(bf16[2048,128]{1,0:T(8,128)(2,1)} %copy-done.10) | copy-start | bytes 1572868
  139.2 9.3 %all-to-all-start.4 = ((bf16[16,24,128]{2,1,0:T(8,128)(2,1)}), bf16[16,24,128]{2,1,0:T(8,128)(2,1)S(1)}, u32[]{:S(2)}, u32[]{:S(2)}) async-start(bf16[16,24,128]{2,1,0:T(8,128)(2,1)} %bitcast.40), calls=%async_computation.4 | async-start | bytes 196608 | tf_op jit(solution)/shard_map/all_to_all | solution.py:93
  149.6 30.0 %all-to-all-start.5 = ((bf16[48,24,128]{2,1,0:T(8,128)(2,1)}), bf16[48,24,128]{2,1,0:T(8,128)(2,1)S(1)}, u32[]{:S(2)}, u32[]{:S(2)}) async-start(bf16[48,24,128]{2,1,0:T(8,128)(2,1)} %broadcast_in_dim.65), calls=%async_computation.5 | async-start | bytes 589824 | tf_op jit(solution)/shard_map/all_to_all | solution.py:104
  158.9 5.6 %collective-permute-start.7 = (bf16[96,320]{1,0:T(8,128)(2,1)S(1)}, bf16[96,320]{1,0:T(8,128)(2,1)S(1)}, u32[]{:S(2)}, u32[]{:S(2)}) collective-permute-start(bf16[96,320]{1,0:T(8,128)(2,1)S(1)} %slice.240), channel_id=1, source_target_pairs={{0,48},{12,60},{24,72},{36,84},{48,96},{60,108},{72,120},{84,132},... | collective-permute-start | bytes 184328 | tf_op jit(solution)/shard_map/ppermute | solution.py:38
  162.9 12.3 %collective-permute-start.8 = (bf16[96,320]{1,0:T(8,128)(2,1)S(1)}, bf16[96,320]{1,0:T(8,128)(2,1)S(1)}, u32[]{:S(2)}, u32[]{:S(2)}) collective-permute-start(bf16[96,320]{1,0:T(8,128)(2,1)S(1)} %pad_maximum_fusion.4), channel_id=1, source_target_pairs={{48,0},{60,12},{72,24},{84,36},{96,48},{108,60},{120,72},{132,84},... | collective-permute-start | bytes 184328 | tf_op jit(solution)/shard_map/ppermute | solution.py:38
  179.7 8.9 %copy-start.4 = (bf16[1,1,128,128]{3,2,1,0:T(8,128)(2,1)S(1)}, bf16[1,1,128,128]{3,2,1,0:T(8,128)(2,1)}, u32[]{:S(2)}) copy-start(bf16[1,1,128,128]{3,2,1,0:T(8,128)(2,1)} %param.17) | copy-start | bytes 98308

commit v6 on v5

--- a/solution.py
+++ b/solution.py
@@ -69,8 +69,10 @@
     y_now = dot(side_by_side(both[:, :n_exc, :width]), z_cols)
     left = both[:, :, width:]
 
-    kept = jnp.where(jnp.arange(rank) < rank_counts[layer], rank_scale[0], F32(0.0))
-    others = (jnp.arange(n_layers) != layer)[:, None, None]
+    ours = jnp.arange(n_layers) == layer
+    count = jnp.sum(jnp.where(ours, rank_counts, 0))
+    kept = jnp.where(jnp.arange(rank) < count, rank_scale[0], F32(0.0))
+    others = ~ours[:, None, None]
     z_outer = z_cols.reshape(n_q, width, width)[:, 2 * FACE_Q :]
     far_to_y = jnp.einsum("qrt,qtc->qrc", left, z_outer, preferred_element_type=F32)
     far_to_y = far_to_y.reshape(n_q * rank, width).astype(BF16)
@@ -98,8 +100,9 @@
             copies, own = lax.optimization_barrier((copies, coupling[0]))
             own = own.reshape(n_layers * rank, rank)
             across = from_other(own, "yl")
-            couple = [own, from_other(own, "core"), across, from_other(across, "core")]
-            couple = jnp.concatenate(couple, 1)
+            theirs = from_other(jnp.stack([own, across]), "core")
+            couple = jnp.concatenate([own, theirs[0], across, theirs[1]], 1)
+            couple = lax.optimization_barrier(couple)
         outer_out = outgoing[:, 2 * FACE_Q :]
         of_layers = lax.all_to_all(copies, SECOND, 0, 0, tiled=True)
         of_layers = of_layers.reshape(n_layers, n_zl, rows, rank)

time: 190 us -> 187 us (0.984)
  other arithmetic: 3.78 us -> 8.24 us
  matrix products: 12.4 us -> 8.56 us
  starting transfers between devices: 65.7 us -> 62.5 us
  waiting for transfers between devices: 50.8 us -> 48.6 us
    ppermute x6, waiting for transfers between devices: 26.8 us -> 21.6 us  [shifted(): lax.ppermute(value, SUB, [(s, s + steps) for s in range(first, last)])]
    dot_general x24, matrix products: 11.1 us -> 7.23 us  [dot(): return jnp.dot(a, b, preferred_element_type=F32)]
    ppermute x3 -> x2, starting transfers between devices: 8.7 us -> 5.8 us  [from_other(): return lax.ppermute(value, axis, [(0, 1), (1, 0)])]
  transfers between devices with their start and end apart: 14 -> 13, of which waited for: 10 -> 9; matrix products, arithmetic and copies ran while one was open for 2% -> 3% of each run, Pallas kernels for 0% -> 0%
where the time goes in v6:
time: 187 us; the launch traced here: 186 us
  starting transfers between devices  62.5 us (33%)
  blocking collectives  51.8 us (28%)
  waiting for transfers between devices  48.6 us (26%)
  matrix products  8.56 us (5%)
  other arithmetic  8.24 us (4%)
  local copies, waits for them, and re-layouts  5.79 us (3%)
    all_to_all x3, starting transfers between devices, per_device(): of_layers = lax.all_to_all(copies, SECOND, 0, 0, tiled=True)  33.1 us
    ppermute x6, waiting for transfers between devices, shifted(): lax.ppermute(value, SUB, [(s, s + steps) for s in range(first, last)])  21.6 us
    all_gather x2, blocking collectives, per_device(): both = lax.all_gather(both, QUARTER)  18.2 us
    all_gather x1, blocking collectives, per_device(): both = lax.all_gather(jnp.concatenate([both, left_basis], 1), QUARTER)  17.2 us
    ppermute x6, starting transfers between devices, shifted(): lax.ppermute(value, SUB, [(s, s + steps) for s in range(first, last)])  16.6 us
    all_to_all x3, waiting for transfers between devices, per_device(): of_layers = lax.all_to_all(copies, SECOND, 0, 0, tiled=True)  15.3 us
    all_to_all x2, waiting for transfers between devices, per_device(): arrived = lax.all_to_all(parts, FIRST, 0, 0, tiled=True)  11.8 us
    all_to_all x1, blocking collectives, per_device(): arrived = lax.all_to_all(parts, FIRST, 0, 0, tiled=True)  8.95 us
  transfers between devices with their start and end apart: 13, of which 9 were waited for; matrix products, arithmetic and copies ran while one was open for 3% of the time, Pallas kernels for 0%

profile of v6, /device:TPU:1, one launch (start us, length us, event | category | flops | bytes accessed | tf_op | source)
XLA Modules:
  0.0 186.0 jit_solution(10338751681953904777)
XLA Ops:
  0.0 0.9 fusion.54
  0.9 17.2 %all-gather = bf16[512,640]{1,0:T(8,128)(2,1)S(1)} all-gather(bf16[128,640]{1,0:T(8,128)(2,1)S(1)} %fusion.54), channel_id=2, replica_groups=mesh['zh'=4,'yh'=4,'yl'=2,'core'=2,'zl'=3,'x'=4] {'yl','core'}, dimensions={0}, use_global_device_ids=true | all-gather | bytes 819200 | tf_op jit(solution)/shard_map/all_gather | solution.py:68
  18.2 1.3 fusion.110
  19.6 1.3 fusion.111
  20.9 2.1 %fusion.18 = bf16[96,512]{1,0:T(8,128)(2,1)S(1)} fusion(bf16[1,1,2048,512]{3,2,1,0:T(8,128)(2,1)} %param.9, bf16[96,512]{1,0:T(8,128)(2,1)S(1)} %get-tuple-element.24, bf16[96,512]{1,0:T(8,128)(2,1)S(1)} %get-tuple-element.25, bf16[96,512]{1,0:T(8,128)(2,1)S(1)} %get-tuple-element.26, bf16[96,512]{1,0:T(8,128)(2,1)S(1)} %get-tuple-element.23), kind=kOutput, calls=%fused_computation.12 | convolution fusion | flops 202948608 | bytes 2588672 | tf_op jit(solution)/shard_map/dot_general | solution.py:19
  23.1 0.7 broadcast_in_dim.62
  23.7 3.5 %all-to-all-start = ((bf16[16,24,128]{2,1,0:T(8,128)(2,1)}), bf16[16,24,128]{2,1,0:T(8,128)(2,1)S(1)}, u32[]{:S(2)}, u32[]{:S(2)}) async-start(bf16[16,24,128]{2,1,0:T(8,128)(2,1)} %bitcast.11), calls=%async_computation | async-start | bytes 196608 | tf_op jit(solution)/shard_map/all_to_all | solution.py:95
  27.2 5.9 %all-to-all-done = bf16[16,24,128]{2,1,0:T(8,128)(2,1)S(1)} async-done(((bf16[16,24,128]{2,1,0:T(8,128)(2,1)}), bf16[16,24,128]{2,1,0:T(8,128)(2,1)S(1)}, u32[]{:S(2)}, u32[]{:S(2)}) %all-to-all-start) | async-done | bytes 98336 | tf_op jit(solution)/shard_map/all_to_all | solution.py:95
  33.1 0.8 broadcast_in_dim.63
  33.9 2.3 %collective-permute-start.2 = (bf16[2048,128]{1,0:T(8,128)(2,1)S(1)}, bf16[2048,128]{1,0:T(8,128)(2,1)S(1)}, u32[]{:S(2)}, u32[]{:S(2)}) collective-permute-start(bf16[2048,128]{1,0:T(8,128)(2,1)S(1)} %bitcast.151), channel_id=1, source_target_pairs={{0,24},{24,0},{1,25},{25,1},{2,26},{26,2},{3,27},{27,3},{4,28},{28... | collective-permute-start | bytes 1572872 | tf_op jit(solution)/shard_map/ppermute | solution.py:27
  36.3 1.3 convolution_convert_fusion
  37.7 13.7 %all-to-all-start.1 = ((bf16[48,24,128]{2,1,0:T(8,128)(2,1)}), bf16[48,24,128]{2,1,0:T(8,128)(2,1)S(1)}, u32[]{:S(2)}, u32[]{:S(2)}) async-start(bf16[48,24,128]{2,1,0:T(8,128)(2,1)} %broadcast_in_dim.63), calls=%async_computation.1 | async-start | bytes 589824 | tf_op jit(solution)/shard_map/all_to_all | solution.py:107
  51.5 1.3 collective-permute-start.1
  52.8 4.9 %collective-permute-start = (bf16[96,320]{1,0:T(8,128)(2,1)S(1)}, bf16[96,320]{1,0:T(8,128)(2,1)S(1)}, u32[]{:S(2)}, u32[]{:S(2)}) collective-permute-start(bf16[96,320]{1,0:T(8,128)(2,1)S(1)} %slice.207), channel_id=1, source_target_pairs={{0,48},{12,60},{24,72},{36,84},{48,96},{60,108},{72,120},{84,132},... | collective-permute-start | bytes 184328 | tf_op jit(solution)/shard_map/ppermute | solution.py:38
  57.9 1.2 pad_maximum_fusion.1
  59.1 3.5 %collective-permute-start.3 = (bf16[2,2048,128]{2,1,0:T(8,128)(2,1)}, bf16[2,2048,128]{2,1,0:T(8,128)(2,1)}, u32[]{:S(2)}, u32[]{:S(2)}) collective-permute-start(bf16[2,2048,128]{2,1,0:T(8,128)(2,1)} %pad_maximum_fusion.1), channel_id=1, source_target_pairs={{0,12},{12,0},{1,13},{13,1},{2,14},{14,2},{3,15},{15,3},{4,16},{16... | collective-permute-start | bytes 3145736 | tf_op jit(solution)/shard_map/ppermute | solution.py:27
  63.1 0.8 fusion.49
  63.9 7.6 %all-to-all-done.1 = bf16[48,24,128]{2,1,0:T(8,128)(2,1)S(1)} async-done(((bf16[48,24,128]{2,1,0:T(8,128)(2,1)}), bf16[48,24,128]{2,1,0:T(8,128)(2,1)S(1)}, u32[]{:S(2)}, u32[]{:S(2)}) %all-to-all-start.1) | async-done | bytes 294944 | tf_op jit(solution)/shard_map/all_to_all | solution.py:107
  71.5 1.3 slice_bitcast_fusion.1
  72.8 1.3 pad_maximum_fusion
  74.1 0.4 fusion.62
  74.6 0.4 copy-done.5
  75.0 9.6 %all-gather.1 = bf16[480,512]{1,0:T(8,128)(2,1)S(1)} all-gather(bf16[120,512]{1,0:T(8,128)(2,1)S(1)} %maximum_maximum_fusion), channel_id=3, replica_groups=mesh['zh'=4,'yh'=4,'yl'=2,'core'=2,'zl'=3,'x'=4] {'yl','core'}, dimensions={0}, use_global_device_ids=true | all-gather | bytes 614400 | tf_op jit(solution)/shard_map/all_gather | solution.py:123
  84.9 0.5 fusion.15
  85.5 8.9 %all_to_all.30 = bf16[16,24,128]{2,1,0:T(8,128)(2,1)S(1)} all-to-all(bf16[16,24,128]{2,1,0:T(8,128)(2,1)S(1)} %bitcast.165), channel_id=1, replica_groups=mesh['zh'=4,'yh'=4,'yl'=2,'core'=2,'zl'=3,'x'=4] {'yl','core','x'}, dimensions={0} | all-to-all | bytes 196608 | tf_op jit(solution)/shard_map/all_to_all | solution.py:95
  94.5 0.7 broadcast_in_dim.67
  95.5 10.1 %all-to-all-start.3 = ((bf16[48,24,128]{2,1,0:T(8,128)(2,1)}), bf16[48,24,128]{2,1,0:T(8,128)(2,1)S(1)}, u32[]{:S(2)}, u32[]{:S(2)}) async-start(bf16[48,24,128]{2,1,0:T(8,128)(2,1)} %broadcast_in_dim.67), calls=%async_computation.3 | async-start | bytes 589824 | tf_op jit(solution)/shard_map/all_to_all | solution.py:107
  105.6 3.9 %collective-permute-start.4 = (bf16[96,320]{1,0:T(8,128)(2,1)S(1)}, bf16[96,320]{1,0:T(8,128)(2,1)S(1)}, u32[]{:S(2)}, u32[]{:S(2)}) collective-permute-start(bf16[96,320]{1,0:T(8,128)(2,1)S(1)} %slice.231), channel_id=1, source_target_pairs={{0,48},{12,60},{24,72},{36,84},{48,96},{60,108},{72,120},{84,132},... | collective-permute-start | bytes 184328 | tf_op jit(solution)/shard_map/ppermute | solution.py:38
  109.6 1.3 collective-permute-start.5
  110.9 0.3 collective-permute-done.4
  111.4 10.6 %collective-permute-done.5 = bf16[96,320]{1,0:T(8,128)(2,1)S(1)} collective-permute-done((bf16[96,320]{1,0:T(8,128)(2,1)S(1)}, bf16[96,320]{1,0:T(8,128)(2,1)S(1)}, u32[]{:S(2)}, u32[]{:S(2)}) %collective-permute-start.5) | collective-permute-done | bytes 61472 | tf_op jit(solution)/shard_map/ppermute | solution.py:38
  122.5 3.8 %all-to-all-done.3 = bf16[48,24,128]{2,1,0:T(8,128)(2,1)S(1)} async-done(((bf16[48,24,128]{2,1,0:T(8,128)(2,1)}), bf16[48,24,128]{2,1,0:T(8,128)(2,1)S(1)}, u32[]{:S(2)}, u32[]{:S(2)}) %all-to-all-start.3) | async-done | bytes 294944 | tf_op jit(solution)/shard_map/all_to_all | solution.py:107
  126.3 0.4 fusion.59
  126.8 8.6 %all-gather.2 = bf16[480,512]{1,0:T(8,128)(2,1)S(1)} all-gather(bf16[120,512]{1,0:T(8,128)(2,1)S(1)} %maximum_maximum_fusion.1), channel_id=4, replica_groups=mesh['zh'=4,'yh'=4,'yl'=2,'core'=2,'zl'=3,'x'=4] {'yl','core'}, dimensions={0}, use_global_device_ids=true | all-gather | bytes 614400 | tf_op jit(solution)/shard_map/all_gather | solution.py:123
  135.7 0.5 fusion.12
  136.3 0.7 broadcast_in_dim.69
  137.0 3.5 %all-to-all-start.4 = ((bf16[16,24,128]{2,1,0:T(8,128)(2,1)}), bf16[16,24,128]{2,1,0:T(8,128)(2,1)S(1)}, u32[]{:S(2)}, u32[]{:S(2)}) async-start(bf16[16,24,128]{2,1,0:T(8,128)(2,1)} %bitcast.43), calls=%async_computation.4 | async-start | bytes 196608 | tf_op jit(solution)/shard_map/all_to_all | solution.py:95
  140.4 5.9 %all-to-all-done.4 = bf16[16,24,128]{2,1,0:T(8,128)(2,1)S(1)} async-done(((bf16[16,24,128]{2,1,0:T(8,128)(2,1)}), bf16[16,24,128]{2,1,0:T(8,128)(2,1)S(1)}, u32[]{:S(2)}, u32[]{:S(2)}) %all-to-all-start.4) | async-done | bytes 98336 | tf_op jit(solution)/shard_map/all_to_all | solution.py:95
  146.3 0.7 broadcast_in_dim.70
  147.3 9.3 %all-to-all-start.5 = ((bf16[48,24,128]{2,1,0:T(8,128)(2,1)}), bf16[48,24,128]{2,1,0:T(8,128)(2,1)S(1)}, u32[]{:S(2)}, u32[]{:S(2)}) async-start(bf16[48,24,128]{2,1,0:T(8,128)(2,1)} %broadcast_in_dim.70), calls=%async_computation.5 | async-start | bytes 589824 | tf_op jit(solution)/shard_map/all_to_all | solution.py:107
  156.7 3.9 %collective-permute-start.6 = (bf16[96,320]{1,0:T(8,128)(2,1)S(1)}, bf16[96,320]{1,0:T(8,128)(2,1)S(1)}, u32[]{:S(2)}, u32[]{:S(2)}) collective-permute-start(bf16[96,320]{1,0:T(8,128)(2,1)S(1)} %slice.248), channel_id=1, source_target_pairs={{0,48},{12,60},{24,72},{36,84},{48,96},{60,108},{72,120},{84,132},... | collective-permute-start | bytes 184328 | tf_op jit(solution)/shard_map/ppermute | solution.py:38
  160.7 1.3 collective-permute-start.7
  162.0 0.3 collective-permute-done.6
  162.6 10.4 %collective-permute-done.7 = bf16[96,320]{1,0:T(8,128)(2,1)S(1)} collective-permute-done((bf16[96,320]{1,0:T(8,128)(2,1)S(1)}, bf16[96,320]{1,0:T(8,128)(2,1)S(1)}, u32[]{:S(2)}, u32[]{:S(2)}) %collective-permute-start.7) | collective-permute-done | bytes 61472 | tf_op jit(solution)/shard_map/ppermute | solution.py:38
  173.3 4.0 %all-to-all-done.5 = bf16[48,24,128]{2,1,0:T(8,128)(2,1)S(1)} async-done(((bf16[48,24,128]{2,1,0:T(8,128)(2,1)}), bf16[48,24,128]{2,1,0:T(8,128)(2,1)S(1)}, u32[]{:S(2)}, u32[]{:S(2)}) %all-to-all-start.5) | async-done | bytes 294944 | tf_op jit(solution)/shard_map/all_to_all | solution.py:107
  177.4 0.4 fusion.56
  177.8 7.4 %all_gather.28 = bf16[4,24,512]{2,1,0:T(8,128)(2,1)S(1)} all-gather(bf16[1,24,512]{2,1,0:T(8,128)(2,1)S(1)} %pad_maximum_fusion.6), channel_id=1, replica_groups=mesh['zh'=4,'yh'=4,'yl'=2,'core'=2,'zl'=3,'x'=4] {'yl','core'}, dimensions={0}, use_global_device_ids=true | all-gather | bytes 122880 | tf_op jit(solution)/shard_map/all_gather | solution.py:127
  185.4 0.7 pad_maximum_fusion.2
  (78 shorter events, 4.3 us)
Async XLA Ops:
  0.0 22.9 %copy-start = (bf16[1,1,128,128]{3,2,1,0:T(8,128)(2,1)S(1)}, bf16[1,1,128,128]{3,2,1,0:T(8,128)(2,1)}, u32[]{:S(2)}) copy-start(bf16[1,1,128,128]{3,2,1,0:T(8,128)(2,1)} %param.13) | copy-start | bytes 98308
  18.2 15.7 %copy-start.1 = (bf16[1,16,128,128]{3,2,1,0:T(8,128)(2,1)S(1)}, bf16[1,16,128,128]{3,2,1,0:T(8,128)(2,1)}, u32[]{:S(2)}) copy-start(bf16[1,16,128,128]{3,2,1,0:T(8,128)(2,1)} %param.16) | copy-start | bytes 1572868
  22.9 34.8 %copy-start.4 = (bf16[1,1,3,128,128]{4,3,2,1,0:T(8,128)(2,1)S(1)}, bf16[1,1,3,128,128]{4,3,2,1,0:T(8,128)(2,1)}, u32[]{:S(2)}) copy-start(bf16[1,1,3,128,128]{4,3,2,1,0:T(8,128)(2,1)} %param.12) | copy-start | bytes 294916
  23.7 9.4 %all-to-all-start = ((bf16[16,24,128]{2,1,0:T(8,128)(2,1)}), bf16[16,24,128]{2,1,0:T(8,128)(2,1)S(1)}, u32[]{:S(2)}, u32[]{:S(2)}) async-start(bf16[16,24,128]{2,1,0:T(8,128)(2,1)} %bitcast.11), calls=%async_computation | async-start | bytes 196608 | tf_op jit(solution)/shard_map/all_to_all | solution.py:95
  33.9 24.0 %collective-permute-start.2 = (bf16[2048,128]{1,0:T(8,128)(2,1)S(1)}, bf16[2048,128]{1,0:T(8,128)(2,1)S(1)}, u32[]{:S(2)}, u32[]{:S(2)}) collective-permute-start(bf16[2048,128]{1,0:T(8,128)(2,1)S(1)} %bitcast.151), channel_id=1, source_target_pairs={{0,24},{24,0},{1,25},{25,1},{2,26},{26,2},{3,27},{27,3},{4,28},{28... | collective-permute-start | bytes 1572872 | tf_op jit(solution)/shard_map/ppermute | solution.py:27
  36.3 26.3 %copy-start.9 = (s32[1,1,192]{2,1,0:T(1,128)S(1)}, s32[1,1,192]{2,1,0:T(1,128)}, u32[]{:S(2)}) copy-start(s32[1,1,192]{2,1,0:T(1,128)} %param.11) | copy-start | bytes 2308
  37.6 25.5 %copy-start.3 = (bf16[1,1,96,512]{3,2,1,0:T(8,128)(2,1)S(1)}, bf16[1,1,96,512]{3,2,1,0:T(8,128)(2,1)}, u32[]{:S(2)}) copy-start(bf16[1,1,96,512]{3,2,1,0:T(8,128)(2,1)} %param.10) | copy-start | bytes 294916
  37.7 33.7 %all-to-all-start.1 = ((bf16[48,24,128]{2,1,0:T(8,128)(2,1)}), bf16[48,24,128]{2,1,0:T(8,128)(2,1)S(1)}, u32[]{:S(2)}, u32[]{:S(2)}) async-start(bf16[48,24,128]{2,1,0:T(8,128)(2,1)} %broadcast_in_dim.63), calls=%async_computation.1 | async-start | bytes 589824 | tf_op jit(solution)/shard_map/all_to_all | solution.py:107
  51.5 11.2 %collective-permute-start.1 = (bf16[96,320]{1,0:T(8,128)(2,1)S(1)}, bf16[96,320]{1,0:T(8,128)(2,1)S(1)}, u32[]{:S(2)}, u32[]{:S(2)}) collective-permute-start(bf16[96,320]{1,0:T(8,128)(2,1)S(1)} %pad_maximum_fusion.3), channel_id=1, source_target_pairs={{48,0},{60,12},{72,24},{84,36},{96,48},{108,60},{120,72},{132,84},... | collective-permute-start | bytes 184328 | tf_op jit(solution)/shard_map/ppermute | solution.py:38
  52.8 9.7 %collective-permute-start = (bf16[96,320]{1,0:T(8,128)(2,1)S(1)}, bf16[96,320]{1,0:T(8,128)(2,1)S(1)}, u32[]{:S(2)}, u32[]{:S(2)}) collective-permute-start(bf16[96,320]{1,0:T(8,128)(2,1)S(1)} %slice.207), channel_id=1, source_target_pairs={{0,48},{12,60},{24,72},{36,84},{48,96},{60,108},{72,120},{84,132},... | collective-permute-start | bytes 184328 | tf_op jit(solution)/shard_map/ppermute | solution.py:38
  57.9 15.0 %copy-start.2 = (bf16[2048,128]{1,0:T(8,128)(2,1)}, bf16[2048,128]{1,0:T(8,128)(2,1)S(1)}, u32[]{:S(2)}) copy-start(bf16[2048,128]{1,0:T(8,128)(2,1)S(1)} %collective-permute-done.2) | copy-start | bytes 1572868
  59.1 12.5 %collective-permute-start.3 = (bf16[2,2048,128]{2,1,0:T(8,128)(2,1)}, bf16[2,2048,128]{2,1,0:T(8,128)(2,1)}, u32[]{:S(2)}, u32[]{:S(2)}) collective-permute-start(bf16[2,2048,128]{2,1,0:T(8,128)(2,1)} %pad_maximum_fusion.1), channel_id=1, source_target_pairs={{0,12},{12,0},{1,13},{13,1},{2,14},{14,2},{3,15},{15,3},{4,16},{16... | collective-permute-start | bytes 3145736 | tf_op jit(solution)/shard_map/ppermute | solution.py:27
  74.1 0.9 copy-start.5
  74.1 10.8 %copy-start.6 = (bf16[1,1,2048,512]{3,2,1,0:T(8,128)(2,1)S(1)}, bf16[1,1,2048,512]{3,2,1,0:T(8,128)(2,1)}, u32[]{:S(2)}) copy-start(bf16[1,1,2048,512]{3,2,1,0:T(8,128)(2,1)} %param.9) | copy-start | bytes 6291460
  95.5 30.8 %all-to-all-start.3 = ((bf16[48,24,128]{2,1,0:T(8,128)(2,1)}), bf16[48,24,128]{2,1,0:T(8,128)(2,1)S(1)}, u32[]{:S(2)}, u32[]{:S(2)}) async-start(bf16[48,24,128]{2,1,0:T(8,128)(2,1)} %broadcast_in_dim.67), calls=%async_computation.3 | async-start | bytes 589824 | tf_op jit(solution)/shard_map/all_to_all | solution.py:107
  105.6 5.6 %collective-permute-start.4 = (bf16[96,320]{1,0:T(8,128)(2,1)S(1)}, bf16[96,320]{1,0:T(8,128)(2,1)S(1)}, u32[]{:S(2)}, u32[]{:S(2)}) collective-permute-start(bf16[96,320]{1,0:T(8,128)(2,1)S(1)} %slice.231), channel_id=1, source_target_pairs={{0,48},{12,60},{24,72},{36,84},{48,96},{60,108},{72,120},{84,132},... | collective-permute-start | bytes 184328 | tf_op jit(solution)/shard_map/ppermute | solution.py:38
  109.6 12.3 %collective-permute-start.5 = (bf16[96,320]{1,0:T(8,128)(2,1)S(1)}, bf16[96,320]{1,0:T(8,128)(2,1)S(1)}, u32[]{:S(2)}, u32[]{:S(2)}) collective-permute-start(bf16[96,320]{1,0:T(8,128)(2,1)S(1)} %pad_maximum_fusion.4), channel_id=1, source_target_pairs={{48,0},{60,12},{72,24},{84,36},{96,48},{108,60},{120,72},{132,84},... | collective-permute-start | bytes 184328 | tf_op jit(solution)/shard_map/ppermute | solution.py:38
  126.3 9.4 %copy-start.7 = (bf16[1,1,2048,512]{3,2,1,0:T(8,128)(2,1)S(1)}, bf16[1,1,2048,512]{3,2,1,0:T(8,128)(2,1)}, u32[]{:S(2)}) copy-start(bf16[1,1,2048,512]{3,2,1,0:T(8,128)(2,1)} %param.9) | copy-start | bytes 6291460
  137.0 9.3 %all-to-all-start.4 = ((bf16[16,24,128]{2,1,0:T(8,128)(2,1)}), bf16[16,24,128]{2,1,0:T(8,128)(2,1)S(1)}, u32[]{:S(2)}, u32[]{:S(2)}) async-start(bf16[16,24,128]{2,1,0:T(8,128)(2,1)} %bitcast.43), calls=%async_computation.4 | async-start | bytes 196608 | tf_op jit(solution)/shard_map/all_to_all | solution.py:95
  147.3 30.0 %all-to-all-start.5 = ((bf16[48,24,128]{2,1,0:T(8,128)(2,1)}), bf16[48,24,128]{2,1,0:T(8,128)(2,1)S(1)}, u32[]{:S(2)}, u32[]{:S(2)}) async-start(bf16[48,24,128]{2,1,0:T(8,128)(2,1)} %broadcast_in_dim.70), calls=%async_computation.5 | async-start | bytes 589824 | tf_op jit(solution)/shard_map/all_to_all | solution.py:107
  156.7 5.6 %collective-permute-start.6 = (bf16[96,320]{1,0:T(8,128)(2,1)S(1)}, bf16[96,320]{1,0:T(8,128)(2,1)S(1)}, u32[]{:S(2)}, u32[]{:S(2)}) collective-permute-start(bf16[96,320]{1,0:T(8,128)(2,1)S(1)} %slice.248), channel_id=1, source_target_pairs={{0,48},{12,60},{24,72},{36,84},{48,96},{60,108},{72,120},{84,132},... | collective-permute-start | bytes 184328 | tf_op jit(solution)/shard_map/ppermute | solution.py:38
  160.7 24.6 %copy-start.8 = (bf16[1,1,128,128]{3,2,1,0:T(8,128)(2,1)S(1)}, bf16[1,1,128,128]{3,2,1,0:T(8,128)(2,1)}, u32[]{:S(2)}) copy-start(bf16[1,1,128,128]{3,2,1,0:T(8,128)(2,1)} %param.17) | copy-start | bytes 98308
  160.7 12.3 %collective-permute-start.7 = (bf16[96,320]{1,0:T(8,128)(2,1)S(1)}, bf16[96,320]{1,0:T(8,128)(2,1)S(1)}, u32[]{:S(2)}, u32[]{:S(2)}) collective-permute-start(bf16[96,320]{1,0:T(8,128)(2,1)S(1)} %pad_maximum_fusion.5), channel_id=1, source_target_pairs={{48,0},{60,12},{72,24},{84,36},{96,48},{108,60},{120,72},{132,84},... | collective-permute-start | bytes 184328 | tf_op jit(solution)/shard_map/ppermute | solution.py:38

commit v7 on v6

--- a/solution.py
+++ b/solution.py
@@ -71,7 +71,7 @@
 
     ours = jnp.arange(n_layers) == layer
     count = jnp.sum(jnp.where(ours, rank_counts, 0))
-    kept = jnp.where(jnp.arange(rank) < count, rank_scale[0], F32(0.0))
+    kept = jnp.arange(rank) < count
     others = ~ours[:, None, None]
     z_outer = z_cols.reshape(n_q, width, width)[:, 2 * FACE_Q :]
     far_to_y = jnp.einsum("qrt,qtc->qrc", left, z_outer, preferred_element_type=F32)
@@ -88,20 +88,22 @@
     for sweep in range(ITERS):
         outgoing = y_now.astype(BF16)
         outer_out = outgoing[:, 2 * FACE_Q :]
-        partial = (dot(outer_out, right_basis) * kept).astype(BF16)
+        partial = (dot(outer_out, right_basis) * rank_scale).astype(BF16)
         parts = jnp.broadcast_to(
             partial.reshape(n_q, 1, rows, rank), (n_q, n_x, rows, rank)
         ).reshape(n_q * n_x, rows, rank)
         arrived = lax.all_to_all(parts, FIRST, 0, 0, tiled=True)
-        coefs = arrived.astype(F32).sum(0).astype(BF16)
+        coefs = jnp.where(kept, arrived.astype(F32).sum(0), F32(0.0)).astype(BF16)
+        if sweep == 0:
+            coefs, far_to_y = lax.optimization_barrier((coefs, far_to_y))
         copies = jnp.broadcast_to(coefs, (n_layers * n_zl, rows, rank))
         copies, outgoing = lax.optimization_barrier((copies, outgoing))
         if sweep == 0:
             copies, own = lax.optimization_barrier((copies, coupling[0]))
             own = own.reshape(n_layers * rank, rank)
             across = from_other(own, "yl")
-            theirs = from_other(jnp.stack([own, across]), "core")
-            couple = jnp.concatenate([own, theirs[0], across, theirs[1]], 1)
+            chips = jnp.concatenate([own, across], 1)
+            couple = jnp.concatenate([chips, from_other(chips, "core")], 1)
             couple = lax.optimization_barrier(couple)
         outer_out = outgoing[:, 2 * FACE_Q :]
         of_layers = lax.all_to_all(copies, SECOND, 0, 0, tiled=True)
@@ -116,7 +118,7 @@
         outer_in = outer_in + dot(above[:, FACE_Q:], tiles[2])
         near = jnp.concatenate([lower_in, lower_above, outer_in], 1) + source.astype(F32)
         far = dot(of_layers.transpose(1, 0, 2).reshape(rows, -1), couple)
-        far = [far[:, k * rank : (k + 1) * rank] for k in range(n_q)]
+        far = [far[:, k * rank : (k + 1) * rank] for k in (0, 2, 1, 3)]
         far = jnp.concatenate(by_quarter(far), 1).astype(BF16)
         if sweep < ITERS - 1:
             both = jnp.concatenate([near.astype(BF16), far], 0)

time: 187 us -> 182 us (0.973)
  other arithmetic: 8.24 us -> 6.12 us
    all_to_all x2, waiting for transfers between devices: 11.8 us -> 9.09 us  [per_device(): arrived = lax.all_to_all(parts, FIRST, 0, 0, tiled=True)]
where the time goes in v7:
time: 182 us; the launch traced here: 181 us
  starting transfers between devices  62.5 us (34%)
  blocking collectives  51.8 us (28%)
  waiting for transfers between devices  47 us (26%)
  matrix products  8.61 us (5%)
  other arithmetic  6.12 us (3%)
  local copies, waits for them, and re-layouts  4.49 us (2%)
    all_to_all x3, starting transfers between devices, per_device(): of_layers = lax.all_to_all(copies, SECOND, 0, 0, tiled=True)  33.1 us
    ppermute x6, waiting for transfers between devices, shifted(): lax.ppermute(value, SUB, [(s, s + steps) for s in range(first, last)])  21.6 us
    all_gather x2, blocking collectives, per_device(): both = lax.all_gather(both, QUARTER)  18.2 us
    all_gather x1, blocking collectives, per_device(): both = lax.all_gather(jnp.concatenate([both, left_basis], 1), QUARTER)  17.2 us
    ppermute x6, starting transfers between devices, shifted(): lax.ppermute(value, SUB, [(s, s + steps) for s in range(first, last)])  16.6 us
    all_to_all x3, waiting for transfers between devices, per_device(): of_layers = lax.all_to_all(copies, SECOND, 0, 0, tiled=True)  16.4 us
    all_to_all x2, waiting for transfers between devices, per_device(): arrived = lax.all_to_all(parts, FIRST, 0, 0, tiled=True)  9.09 us
    all_to_all x1, blocking collectives, per_device(): arrived = lax.all_to_all(parts, FIRST, 0, 0, tiled=True)  8.94 us
  transfers between devices with their start and end apart: 13, of which 9 were waited for; matrix products, arithmetic and copies ran while one was open for 3% of the time, Pallas kernels for 0%

profile of v7, /device:TPU:1, one launch (start us, length us, event | category | flops | bytes accessed | tf_op | source)
XLA Modules:
  0.0 181.1 jit_solution(4272741841019312134)
XLA Ops:
  0.0 0.9 fusion.54
  0.9 17.2 %all-gather = bf16[512,640]{1,0:T(8,128)(2,1)S(1)} all-gather(bf16[128,640]{1,0:T(8,128)(2,1)S(1)} %fusion.54), channel_id=2, replica_groups=mesh['zh'=4,'yh'=4,'yl'=2,'core'=2,'zl'=3,'x'=4] {'yl','core'}, dimensions={0}, use_global_device_ids=true | all-gather | bytes 819200 | tf_op jit(solution)/shard_map/all_gather | solution.py:68
  18.2 2.1 %fusion.18 = bf16[96,512]{1,0:T(8,128)(2,1)S(1)} fusion(bf16[1,1,2048,512]{3,2,1,0:T(8,128)(2,1)} %param.9, bf16[96,512]{1,0:T(8,128)(2,1)S(1)} %get-tuple-element.26, bf16[96,512]{1,0:T(8,128)(2,1)S(1)} %get-tuple-element.27, bf16[96,512]{1,0:T(8,128)(2,1)S(1)} %get-tuple-element.28, bf16[96,512]{1,0:T(8,128)(2,1)S(1)} %get-tuple-element.25), kind=kOutput, calls=%fused_computation.12 | convolution fusion | flops 202948608 | bytes 2588672 | tf_op jit(solution)/shard_map/dot_general | solution.py:19
  20.5 0.7 broadcast_in_dim.67
  21.1 3.5 %all-to-all-start = ((bf16[16,24,128]{2,1,0:T(8,128)(2,1)}), bf16[16,24,128]{2,1,0:T(8,128)(2,1)S(1)}, u32[]{:S(2)}, u32[]{:S(2)}) async-start(bf16[16,24,128]{2,1,0:T(8,128)(2,1)} %bitcast.11), calls=%async_computation | async-start | bytes 196608 | tf_op jit(solution)/shard_map/all_to_all | solution.py:95
  24.6 0.7 fusion.110
  25.3 0.6 iota_compare_fusion.5
  26.0 1.3 convolution_convert_fusion
  27.3 3.2 %all-to-all-done = bf16[16,24,128]{2,1,0:T(8,128)(2,1)S(1)} async-done(((bf16[16,24,128]{2,1,0:T(8,128)(2,1)}), bf16[16,24,128]{2,1,0:T(8,128)(2,1)S(1)}, u32[]{:S(2)}, u32[]{:S(2)}) %all-to-all-start) | async-done | bytes 98336 | tf_op jit(solution)/shard_map/all_to_all | solution.py:95
  30.6 0.8 broadcast_in_dim.69
  31.3 2.3 %collective-permute-start.2 = (bf16[2048,128]{1,0:T(8,128)(2,1)S(1)}, bf16[2048,128]{1,0:T(8,128)(2,1)S(1)}, u32[]{:S(2)}, u32[]{:S(2)}) collective-permute-start(bf16[2048,128]{1,0:T(8,128)(2,1)S(1)} %bitcast.144), channel_id=1, source_target_pairs={{0,24},{24,0},{1,25},{25,1},{2,26},{26,2},{3,27},{27,3},{4,28},{28... | collective-permute-start | bytes 1572872 | tf_op jit(solution)/shard_map/ppermute | solution.py:27
  33.8 13.7 %all-to-all-start.1 = ((bf16[48,24,128]{2,1,0:T(8,128)(2,1)}), bf16[48,24,128]{2,1,0:T(8,128)(2,1)S(1)}, u32[]{:S(2)}, u32[]{:S(2)}) async-start(bf16[48,24,128]{2,1,0:T(8,128)(2,1)} %broadcast_in_dim.69), calls=%async_computation.1 | async-start | bytes 589824 | tf_op jit(solution)/shard_map/all_to_all | solution.py:109
  47.6 1.3 collective-permute-start.1
  48.9 4.9 %collective-permute-start = (bf16[96,320]{1,0:T(8,128)(2,1)S(1)}, bf16[96,320]{1,0:T(8,128)(2,1)S(1)}, u32[]{:S(2)}, u32[]{:S(2)}) collective-permute-start(bf16[96,320]{1,0:T(8,128)(2,1)S(1)} %slice.203), channel_id=1, source_target_pairs={{0,48},{12,60},{24,72},{36,84},{48,96},{60,108},{72,120},{84,132},... | collective-permute-start | bytes 184328 | tf_op jit(solution)/shard_map/ppermute | solution.py:38
  54.1 3.5 %collective-permute-start.3 = (bf16[2048,256]{1,0:T(8,128)(2,1)S(1)}, bf16[2048,256]{1,0:T(8,128)(2,1)}, u32[]{:S(2)}, u32[]{:S(2)}) collective-permute-start(bf16[2048,256]{1,0:T(8,128)(2,1)S(1)} %pad_maximum_fusion.1), channel_id=1, source_target_pairs={{0,12},{12,0},{1,13},{13,1},{2,14},{14,2},{3,15},{15,3},{4,16},{16... | collective-permute-start | bytes 3145736 | tf_op jit(solution)/shard_map/ppermute | solution.py:27
  58.2 0.8 fusion.49
  58.9 8.6 %all-to-all-done.1 = bf16[48,24,128]{2,1,0:T(8,128)(2,1)S(1)} async-done(((bf16[48,24,128]{2,1,0:T(8,128)(2,1)}), bf16[48,24,128]{2,1,0:T(8,128)(2,1)S(1)}, u32[]{:S(2)}, u32[]{:S(2)}) %all-to-all-start.1) | async-done | bytes 294944 | tf_op jit(solution)/shard_map/all_to_all | solution.py:109
  67.6 1.5 pad_maximum_fusion
  69.2 0.4 fusion.62
  69.6 0.4 copy-done.5
  70.1 9.6 %all-gather.1 = bf16[480,512]{1,0:T(8,128)(2,1)S(1)} all-gather(bf16[120,512]{1,0:T(8,128)(2,1)S(1)} %maximum_maximum_fusion), channel_id=3, replica_groups=mesh['zh'=4,'yh'=4,'yl'=2,'core'=2,'zl'=3,'x'=4] {'yl','core'}, dimensions={0}, use_global_device_ids=true | all-gather | bytes 614400 | tf_op jit(solution)/shard_map/all_gather | solution.py:125
  79.7 0.2 fusion.119
  80.0 0.5 fusion.15
  80.6 8.9 %all_to_all.30 = bf16[16,24,128]{2,1,0:T(8,128)(2,1)S(1)} all-to-all(bf16[16,24,128]{2,1,0:T(8,128)(2,1)S(1)} %bitcast.157), channel_id=1, replica_groups=mesh['zh'=4,'yh'=4,'yl'=2,'core'=2,'zl'=3,'x'=4] {'yl','core','x'}, dimensions={0} | all-to-all | bytes 196608 | tf_op jit(solution)/shard_map/all_to_all | solution.py:95
  89.6 0.7 broadcast_in_dim.73
  90.6 10.1 %all-to-all-start.3 = ((bf16[48,24,128]{2,1,0:T(8,128)(2,1)}), bf16[48,24,128]{2,1,0:T(8,128)(2,1)S(1)}, u32[]{:S(2)}, u32[]{:S(2)}) async-start(bf16[48,24,128]{2,1,0:T(8,128)(2,1)} %broadcast_in_dim.73), calls=%async_computation.3 | async-start | bytes 589824 | tf_op jit(solution)/shard_map/all_to_all | solution.py:109
  100.7 3.9 %collective-permute-start.4 = (bf16[96,320]{1,0:T(8,128)(2,1)S(1)}, bf16[96,320]{1,0:T(8,128)(2,1)S(1)}, u32[]{:S(2)}, u32[]{:S(2)}) collective-permute-start(bf16[96,320]{1,0:T(8,128)(2,1)S(1)} %slice.223), channel_id=1, source_target_pairs={{0,48},{12,60},{24,72},{36,84},{48,96},{60,108},{72,120},{84,132},... | collective-permute-start | bytes 184328 | tf_op jit(solution)/shard_map/ppermute | solution.py:38
  104.7 1.3 collective-permute-start.5
  106.0 0.3 collective-permute-done.4
  106.4 10.6 %collective-permute-done.5 = bf16[96,320]{1,0:T(8,128)(2,1)S(1)} collective-permute-done((bf16[96,320]{1,0:T(8,128)(2,1)S(1)}, bf16[96,320]{1,0:T(8,128)(2,1)S(1)}, u32[]{:S(2)}, u32[]{:S(2)}) %collective-permute-start.5) | collective-permute-done | bytes 61472 | tf_op jit(solution)/shard_map/ppermute | solution.py:38
  117.5 3.8 %all-to-all-done.3 = bf16[48,24,128]{2,1,0:T(8,128)(2,1)S(1)} async-done(((bf16[48,24,128]{2,1,0:T(8,128)(2,1)}), bf16[48,24,128]{2,1,0:T(8,128)(2,1)S(1)}, u32[]{:S(2)}, u32[]{:S(2)}) %all-to-all-start.3) | async-done | bytes 294944 | tf_op jit(solution)/shard_map/all_to_all | solution.py:109
  121.4 0.4 fusion.59
  121.8 8.6 %all-gather.2 = bf16[480,512]{1,0:T(8,128)(2,1)S(1)} all-gather(bf16[120,512]{1,0:T(8,128)(2,1)S(1)} %maximum_maximum_fusion.1), channel_id=4, replica_groups=mesh['zh'=4,'yh'=4,'yl'=2,'core'=2,'zl'=3,'x'=4] {'yl','core'}, dimensions={0}, use_global_device_ids=true | all-gather | bytes 614400 | tf_op jit(solution)/shard_map/all_gather | solution.py:125
  130.5 0.2 fusion.120
  130.8 0.5 fusion.12
  131.4 0.7 broadcast_in_dim.75
  132.0 3.5 %all-to-all-start.4 = ((bf16[16,24,128]{2,1,0:T(8,128)(2,1)}), bf16[16,24,128]{2,1,0:T(8,128)(2,1)S(1)}, u32[]{:S(2)}, u32[]{:S(2)}) async-start(bf16[16,24,128]{2,1,0:T(8,128)(2,1)} %bitcast.39), calls=%async_computation.4 | async-start | bytes 196608 | tf_op jit(solution)/shard_map/all_to_all | solution.py:95
  135.5 5.9 %all-to-all-done.4 = bf16[16,24,128]{2,1,0:T(8,128)(2,1)S(1)} async-done(((bf16[16,24,128]{2,1,0:T(8,128)(2,1)}), bf16[16,24,128]{2,1,0:T(8,128)(2,1)S(1)}, u32[]{:S(2)}, u32[]{:S(2)}) %all-to-all-start.4) | async-done | bytes 98336 | tf_op jit(solution)/shard_map/all_to_all | solution.py:95
  141.4 0.7 broadcast_in_dim.76
  142.4 9.3 %all-to-all-start.5 = ((bf16[48,24,128]{2,1,0:T(8,128)(2,1)}), bf16[48,24,128]{2,1,0:T(8,128)(2,1)S(1)}, u32[]{:S(2)}, u32[]{:S(2)}) async-start(bf16[48,24,128]{2,1,0:T(8,128)(2,1)} %broadcast_in_dim.76), calls=%async_computation.5 | async-start | bytes 589824 | tf_op jit(solution)/shard_map/all_to_all | solution.py:109
  151.7 3.9 %collective-permute-start.6 = (bf16[96,320]{1,0:T(8,128)(2,1)S(1)}, bf16[96,320]{1,0:T(8,128)(2,1)S(1)}, u32[]{:S(2)}, u32[]{:S(2)}) collective-permute-start(bf16[96,320]{1,0:T(8,128)(2,1)S(1)} %slice.240), channel_id=1, source_target_pairs={{0,48},{12,60},{24,72},{36,84},{48,96},{60,108},{72,120},{84,132},... | collective-permute-start | bytes 184328 | tf_op jit(solution)/shard_map/ppermute | solution.py:38
  155.8 1.3 collective-permute-start.7
  157.1 0.3 collective-permute-done.6
  157.7 10.4 %collective-permute-done.7 = bf16[96,320]{1,0:T(8,128)(2,1)S(1)} collective-permute-done((bf16[96,320]{1,0:T(8,128)(2,1)S(1)}, bf16[96,320]{1,0:T(8,128)(2,1)S(1)}, u32[]{:S(2)}, u32[]{:S(2)}) %collective-permute-start.7) | collective-permute-done | bytes 61472 | tf_op jit(solution)/shard_map/ppermute | solution.py:38
  168.4 4.0 %all-to-all-done.5 = bf16[48,24,128]{2,1,0:T(8,128)(2,1)S(1)} async-done(((bf16[48,24,128]{2,1,0:T(8,128)(2,1)}), bf16[48,24,128]{2,1,0:T(8,128)(2,1)S(1)}, u32[]{:S(2)}, u32[]{:S(2)}) %all-to-all-start.5) | async-done | bytes 294944 | tf_op jit(solution)/shard_map/all_to_all | solution.py:109
  172.4 0.4 fusion.56
  172.9 7.4 %all_gather.28 = bf16[4,24,512]{2,1,0:T(8,128)(2,1)S(1)} all-gather(bf16[1,24,512]{2,1,0:T(8,128)(2,1)S(1)} %pad_maximum_fusion.6), channel_id=1, replica_groups=mesh['zh'=4,'yh'=4,'yl'=2,'core'=2,'zl'=3,'x'=4] {'yl','core'}, dimensions={0}, use_global_device_ids=true | all-gather | bytes 122880 | tf_op jit(solution)/shard_map/all_gather | solution.py:129
  180.4 0.7 pad_maximum_fusion.2
  (84 shorter events, 4.0 us)
Async XLA Ops:
  0.0 20.3 %copy-start = (bf16[1,1,128,128]{3,2,1,0:T(8,128)(2,1)S(1)}, bf16[1,1,128,128]{3,2,1,0:T(8,128)(2,1)}, u32[]{:S(2)}) copy-start(bf16[1,1,128,128]{3,2,1,0:T(8,128)(2,1)} %param.13) | copy-start | bytes 98308
  18.1 2.2 %copy-start.10 = (f32[1,128]{1,0:T(1,128)S(1)}, f32[1,128]{1,0:T(1,128)}, u32[]{:S(2)}) copy-start(f32[1,128]{1,0:T(1,128)} %param.14) | copy-start | bytes 1540
  18.2 6.5 %copy-start.11 = (s32[16]{0:T(128)S(1)}, s32[16]{0:T(128)}, u32[]{:S(2)}) copy-start(s32[16]{0:T(128)} %param.15) | copy-start | bytes 196
  18.2 13.1 %copy-start.1 = (bf16[1,16,128,128]{3,2,1,0:T(8,128)(2,1)S(1)}, bf16[1,16,128,128]{3,2,1,0:T(8,128)(2,1)}, u32[]{:S(2)}) copy-start(bf16[1,16,128,128]{3,2,1,0:T(8,128)(2,1)} %param.16) | copy-start | bytes 1572868
  20.3 33.5 %copy-start.4 = (bf16[1,1,3,128,128]{4,3,2,1,0:T(8,128)(2,1)S(1)}, bf16[1,1,3,128,128]{4,3,2,1,0:T(8,128)(2,1)}, u32[]{:S(2)}) copy-start(bf16[1,1,3,128,128]{4,3,2,1,0:T(8,128)(2,1)} %param.12) | copy-start | bytes 294916
  21.1 9.4 %all-to-all-start = ((bf16[16,24,128]{2,1,0:T(8,128)(2,1)}), bf16[16,24,128]{2,1,0:T(8,128)(2,1)S(1)}, u32[]{:S(2)}, u32[]{:S(2)}) async-start(bf16[16,24,128]{2,1,0:T(8,128)(2,1)} %bitcast.11), calls=%async_computation | async-start | bytes 196608 | tf_op jit(solution)/shard_map/all_to_all | solution.py:95
  27.3 30.3 %copy-start.9 = (s32[1,1,192]{2,1,0:T(1,128)S(1)}, s32[1,1,192]{2,1,0:T(1,128)}, u32[]{:S(2)}) copy-start(s32[1,1,192]{2,1,0:T(1,128)} %param.11) | copy-start | bytes 2308
  30.5 27.6 %copy-start.3 = (bf16[1,1,96,512]{3,2,1,0:T(8,128)(2,1)S(1)}, bf16[1,1,96,512]{3,2,1,0:T(8,128)(2,1)}, u32[]{:S(2)}) copy-start(bf16[1,1,96,512]{3,2,1,0:T(8,128)(2,1)} %param.10) | copy-start | bytes 294916
  31.3 22.6 %collective-permute-start.2 = (bf16[2048,128]{1,0:T(8,128)(2,1)S(1)}, bf16[2048,128]{1,0:T(8,128)(2,1)S(1)}, u32[]{:S(2)}, u32[]{:S(2)}) collective-permute-start(bf16[2048,128]{1,0:T(8,128)(2,1)S(1)} %bitcast.144), channel_id=1, source_target_pairs={{0,24},{24,0},{1,25},{25,1},{2,26},{26,2},{3,27},{27,3},{4,28},{28... | collective-permute-start | bytes 1572872 | tf_op jit(solution)/shard_map/ppermute | solution.py:27
  33.8 33.8 %all-to-all-start.1 = ((bf16[48,24,128]{2,1,0:T(8,128)(2,1)}), bf16[48,24,128]{2,1,0:T(8,128)(2,1)S(1)}, u32[]{:S(2)}, u32[]{:S(2)}) async-start(bf16[48,24,128]{2,1,0:T(8,128)(2,1)} %broadcast_in_dim.69), calls=%async_computation.1 | async-start | bytes 589824 | tf_op jit(solution)/shard_map/all_to_all | solution.py:109
  47.6 10.1 %collective-permute-start.1 = (bf16[96,320]{1,0:T(8,128)(2,1)S(1)}, bf16[96,320]{1,0:T(8,128)(2,1)S(1)}, u32[]{:S(2)}, u32[]{:S(2)}) collective-permute-start(bf16[96,320]{1,0:T(8,128)(2,1)S(1)} %pad_maximum_fusion.3), channel_id=1, source_target_pairs={{48,0},{60,12},{72,24},{84,36},{96,48},{108,60},{120,72},{132,84},... | collective-permute-start | bytes 184328 | tf_op jit(solution)/shard_map/ppermute | solution.py:38
  48.9 8.7 %collective-permute-start = (bf16[96,320]{1,0:T(8,128)(2,1)S(1)}, bf16[96,320]{1,0:T(8,128)(2,1)S(1)}, u32[]{:S(2)}, u32[]{:S(2)}) collective-permute-start(bf16[96,320]{1,0:T(8,128)(2,1)S(1)} %slice.203), channel_id=1, source_target_pairs={{0,48},{12,60},{24,72},{36,84},{48,96},{60,108},{72,120},{84,132},... | collective-permute-start | bytes 184328 | tf_op jit(solution)/shard_map/ppermute | solution.py:38
  53.9 13.7 %copy-start.2 = (bf16[2048,128]{1,0:T(8,128)(2,1)}, bf16[2048,128]{1,0:T(8,128)(2,1)S(1)}, u32[]{:S(2)}) copy-start(bf16[2048,128]{1,0:T(8,128)(2,1)S(1)} %collective-permute-done.2) | copy-start | bytes 1572868
  54.1 13.6 %collective-permute-start.3 = (bf16[2048,256]{1,0:T(8,128)(2,1)S(1)}, bf16[2048,256]{1,0:T(8,128)(2,1)}, u32[]{:S(2)}, u32[]{:S(2)}) collective-permute-start(bf16[2048,256]{1,0:T(8,128)(2,1)S(1)} %pad_maximum_fusion.1), channel_id=1, source_target_pairs={{0,12},{12,0},{1,13},{13,1},{2,14},{14,2},{3,15},{15,3},{4,16},{16... | collective-permute-start | bytes 3145736 | tf_op jit(solution)/shard_map/ppermute | solution.py:27
  69.2 0.9 copy-start.5
  69.2 10.8 %copy-start.6 = (bf16[1,1,2048,512]{3,2,1,0:T(8,128)(2,1)S(1)}, bf16[1,1,2048,512]{3,2,1,0:T(8,128)(2,1)}, u32[]{:S(2)}) copy-start(bf16[1,1,2048,512]{3,2,1,0:T(8,128)(2,1)} %param.9) | copy-start | bytes 6291460
  90.6 30.8 %all-to-all-start.3 = ((bf16[48,24,128]{2,1,0:T(8,128)(2,1)}), bf16[48,24,128]{2,1,0:T(8,128)(2,1)S(1)}, u32[]{:S(2)}, u32[]{:S(2)}) async-start(bf16[48,24,128]{2,1,0:T(8,128)(2,1)} %broadcast_in_dim.73), calls=%async_computation.3 | async-start | bytes 589824 | tf_op jit(solution)/shard_map/all_to_all | solution.py:109
  100.7 5.6 %collective-permute-start.4 = (bf16[96,320]{1,0:T(8,128)(2,1)S(1)}, bf16[96,320]{1,0:T(8,128)(2,1)S(1)}, u32[]{:S(2)}, u32[]{:S(2)}) collective-permute-start(bf16[96,320]{1,0:T(8,128)(2,1)S(1)} %slice.223), channel_id=1, source_target_pairs={{0,48},{12,60},{24,72},{36,84},{48,96},{60,108},{72,120},{84,132},... | collective-permute-start | bytes 184328 | tf_op jit(solution)/shard_map/ppermute | solution.py:38
  104.7 12.3 %collective-permute-start.5 = (bf16[96,320]{1,0:T(8,128)(2,1)S(1)}, bf16[96,320]{1,0:T(8,128)(2,1)S(1)}, u32[]{:S(2)}, u32[]{:S(2)}) collective-permute-start(bf16[96,320]{1,0:T(8,128)(2,1)S(1)} %pad_maximum_fusion.4), channel_id=1, source_target_pairs={{48,0},{60,12},{72,24},{84,36},{96,48},{108,60},{120,72},{132,84},... | collective-permute-start | bytes 184328 | tf_op jit(solution)/shard_map/ppermute | solution.py:38
  121.4 9.4 %copy-start.7 = (bf16[1,1,2048,512]{3,2,1,0:T(8,128)(2,1)S(1)}, bf16[1,1,2048,512]{3,2,1,0:T(8,128)(2,1)}, u32[]{:S(2)}) copy-start(bf16[1,1,2048,512]{3,2,1,0:T(8,128)(2,1)} %param.9) | copy-start | bytes 6291460
  132.0 9.4 %all-to-all-start.4 = ((bf16[16,24,128]{2,1,0:T(8,128)(2,1)}), bf16[16,24,128]{2,1,0:T(8,128)(2,1)S(1)}, u32[]{:S(2)}, u32[]{:S(2)}) async-start(bf16[16,24,128]{2,1,0:T(8,128)(2,1)} %bitcast.39), calls=%async_computation.4 | async-start | bytes 196608 | tf_op jit(solution)/shard_map/all_to_all | solution.py:95
  142.4 30.0 %all-to-all-start.5 = ((bf16[48,24,128]{2,1,0:T(8,128)(2,1)}), bf16[48,24,128]{2,1,0:T(8,128)(2,1)S(1)}, u32[]{:S(2)}, u32[]{:S(2)}) async-start(bf16[48,24,128]{2,1,0:T(8,128)(2,1)} %broadcast_in_dim.76), calls=%async_computation.5 | async-start | bytes 589824 | tf_op jit(solution)/shard_map/all_to_all | solution.py:109
  151.7 5.6 %collective-permute-start.6 = (bf16[96,320]{1,0:T(8,128)(2,1)S(1)}, bf16[96,320]{1,0:T(8,128)(2,1)S(1)}, u32[]{:S(2)}, u32[]{:S(2)}) collective-permute-start(bf16[96,320]{1,0:T(8,128)(2,1)S(1)} %slice.240), channel_id=1, source_target_pairs={{0,48},{12,60},{24,72},{36,84},{48,96},{60,108},{72,120},{84,132},... | collective-permute-start | bytes 184328 | tf_op jit(solution)/shard_map/ppermute | solution.py:38
  155.7 24.6 %copy-start.8 = (bf16[1,1,128,128]{3,2,1,0:T(8,128)(2,1)S(1)}, bf16[1,1,128,128]{3,2,1,0:T(8,128)(2,1)}, u32[]{:S(2)}) copy-start(bf16[1,1,128,128]{3,2,1,0:T(8,128)(2,1)} %param.17) | copy-start | bytes 98308
  155.8 12.3 %collective-permute-start.7 = (bf16[96,320]{1,0:T(8,128)(2,1)S(1)}, bf16[96,320]{1,0:T(8,128)(2,1)S(1)}, u32[]{:S(2)}, u32[]{:S(2)}) collective-permute-start(bf16[96,320]{1,0:T(8,128)(2,1)S(1)} %pad_maximum_fusion.5), channel_id=1, source_target_pairs={{48,0},{60,12},{72,24},{84,36},{96,48},{108,60},{120,72},{132,84},... | collective-permute-start | bytes 184328 | tf_op jit(solution)/shard_map/ppermute | solution.py:38
